TPU v7x, 32 devices: a whole 2x2x4 slice. The times are simulated.
32 devices in a mesh: tm: 2 (over x), space: 16 (over z, y, core).
Axes of the slice: x: 2, y: 2, z: 4, core: 2. Of those that a mesh axis runs over, the one named last changes fastest.
Arguments:
- orbitals: bfloat16 [13824, 320], P('space'), may hold values from -6 to 6
- gaps: float32 [320], replicated, may hold values from 0.005 to 50
- times: float32 [2], P('tm'), may hold values from 0.01 to 100, as said below
- cos_weights: float32 [2, 2], replicated, may hold values from -1 to 1
Outputs:
- polarizability: float32 [2, 864, 864], P('tm', 'space')
Inputs may be any that keep to these rules, and one draw needn't show every extreme that they name: times rise with their index.
All inputs are finite; a program needn't handle non-finite values.
Results may differ from a plain program's by a relative error of at most 0.0044.
Values may be sent and summed in bfloat16 or wider, within the bound.
No kernel may reach another device: no remote copies, remote signals or barrier semaphores. Data moves between devices by JAX's collectives and lax.ppermute only.
A program may use at most 192 MiB of HBM per device.

v0:
```python
import functools
import math

import jax
import jax.numpy as jnp
from jax import lax
from jax.experimental import pallas as pl
from jax.experimental.pallas import tpu as pltpu
from jax.sharding import PartitionSpec as P

SIDE = 24
NG = 864
NOCC = 64
NEMP = 256
LANES = 128


def round_up(value, step):
    return -(-value // step) * step


def class_waves(mode_count, grid_side, width):
    first, second = grid_side // 2, grid_side // 4
    third = mode_count // 2 // (first * second)
    shape = (4, width)
    kind = lax.broadcasted_iota(jnp.int32, shape, 0)
    column = lax.broadcasted_iota(jnp.int32, shape, 1)
    a_odd, b_odd = kind // 2, kind % 2
    a_step = column % (first // 2)
    b_step = column // (first // 2) % (second // 2)
    c_step = column // (first // 2 * (second // 2)) % third
    sine = column // (first // 2 * (second // 2) * third)
    a_index = 2 * a_step + (a_odd + first // 2) % 2
    b_index = 2 * b_step + (b_odd + second // 2) % 2
    row = sine * (mode_count // 2) + c_step * first * second + b_index * first + a_index
    row = jnp.where(column < mode_count // 4, row, -1)
    return a_index - first // 2, b_index - second // 2, c_step + 1, sine, row


def table_factors(grid_side, mode_count, steps, width):
    half = grid_side // 2
    a, b, c, sine, row = class_waves(mode_count, grid_side, width)
    x = jnp.arange(half, dtype=jnp.int32)
    y = jnp.arange(half, dtype=jnp.int32)
    z = jnp.arange(grid_side, dtype=jnp.int32)
    unit = 2.0 * math.pi / grid_side
    scaling = math.sqrt(2.0 / grid_side**3)
    p = jnp.mod(x[:, None, None] * a, grid_side).astype(jnp.float32) * unit
    p = p.reshape(steps, half // steps, 4, width).transpose(0, 2, 1, 3)
    q = jnp.mod(y[:, None, None] * b, grid_side).astype(jnp.float32) * unit
    s = jnp.mod(z[:, None, None] * c, grid_side).astype(jnp.float32) * unit
    size = jnp.where(row >= 0, scaling, 0.0)
    q, s = q.transpose(1, 0, 2)[:, :, None, :], s.transpose(1, 0, 2)[:, None, :, :]
    inner_cos = jnp.cos(q) * jnp.cos(s) - jnp.sin(q) * jnp.sin(s)
    inner_sin = jnp.sin(q) * jnp.cos(s) + jnp.cos(q) * jnp.sin(s)
    is_sine = (sine == 1)[:, None, None, :]
    size = size[:, None, None, :]
    with_cos = jnp.where(is_sine, inner_sin, inner_cos) * size
    with_sin = jnp.where(is_sine, inner_cos, -inner_sin) * size
    flat = (4, 1, half * grid_side, width)
    return jnp.cos(p), jnp.sin(p), with_cos.reshape(flat), with_sin.reshape(flat)


def table_piece(cos_p, sin_p, with_cos, with_sin):
    table = cos_p[:, :, None, :] * with_cos + sin_p[:, :, None, :] * with_sin
    return table.astype(jnp.bfloat16).reshape(4, -1, cos_p.shape[-1])


def column_order(grid_side, mode_count, width):
    row = class_waves(mode_count, grid_side, width)[4].reshape(-1, 1)
    return (row == jnp.arange(mode_count, dtype=jnp.int32)[None, :]).astype(jnp.bfloat16)


def pair_kernel(
    place_ref,
    weight_ref,
    emp_own_ref,
    emp_other_ref,
    order_hbm,
    *refs,
):
    chips = emp_own_ref.shape[0]
    steps = refs[-4].shape[0]
    occ_refs, refs = refs[:chips], refs[chips:]
    tables_hbm, refs = refs[:steps], refs[steps:]
    keep_ref, send_ref = refs[:2]
    raw_occ, raw_emp, occ_wide, emp_wide, first, second, rho, blocks, table, order, table_sem, order_sem = refs[
        2:
    ]
    _, _, depth, width = table.shape
    n_occ, n_rows = raw_occ.shape[1:]
    n_emp = raw_emp.shape[1]
    per_group = 2 * chips // (2 * steps)
    plane = SIDE * SIDE // 2

    used = tables_hbm[0].shape[1]
    table_copies = [
        pltpu.make_async_copy(tables_hbm[s], table.at[s, :, pl.ds(0, used)], table_sem.at[s])
        for s in range(steps)
    ]
    for copy in table_copies:
        copy.start()
    order_copy = pltpu.make_async_copy(order_hbm, order, order_sem)
    order_copy.start()

    core = place_ref[chips]
    me = place_ref[chips + 1]
    for index, ref in enumerate(occ_refs):
        chip = place_ref[index]
        raw_occ[chip * 2 + core] = ref[0]
        raw_occ[chip * 2 + 1 - core] = ref[1]
    for chip in range(chips):
        raw_emp[chip * 2 + core] = emp_own_ref[chip]
        raw_emp[chip * 2 + 1 - core] = emp_other_ref[chip]

    def halves(raw, group, upper):
        pieces = []
        for x in range(3):
            start = (2 * x + upper) * plane
            stop = start + plane
            while start < stop:
                shard, offset = divmod(start, n_rows)
                count = min(stop - start, n_rows - offset)
                rows = raw[group * per_group + shard].astype(jnp.float32)
                pieces.append(rows[:, offset : offset + count])
                start += count
        pieces.append(jnp.zeros((raw.shape[1], depth - 3 * plane), jnp.float32))
        return jnp.concatenate(pieces, axis=1)

    for group in range(2 * steps):
        for upper in range(2):
            occ_wide[group, upper] = halves(raw_occ, group, upper)
            emp_wide[group, upper] = halves(raw_emp, group, upper).astype(jnp.bfloat16)

    rho[...] = jnp.zeros_like(rho)
    for s in range(steps):
        table[s, :, used:, :] = jnp.zeros((4, depth - used, width), jnp.bfloat16)
    quarter = n_occ // 4

    def build(step, target, part):
        sources = [(step, 0), (step, 1), (step + steps, 0), (step + steps, 1)]
        for lane in range(0, depth, LANES):
            cut = slice(lane, lane + LANES)
            occ_rows = [
                occ_wide[group, upper, part * quarter : (part + 1) * quarter, cut] for group, upper in sources
            ]
            emp_rows = [emp_wide[group, upper, :, cut] for group, upper in sources]
            for i in range(quarter):
                near_low, near_high, far_low, far_high = (
                    jnp.broadcast_to(occ_rows[k][i : i + 1], (n_emp, LANES)).astype(jnp.bfloat16) * emp_rows[k]
                    for k in range(4)
                )
                even_low, odd_low = near_low + far_low, near_low - far_low
                even_high, odd_high = near_high + far_high, near_high - far_high
                start = (part * quarter + i) * n_emp
                target[0, start : start + n_emp, cut] = even_low + even_high
                target[1, start : start + n_emp, cut] = even_low - even_high
                target[2, start : start + n_emp, cut] = odd_low + odd_high
                target[3, start : start + n_emp, cut] = odd_low - odd_high

    def multiply(step, source, k):
        rho[k] += jnp.dot(source[k], table[step, k], preferred_element_type=jnp.float32)

    for part in range(4):
        build(0, first, part)

    def two_steps(t, carry):
        for offset, (now, later) in enumerate(((first, second), (second, first))):
            step = 2 * t + offset
            pltpu.make_async_copy(
                tables_hbm[0], table.at[step, :, pl.ds(0, used)], table_sem.at[step]
            ).wait()
            following = lax.rem(step + 1, steps)
            for k in range(4):
                build(following, later, k)
                multiply(step, now, k)
        return carry

    lax.fori_loop(0, steps // 2, two_steps, 0)

    order_copy.wait()
    columns = jnp.concatenate([rho[k].astype(jnp.bfloat16) for k in range(4)], axis=1)
    ordered = jnp.dot(columns, order[...], preferred_element_type=jnp.float32)
    weighted = (ordered * weight_ref[...]).astype(jnp.bfloat16)
    moment = lax.dot_general(
        weighted,
        ordered.astype(jnp.bfloat16),
        (((0,), (0,)), ((), ())),
        preferred_element_type=jnp.float32,
    )
    count, rows = blocks.shape[:2]
    for k in range(count):
        blocks[k] = moment[k * rows : (k + 1) * rows]
    for k in range(count // 2):
        keep_ref[k] = blocks[jnp.bitwise_xor(me, 2 * k)]
        send_ref[k] = blocks[jnp.bitwise_xor(me, 2 * k + 1)].astype(jnp.bfloat16)


def pair_moment(place, weights, occ_blocks, emp_own, emp_other, tables, order):
    chips, n_emp, n_rows = emp_own.shape
    n_occ = occ_blocks[0].shape[1]
    steps = len(tables)
    _, used, width = tables[0].shape
    depth = round_up(used, LANES)
    pairs = n_occ * n_emp
    modes = order.shape[1]
    blocks = 2 * chips
    rows = modes // blocks
    vmem = pl.BlockSpec(memory_space=pltpu.VMEM)
    hbm = pl.BlockSpec(memory_space=pl.ANY)
    return pl.pallas_call(
        pair_kernel,
        out_shape=(
            jax.ShapeDtypeStruct((blocks // 2, rows, modes), jnp.float32),
            jax.ShapeDtypeStruct((blocks // 2, rows, modes), jnp.bfloat16),
        ),
        in_specs=[pl.BlockSpec(memory_space=pltpu.SMEM), vmem, vmem, vmem, hbm]
        + [vmem] * chips
        + [hbm] * steps,
        out_specs=(vmem, vmem),
        scratch_shapes=[
            pltpu.VMEM((2 * chips, n_occ, n_rows), jnp.bfloat16),
            pltpu.VMEM((2 * chips, n_emp, n_rows), jnp.bfloat16),
            pltpu.VMEM((2 * steps, 2, n_occ, depth), jnp.float32),
            pltpu.VMEM((2 * steps, 2, n_emp, depth), jnp.bfloat16),
            pltpu.VMEM((4, pairs, depth), jnp.bfloat16),
            pltpu.VMEM((4, pairs, depth), jnp.bfloat16),
            pltpu.VMEM((4, pairs, width), jnp.float32),
            pltpu.VMEM((blocks, rows, modes), jnp.float32),
            pltpu.VMEM((steps, 4, depth, width), jnp.bfloat16),
            pltpu.VMEM(order.shape, jnp.bfloat16),
            pltpu.SemaphoreType.DMA((steps,)),
            pltpu.SemaphoreType.DMA,
        ],
        compiler_params=pltpu.CompilerParams(vmem_limit_bytes=60 * 1024 * 1024),
        cost_estimate=pl.CostEstimate(
            flops=2 * steps * 4 * pairs * depth * width, bytes_accessed=16 * 2**20, transcendentals=0
        ),
        name="pair_moment",
    )(place, weights, emp_own, emp_other, order, *occ_blocks, *tables)


def ring_of(chips):
    return list(range(0, chips, 2)) + list(range(chips - 1, 0, -2))


def gather_ring(block, chips, between):
    ring = ring_of(chips)
    ahead, back = [], []
    for position in range(chips):
        for core in range(2):
            here = 2 * ring[position] + core
            right = 2 * ring[(position + 1) % chips] + core
            ahead.append((here, right))
            back.append((right, here))
    found, offsets, made = [block], [0], []
    from_left = from_right = block
    for hop in range(1, chips // 2 + 1):
        if hop <= len(between):
            function, arguments = between[hop - 1]
            (from_left, from_right), arguments = lax.optimization_barrier(((from_left, from_right), arguments))
            made.append(function(*arguments))
        from_left = lax.ppermute(from_left, "space", ahead)
        found.append(from_left)
        offsets.append(-hop)
        if 2 * hop < chips:
            from_right = lax.ppermute(from_right, "space", back)
            found.append(from_right)
            offsets.append(hop)
    return found, offsets, made


def local(space, tm, orbitals, gaps, times, cos_weights):
    rows = orbitals.shape[0]
    chips = space // 2
    columns = orbitals.T
    own_occ, own_emp = NOCC // 2, NEMP // chips
    me = lax.axis_index("space")
    core, chip = me % 2, me // 2
    swap = [(d, d ^ 1) for d in range(space)]

    occ = columns[:NOCC].reshape(2, own_occ, rows)
    occ_mine = lax.dynamic_index_in_dim(occ, core, 0, keepdims=False)
    occ_theirs = lax.dynamic_index_in_dim(occ, 1 - core, 0, keepdims=False)
    occ_pair = jnp.stack([occ_mine, lax.ppermute(occ_theirs, "space", swap)])
    emp_own = lax.all_to_all(
        columns[NOCC:].reshape(chips, own_emp, rows),
        "space",
        split_axis=0,
        concat_axis=0,
        axis_index_groups=[[2 * k + c for k in range(chips)] for c in range(2)],
    )
    planes = 3
    steps = SIDE // 2 // planes
    width = round_up(NG // 4, 2 * LANES)
    cos_p, sin_p, with_cos, with_sin = table_factors(SIDE, NG, steps, width)
    between = [(table_piece, (cos_p[k], sin_p[k], with_cos, with_sin)) for k in range(steps)]
    occ_blocks, offsets, tables = gather_ring(occ_pair, chips, between)
    emp_other = lax.ppermute(emp_own, "space", swap)
    order = column_order(SIDE, NG, width)

    position = jnp.where(chip % 2 == 0, chip // 2, chips - (chip + 1) // 2)
    places = (position + jnp.array(offsets, jnp.int32)) % chips
    on_ring = jnp.where(places < chips // 2, 2 * places, 2 * (chips - places) - 1)
    place = jnp.concatenate([on_ring, jnp.stack([core, me])]).astype(jnp.int32)

    own_count = cos_weights.shape[0] // tm
    tm_index = lax.axis_index("tm")
    pair_weights = 0.0
    for hop in range(tm):
        source = (tm_index + hop) % tm
        their_times = times
        if hop:
            their_times = lax.ppermute(times, "tm", [((d + hop) % tm, d) for d in range(tm)])
        factors = jnp.exp(-gaps[None, :] * their_times[:, None])
        occ_factors = lax.dynamic_slice_in_dim(factors, core * own_occ, own_occ, 1) * NOCC ** (-0.5)
        emp_factors = lax.dynamic_slice_in_dim(factors, NOCC + chip * own_emp, own_emp, 1) * NEMP ** (-0.5)
        weights = lax.dynamic_slice(
            cos_weights,
            (tm_index * own_count, source * times.shape[0]),
            (own_count, times.shape[0]),
        )
        pair_weights = pair_weights + jnp.sum(
            weights[:, :, None, None] * (occ_factors[:, :, None] * emp_factors[:, None, :])[None], axis=1
        )
    pair_weights = pair_weights.reshape(own_count, own_occ * own_emp, 1)

    results = []
    for w in range(own_count):
        keep, send = pair_moment(place, pair_weights[w], occ_blocks, emp_own, emp_other, tables, order)
        received = lax.ppermute(send, "space", swap)
        total = keep + received.astype(jnp.float32)
        parts = total.astype(jnp.bfloat16)
        result = total[0]
        for distance in range(1, chips):
            part = lax.ppermute(
                parts[distance], "space", [(d, d ^ (2 * distance)) for d in range(space)]
            )
            result = result + part.astype(jnp.float32)
        results.append(result)
    return jnp.stack(results)


def solution(mesh):
    return jax.shard_map(
        functools.partial(local, mesh.shape["space"], mesh.shape["tm"]),
        mesh=mesh,
        in_specs=(P("space", None), P(), P("tm"), P()),
        out_specs=P("tm", "space", None),
        check_vma=False,
    )
```

profile of v0, /device:TPU:0, one launch (start us, length us, event | category | flops | bytes accessed | tf_op | source)
XLA Modules:
  0.0 99.2 jit_solution(2361615788344462484)
XLA Ops:
  0.0 2.9 %collective-permute-start = (f32[1]{0:T(128)}, f32[1]{0:T(128)}, u32[]{:S(2)}, u32[]{:S(2)}) collective-permute-start(f32[1]{0:T(128)} %param.7), channel_id=1, source_target_pairs={{16,0},{0,16},{17,1},{1,17},{18,2},{2,18},{19,3},{3,19},{20,4},{4,... | collective-permute-start | bytes 20 | tf_op jit(solution)/shard_map/ppermute | solution.py:314
  2.9 0.9 slice.73
  3.9 0.1 collective-permute-start.2
  4.0 1.8 %slice.72 = bf16[256,864]{1,0:T(8,128)(2,1)} slice(bf16[320,864]{1,0:T(8,128)(2,1)} %bitcast.120), slice={[64:320], [0:864]} | slice | bytes 884736 | tf_op jit(solution)/shard_map/slice | solution.py:287
  5.8 6.0 %all-to-all-start = ((bf16[8,32,864]{2,1,0:T(8,128)(2,1)}), bf16[8,32,864]{2,1,0:T(8,128)(2,1)S(1)}, u32[]{:S(2)}, u32[]{:S(2)}) async-start(bf16[8,32,864]{2,1,0:T(8,128)(2,1)} %bitcast.7), calls=%async_computation | async-start | bytes 917504 | tf_op jit(solution)/shard_map/all_to_all | solution.py:286
  12.7 0.1 broadcast_add_fusion.1
  12.8 0.1 broadcast_add_fusion
  12.9 0.1 fusion.65
  13.0 0.6 fusion.30
  13.7 0.3 fusion.25
  14.0 0.4 fusion.16
  14.4 1.7 %fusion.order_hbm = bf16[1024,864]{1,0:T(8,128)(2,1)} fusion(s32[1024]{0:T(1024)S(1)} %fusion.41), kind=kLoop, calls=%fused_computation.1 | loop fusion | flops 1769472 | bytes 1773568 | tf_op jit(solution)/shard_map/convert_element_type | solution.py:71
  16.1 0.7 pad_add_fusion.place_ref
  16.8 0.6 fusion.72
  17.4 0.3 multiply_add_fusion
  17.6 0.0 copy-start.2
  17.7 0.3 fusion.2
  17.9 0.0 collective-permute-done
  17.9 0.4 copy-done.2
  18.3 0.6 multiply_exponential_fusion.1
  18.9 0.1 dynamic-slice_multiply_fusion.1
  19.0 1.3 %multiply_add_fusion.1 = f32[32,1,32]{2,0,1:T(8,128)S(1)} fusion(f32[32]{0:T(128)S(1)} %get-tuple-element.95, f32[32]{0:T(128)S(1)} %get-tuple-element.94, f32[]{:T(128)} %bitcast.4, f32[32]{0:T(128)S(1)} %get-tuple-element.102, f32[32]{0:T(128)S(1)} %get-tuple-element.103, f32[]{:T(128)} %bitcast.2), kind=kLoop, calls=%fused_computation.67 | loop fusion | flops 5120 | bytes 4616 | tf_op jit(solution)/shard_map/add | solution.py:323
  20.3 1.3 %add.814.weight_ref = f32[1024,1]{1,0:T(8,128)} reshape(f32[32,1,32]{2,0,1:T(8,128)S(1)} %multiply_add_fusion.1) | data formatting | bytes 8192 | tf_op jit(solution)/shard_map/add | solution.py:323
  21.6 0.0 collective-permute-done.2
  21.7 0.0 copy-start.1
  21.7 2.1 %collective-permute-start.3 = (bf16[2,32,864]{2,1,0:T(8,128)(2,1)S(1)}, bf16[2,32,864]{2,1,0:T(8,128)(2,1)S(1)}, u32[]{:S(2)}, u32[]{:S(2)}) collective-permute-start(bf16[2,32,864]{2,1,0:T(8,128)(2,1)S(1)} %pad_maximum_fusion.refs_0_), channel_id=1, source_target_pairs={{0,4},{1,5},{4,8},{5,9},{8,12},{9,13},{12,14},{13,15},{14,10},{15,... | collective-permute-start | bytes 331784 | tf_op jit(solution)/shard_map/ppermute | solution.py:263
  23.7 0.1 collective-permute-start.4
  23.8 1.7 %add_convert_fusion.3 = bf16[4,3,288,256]{3,2,1,0:T(8,128)(2,1)} fusion(f32[4,288,256]{2,1,0:T(8,128)S(1)} %bitcast.107, f32[4,3,256]{2,1,0:T(4,128)S(1)} %get-tuple-element.39, f32[4,288,256]{2,1,0:T(8,128)S(1)} %bitcast.111, f32[4,3,256]{2,1,0:T(4,128)S(1)} %get-tuple-element.37), kind=kLoop, calls=%fused_computation.5 | loop fusion | flops 3538944 | bytes 4153344 | tf_op jit(solution)/shard_map/convert_element_type | solution.py:66
  25.5 1.5 %collective-permute-done.3.refs_1_ = bf16[2,32,864]{2,1,0:T(8,128)(2,1)S(1)} collective-permute-done((bf16[2,32,864]{2,1,0:T(8,128)(2,1)S(1)}, bf16[2,32,864]{2,1,0:T(8,128)(2,1)S(1)}, u32[]{:S(2)}, u32[]{:S(2)}) %collective-permute-start.3) | collective-permute-done | bytes 110624 | tf_op jit(solution)/shard_map/ppermute | solution.py:263
  27.0 1.5 %collective-permute-done.4.refs_2_ = bf16[2,32,864]{2,1,0:T(8,128)(2,1)S(1)} collective-permute-done((bf16[2,32,864]{2,1,0:T(8,128)(2,1)S(1)}, bf16[2,32,864]{2,1,0:T(8,128)(2,1)S(1)}, u32[]{:S(2)}, u32[]{:S(2)}) %collective-permute-start.4) | collective-permute-done | bytes 110624 | tf_op jit(solution)/shard_map/ppermute | solution.py:267
  28.5 1.5 %collective-permute-start.5 = (bf16[2,32,864]{2,1,0:T(8,128)(2,1)S(1)}, bf16[2,32,864]{2,1,0:T(8,128)(2,1)S(1)}, u32[]{:S(2)}, u32[]{:S(2)}) collective-permute-start(bf16[2,32,864]{2,1,0:T(8,128)(2,1)S(1)} %collective-permute-done.3.refs_1_), channel_id=1, source_target_pairs={{0,4},{1,5},{4,8},{5,9},{8,12},{9,13},{12,14},{13,15},{14,10},{15,... | collective-permute-start | bytes 331784 | tf_op jit(solution)/shard_map/ppermute | solution.py:263
  30.0 0.6 collective-permute-start.6
  30.6 1.7 %add_convert_fusion.2 = bf16[4,3,288,256]{3,2,1,0:T(8,128)(2,1)} fusion(f32[4,288,256]{2,1,0:T(8,128)S(1)} %bitcast.108, f32[4,3,256]{2,1,0:T(4,128)S(1)} %get-tuple-element.43, f32[4,288,256]{2,1,0:T(8,128)S(1)} %bitcast.112, f32[4,3,256]{2,1,0:T(4,128)S(1)} %get-tuple-element.41), kind=kLoop, calls=%fused_computation.4 | loop fusion | flops 3538944 | bytes 4153344 | tf_op jit(solution)/shard_map/convert_element_type | solution.py:66
  32.3 1.1 %collective-permute-done.5.refs_3_ = bf16[2,32,864]{2,1,0:T(8,128)(2,1)S(1)} collective-permute-done((bf16[2,32,864]{2,1,0:T(8,128)(2,1)S(1)}, bf16[2,32,864]{2,1,0:T(8,128)(2,1)S(1)}, u32[]{:S(2)}, u32[]{:S(2)}) %collective-permute-start.5) | collective-permute-done | bytes 110624 | tf_op jit(solution)/shard_map/ppermute | solution.py:263
  33.3 1.5 %collective-permute-done.6.refs_4_ = bf16[2,32,864]{2,1,0:T(8,128)(2,1)S(1)} collective-permute-done((bf16[2,32,864]{2,1,0:T(8,128)(2,1)S(1)}, bf16[2,32,864]{2,1,0:T(8,128)(2,1)S(1)}, u32[]{:S(2)}, u32[]{:S(2)}) %collective-permute-start.6) | collective-permute-done | bytes 110624 | tf_op jit(solution)/shard_map/ppermute | solution.py:267
  34.8 1.5 %collective-permute-start.7 = (bf16[2,32,864]{2,1,0:T(8,128)(2,1)S(1)}, bf16[2,32,864]{2,1,0:T(8,128)(2,1)S(1)}, u32[]{:S(2)}, u32[]{:S(2)}) collective-permute-start(bf16[2,32,864]{2,1,0:T(8,128)(2,1)S(1)} %collective-permute-done.5.refs_3_), channel_id=1, source_target_pairs={{0,4},{1,5},{4,8},{5,9},{8,12},{9,13},{12,14},{13,15},{14,10},{15,... | collective-permute-start | bytes 331784 | tf_op jit(solution)/shard_map/ppermute | solution.py:263
  36.3 0.6 collective-permute-start.8
  36.8 1.7 %add_convert_fusion.1 = bf16[4,3,288,256]{3,2,1,0:T(8,128)(2,1)} fusion(f32[4,288,256]{2,1,0:T(8,128)S(1)} %bitcast.109, f32[4,3,256]{2,1,0:T(4,128)S(1)} %get-tuple-element.47, f32[4,288,256]{2,1,0:T(8,128)S(1)} %bitcast.113, f32[4,3,256]{2,1,0:T(4,128)S(1)} %get-tuple-element.45), kind=kLoop, calls=%fused_computation.3 | loop fusion | flops 3538944 | bytes 4153344 | tf_op jit(solution)/shard_map/convert_element_type | solution.py:66
  38.5 1.1 %collective-permute-done.7.refs_5_ = bf16[2,32,864]{2,1,0:T(8,128)(2,1)S(1)} collective-permute-done((bf16[2,32,864]{2,1,0:T(8,128)(2,1)S(1)}, bf16[2,32,864]{2,1,0:T(8,128)(2,1)S(1)}, u32[]{:S(2)}, u32[]{:S(2)}) %collective-permute-start.7) | collective-permute-done | bytes 110624 | tf_op jit(solution)/shard_map/ppermute | solution.py:263
  39.6 1.5 %collective-permute-done.8.refs_6_ = bf16[2,32,864]{2,1,0:T(8,128)(2,1)S(1)} collective-permute-done((bf16[2,32,864]{2,1,0:T(8,128)(2,1)S(1)}, bf16[2,32,864]{2,1,0:T(8,128)(2,1)S(1)}, u32[]{:S(2)}, u32[]{:S(2)}) %collective-permute-start.8) | collective-permute-done | bytes 110624 | tf_op jit(solution)/shard_map/ppermute | solution.py:267
  41.1 1.5 %collective-permute-start.9 = (bf16[2,32,864]{2,1,0:T(8,128)(2,1)S(1)}, bf16[2,32,864]{2,1,0:T(8,128)(2,1)S(1)}, u32[]{:S(2)}, u32[]{:S(2)}) collective-permute-start(bf16[2,32,864]{2,1,0:T(8,128)(2,1)S(1)} %collective-permute-done.7.refs_5_), channel_id=1, source_target_pairs={{0,4},{1,5},{4,8},{5,9},{8,12},{9,13},{12,14},{13,15},{14,10},{15,... | collective-permute-start | bytes 331784 | tf_op jit(solution)/shard_map/ppermute | solution.py:263
  42.5 1.8 %add_convert_fusion = bf16[4,3,288,256]{3,2,1,0:T(8,128)(2,1)} fusion(f32[4,288,256]{2,1,0:T(8,128)S(1)} %bitcast.110, f32[4,3,256]{2,1,0:T(4,128)S(1)} %get-tuple-element.51, f32[4,288,256]{2,1,0:T(8,128)S(1)} %bitcast.114, f32[4,3,256]{2,1,0:T(4,128)S(1)} %get-tuple-element.49), kind=kLoop, calls=%fused_computation.2 | loop fusion | flops 3538944 | bytes 4153344 | tf_op jit(solution)/shard_map/convert_element_type | solution.py:66
  44.3 1.5 %collective-permute-done.9.refs_7_ = bf16[2,32,864]{2,1,0:T(8,128)(2,1)S(1)} collective-permute-done((bf16[2,32,864]{2,1,0:T(8,128)(2,1)S(1)}, bf16[2,32,864]{2,1,0:T(8,128)(2,1)S(1)}, u32[]{:S(2)}, u32[]{:S(2)}) %collective-permute-start.9) | collective-permute-done | bytes 110624 | tf_op jit(solution)/shard_map/ppermute | solution.py:263
  45.9 0.6 copy-done.11
  46.5 0.2 copy-done.4
  46.7 23.4 %pair_moment.1 = (f32[8,54,864]{2,1,0:T(8,128)}, bf16[8,54,864]{2,1,0:T(8,128)(2,1)}) custom-call(s32[10]{0:T(128)} %pad_add_fusion.place_ref, f32[1024,1]{1,0:T(8,128)} %add.814.weight_ref, bf16[8,32,864]{2,1,0:T(8,128)(2,1)} %copy-done, bf16[8,32,864]{2,1,0:T(8,128)(2,1)} %copy-done.4, bf16[1024,864]{1,0:T(8,128)(2,1)} %fusion.order_hbm, ...), custom_call_target="tpu_custom_call" | custom-call | flops 7516192768 | bytes 16777216 | tf_op jit(solution)/shard_map/pair_moment/pallas_call | solution.py:211
  70.0 1.2 %copy.10 = bf16[8,54,864]{2,0,1:T(8,128)(2,1)S(1)} copy(bf16[8,54,864]{2,1,0:T(8,128)(2,1)} %get-tuple-element.54) | data formatting | bytes 1492992 | tf_op jit(solution)/shard_map/pair_moment/pallas_call | solution.py:211
  71.3 0.1 collective-permute-start.10
  71.3 2.3 %collective-permute-done.10 = bf16[8,54,864]{2,0,1:T(8,128)(2,1)S(1)} collective-permute-done((bf16[8,54,864]{2,0,1:T(8,128)(2,1)S(1)}, bf16[8,54,864]{2,0,1:T(8,128)(2,1)S(1)}, u32[]{:S(2)}, u32[]{:S(2)}) %collective-permute-start.10) | collective-permute-done | bytes 746528 | tf_op jit(solution)/shard_map/ppermute | solution.py:331
  73.6 1.6 %fusion.71 = (bf16[8,54,864]{2,1,0:T(8,128)(2,1)S(1)}, f32[8,54,864]{2,1,0:T(8,128)S(1)}) fusion(f32[8,54,864]{2,1,0:T(8,128)} %get-tuple-element.53, bf16[8,54,864]{2,0,1:T(8,128)(2,1)S(1)} %collective-permute-done.10), kind=kLoop, calls=%fused_computation.167 | loop fusion | flops 1119744 | bytes 4478976 | tf_op jit(solution)/shard_map/convert_element_type | solution.py:333
  75.2 0.1 slice_bitcast_fusion.7
  75.3 0.6 collective-permute-start.11
  75.9 2.4 %collective-permute-start.17 = (bf16[54,864]{1,0:T(8,128)(2,1)S(1)}, bf16[54,864]{1,0:T(8,128)(2,1)S(1)}, u32[]{:S(2)}, u32[]{:S(2)}) collective-permute-start(bf16[54,864]{1,0:T(8,128)(2,1)S(1)} %get-tuple-element.60), channel_id=1, source_target_pairs={{0,14},{1,15},{2,12},{3,13},{4,10},{5,11},{6,8},{7,9},{8,6},{9,7},... | collective-permute-start | bytes 279944 | tf_op jit(solution)/shard_map/ppermute | solution.py:336
  78.3 2.4 %collective-permute-start.16 = (bf16[54,864]{1,0:T(8,128)(2,1)S(1)}, bf16[54,864]{1,0:T(8,128)(2,1)S(1)}, u32[]{:S(2)}, u32[]{:S(2)}) collective-permute-start(bf16[54,864]{1,0:T(8,128)(2,1)S(1)} %get-tuple-element.61), channel_id=1, source_target_pairs={{0,12},{1,13},{2,14},{3,15},{4,8},{5,9},{6,10},{7,11},{8,4},{9,5},... | collective-permute-start | bytes 279944 | tf_op jit(solution)/shard_map/ppermute | solution.py:336
  80.6 2.9 %collective-permute-start.14 = (bf16[54,864]{1,0:T(8,128)(2,1)S(1)}, bf16[54,864]{1,0:T(8,128)(2,1)S(1)}, u32[]{:S(2)}, u32[]{:S(2)}) collective-permute-start(bf16[54,864]{1,0:T(8,128)(2,1)S(1)} %get-tuple-element.63), channel_id=1, source_target_pairs={{0,8},{1,9},{2,10},{3,11},{4,12},{5,13},{6,14},{7,15},{8,0},{9,1},... | collective-permute-start | bytes 279944 | tf_op jit(solution)/shard_map/ppermute | solution.py:336
  83.6 0.0 collective-permute-done.11
  83.6 0.6 collective-permute-start.13
  84.1 0.2 collective-permute-done.17
  84.3 7.8 %collective-permute-start.12 = (bf16[54,864]{1,0:T(8,128)(2,1)S(1)}, bf16[54,864]{1,0:T(8,128)(2,1)S(1)}, u32[]{:S(2)}, u32[]{:S(2)}) collective-permute-start(bf16[54,864]{1,0:T(8,128)(2,1)S(1)} %get-tuple-element.65), channel_id=1, source_target_pairs={{0,4},{1,5},{2,6},{3,7},{4,0},{5,1},{6,2},{7,3},{8,12},{9,13},{10,... | collective-permute-start | bytes 279944 | tf_op jit(solution)/shard_map/ppermute | solution.py:336
  92.1 3.8 %collective-permute-done.15 = bf16[54,864]{1,0:T(8,128)(2,1)S(1)} collective-permute-done((bf16[54,864]{1,0:T(8,128)(2,1)S(1)}, bf16[54,864]{1,0:T(8,128)(2,1)S(1)}, u32[]{:S(2)}, u32[]{:S(2)}) %collective-permute-start.15) | collective-permute-done | bytes 93344 | tf_op jit(solution)/shard_map/ppermute | solution.py:336
  96.0 1.5 %collective-permute-done.14 = bf16[54,864]{1,0:T(8,128)(2,1)S(1)} collective-permute-done((bf16[54,864]{1,0:T(8,128)(2,1)S(1)}, bf16[54,864]{1,0:T(8,128)(2,1)S(1)}, u32[]{:S(2)}, u32[]{:S(2)}) %collective-permute-start.14) | collective-permute-done | bytes 93344 | tf_op jit(solution)/shard_map/ppermute | solution.py:336
  97.5 0.8 collective-permute-done.12
  98.2 0.1 fusion.10
  98.4 0.9 copy.12
  (55 shorter events, 0.3 us)
Async XLA Ops:
  0.0 17.9 %collective-permute-start = (f32[1]{0:T(128)}, f32[1]{0:T(128)}, u32[]{:S(2)}, u32[]{:S(2)}) collective-permute-start(f32[1]{0:T(128)} %param.7), channel_id=1, source_target_pairs={{16,0},{0,16},{17,1},{1,17},{18,2},{2,18},{19,3},{3,19},{20,4},{4,... | collective-permute-start | bytes 20 | tf_op jit(solution)/shard_map/ppermute | solution.py:314
  3.9 17.7 %collective-permute-start.2 = (bf16[32,864]{1,0:T(8,128)(2,1)S(1)}, bf16[32,864]{1,0:T(8,128)(2,1)S(1)}, u32[]{:S(2)}, u32[]{:S(2)}) collective-permute-start(bf16[32,864]{1,0:T(8,128)(2,1)S(1)} %get-tuple-element.69), channel_id=1, source_target_pairs={{0,1},{1,0},{2,3},{3,2},{4,5},{5,4},{6,7},{7,6},{8,9},{9,8},{10,11... | collective-permute-start | bytes 165896 | tf_op jit(solution)/shard_map/ppermute | solution.py:285
  5.8 10.3 %copy-start.12 = (s32[8]{0:T(128)S(1)}, s32[8]{0:T(128)}, u32[]{:S(2)}) copy-start(s32[8]{0:T(128)} %constant.247.clone) | copy-start | bytes 100
  5.8 11.0 %copy-start.3 = (f32[2,2]{1,0:T(2,128)S(1)}, f32[2,2]{1,0:T(2,128)}, u32[]{:S(2)}) copy-start(f32[2,2]{1,0:T(2,128)} %param.8) | copy-start | bytes 52
  5.8 31.0 %all-to-all-start = ((bf16[8,32,864]{2,1,0:T(8,128)(2,1)}), bf16[8,32,864]{2,1,0:T(8,128)(2,1)S(1)}, u32[]{:S(2)}, u32[]{:S(2)}) async-start(bf16[8,32,864]{2,1,0:T(8,128)(2,1)} %bitcast.7), calls=%async_computation | async-start | bytes 917504 | tf_op jit(solution)/shard_map/all_to_all | solution.py:286
  17.6 0.7 copy-start.2
  21.7 3.8 %copy-start.1 = (bf16[2,32,864]{2,1,0:T(8,128)(2,1)}, bf16[2,32,864]{2,1,0:T(8,128)(2,1)S(1)}, u32[]{:S(2)}) copy-start(bf16[2,32,864]{2,1,0:T(8,128)(2,1)S(1)} %pad_maximum_fusion.refs_0_) | copy-start | bytes 331780
  21.7 5.3 %collective-permute-start.3 = (bf16[2,32,864]{2,1,0:T(8,128)(2,1)S(1)}, bf16[2,32,864]{2,1,0:T(8,128)(2,1)S(1)}, u32[]{:S(2)}, u32[]{:S(2)}) collective-permute-start(bf16[2,32,864]{2,1,0:T(8,128)(2,1)S(1)} %pad_maximum_fusion.refs_0_), channel_id=1, source_target_pairs={{0,4},{1,5},{4,8},{5,9},{8,12},{9,13},{12,14},{13,15},{14,10},{15,... | collective-permute-start | bytes 331784 | tf_op jit(solution)/shard_map/ppermute | solution.py:263
  23.7 4.8 %collective-permute-start.4 = (bf16[2,32,864]{2,1,0:T(8,128)(2,1)S(1)}, bf16[2,32,864]{2,1,0:T(8,128)(2,1)S(1)}, u32[]{:S(2)}, u32[]{:S(2)}) collective-permute-start(bf16[2,32,864]{2,1,0:T(8,128)(2,1)S(1)} %pad_maximum_fusion.refs_0_), channel_id=1, source_target_pairs={{4,0},{5,1},{8,4},{9,5},{12,8},{13,9},{14,12},{15,13},{10,14},{11,... | collective-permute-start | bytes 331784 | tf_op jit(solution)/shard_map/ppermute | solution.py:267
  27.0 5.3 %copy-start.5 = (bf16[2,32,864]{2,1,0:T(8,128)(2,1)}, bf16[2,32,864]{2,1,0:T(8,128)(2,1)S(1)}, u32[]{:S(2)}) copy-start(bf16[2,32,864]{2,1,0:T(8,128)(2,1)S(1)} %collective-permute-done.3.refs_1_) | copy-start | bytes 331780
  28.5 3.7 %copy-start.6 = (bf16[2,32,864]{2,1,0:T(8,128)(2,1)}, bf16[2,32,864]{2,1,0:T(8,128)(2,1)S(1)}, u32[]{:S(2)}) copy-start(bf16[2,32,864]{2,1,0:T(8,128)(2,1)S(1)} %collective-permute-done.4.refs_2_) | copy-start | bytes 331780
  28.5 4.8 %collective-permute-start.5 = (bf16[2,32,864]{2,1,0:T(8,128)(2,1)S(1)}, bf16[2,32,864]{2,1,0:T(8,128)(2,1)S(1)}, u32[]{:S(2)}, u32[]{:S(2)}) collective-permute-start(bf16[2,32,864]{2,1,0:T(8,128)(2,1)S(1)} %collective-permute-done.3.refs_1_), channel_id=1, source_target_pairs={{0,4},{1,5},{4,8},{5,9},{8,12},{9,13},{12,14},{13,15},{14,10},{15,... | collective-permute-start | bytes 331784 | tf_op jit(solution)/shard_map/ppermute | solution.py:263
  30.0 4.8 %collective-permute-start.6 = (bf16[2,32,864]{2,1,0:T(8,128)(2,1)S(1)}, bf16[2,32,864]{2,1,0:T(8,128)(2,1)S(1)}, u32[]{:S(2)}, u32[]{:S(2)}) collective-permute-start(bf16[2,32,864]{2,1,0:T(8,128)(2,1)S(1)} %collective-permute-done.4.refs_2_), channel_id=1, source_target_pairs={{4,0},{5,1},{8,4},{9,5},{12,8},{13,9},{14,12},{15,13},{10,14},{11,... | collective-permute-start | bytes 331784 | tf_op jit(solution)/shard_map/ppermute | solution.py:267
  33.3 5.2 %copy-start.7 = (bf16[2,32,864]{2,1,0:T(8,128)(2,1)}, bf16[2,32,864]{2,1,0:T(8,128)(2,1)S(1)}, u32[]{:S(2)}) copy-start(bf16[2,32,864]{2,1,0:T(8,128)(2,1)S(1)} %collective-permute-done.5.refs_3_) | copy-start | bytes 331780
  34.8 3.7 %copy-start.8 = (bf16[2,32,864]{2,1,0:T(8,128)(2,1)}, bf16[2,32,864]{2,1,0:T(8,128)(2,1)S(1)}, u32[]{:S(2)}) copy-start(bf16[2,32,864]{2,1,0:T(8,128)(2,1)S(1)} %collective-permute-done.6.refs_4_) | copy-start | bytes 331780
  34.8 4.8 %collective-permute-start.7 = (bf16[2,32,864]{2,1,0:T(8,128)(2,1)S(1)}, bf16[2,32,864]{2,1,0:T(8,128)(2,1)S(1)}, u32[]{:S(2)}, u32[]{:S(2)}) collective-permute-start(bf16[2,32,864]{2,1,0:T(8,128)(2,1)S(1)} %collective-permute-done.5.refs_3_), channel_id=1, source_target_pairs={{0,4},{1,5},{4,8},{5,9},{8,12},{9,13},{12,14},{13,15},{14,10},{15,... | collective-permute-start | bytes 331784 | tf_op jit(solution)/shard_map/ppermute | solution.py:263
  36.3 4.8 %collective-permute-start.8 = (bf16[2,32,864]{2,1,0:T(8,128)(2,1)S(1)}, bf16[2,32,864]{2,1,0:T(8,128)(2,1)S(1)}, u32[]{:S(2)}, u32[]{:S(2)}) collective-permute-start(bf16[2,32,864]{2,1,0:T(8,128)(2,1)S(1)} %collective-permute-done.6.refs_4_), channel_id=1, source_target_pairs={{4,0},{5,1},{8,4},{9,5},{12,8},{13,9},{14,12},{15,13},{10,14},{11,... | collective-permute-start | bytes 331784 | tf_op jit(solution)/shard_map/ppermute | solution.py:267
  36.8 1.7 %copy-start = (bf16[8,32,864]{2,1,0:T(8,128)(2,1)}, bf16[8,32,864]{2,1,0:T(8,128)(2,1)S(1)}, u32[]{:S(2)}) copy-start(bf16[8,32,864]{2,1,0:T(8,128)(2,1)S(1)} %all-to-all-done.emp_own_ref) | copy-start | bytes 1327108
  36.8 9.0 %collective-permute-start.1 = (bf16[8,32,864]{2,1,0:T(8,128)(2,1)S(1)}, bf16[8,32,864]{2,1,0:T(8,128)(2,1)S(1)}, u32[]{:S(2)}, u32[]{:S(2)}) collective-permute-start(bf16[8,32,864]{2,1,0:T(8,128)(2,1)S(1)} %all-to-all-done.emp_own_ref), channel_id=1, source_target_pairs={{0,1},{1,0},{2,3},{3,2},{4,5},{5,4},{6,7},{7,6},{8,9},{9,8},{10,11... | collective-permute-start | bytes 1327112 | tf_op jit(solution)/shard_map/ppermute | solution.py:299
  39.6 4.7 %copy-start.9 = (bf16[2,32,864]{2,1,0:T(8,128)(2,1)}, bf16[2,32,864]{2,1,0:T(8,128)(2,1)S(1)}, u32[]{:S(2)}) copy-start(bf16[2,32,864]{2,1,0:T(8,128)(2,1)S(1)} %collective-permute-done.7.refs_5_) | copy-start | bytes 331780
  41.1 3.3 %copy-start.10 = (bf16[2,32,864]{2,1,0:T(8,128)(2,1)}, bf16[2,32,864]{2,1,0:T(8,128)(2,1)S(1)}, u32[]{:S(2)}) copy-start(bf16[2,32,864]{2,1,0:T(8,128)(2,1)S(1)} %collective-permute-done.8.refs_6_) | copy-start | bytes 331780
  41.1 4.8 %collective-permute-start.9 = (bf16[2,32,864]{2,1,0:T(8,128)(2,1)S(1)}, bf16[2,32,864]{2,1,0:T(8,128)(2,1)S(1)}, u32[]{:S(2)}, u32[]{:S(2)}) collective-permute-start(bf16[2,32,864]{2,1,0:T(8,128)(2,1)S(1)} %collective-permute-done.7.refs_5_), channel_id=1, source_target_pairs={{0,4},{1,5},{4,8},{5,9},{8,12},{9,13},{12,14},{13,15},{14,10},{15,... | collective-permute-start | bytes 331784 | tf_op jit(solution)/shard_map/ppermute | solution.py:263
  45.9 0.6 copy-start.11
  45.9 0.8 copy-start.4
  71.3 2.3 %collective-permute-start.10 = (bf16[8,54,864]{2,0,1:T(8,128)(2,1)S(1)}, bf16[8,54,864]{2,0,1:T(8,128)(2,1)S(1)}, u32[]{:S(2)}, u32[]{:S(2)}) collective-permute-start(bf16[8,54,864]{2,0,1:T(8,128)(2,1)S(1)} %copy.10), channel_id=1, source_target_pairs={{0,1},{1,0},{2,3},{3,2},{4,5},{5,4},{6,7},{7,6},{8,9},{9,8},{10,11... | collective-permute-start | bytes 2239496 | tf_op jit(solution)/shard_map/ppermute | solution.py:331
  75.3 8.3 %collective-permute-start.11 = (bf16[54,864]{1,0:T(8,128)(2,1)S(1)}, bf16[54,864]{1,0:T(8,128)(2,1)S(1)}, u32[]{:S(2)}, u32[]{:S(2)}) collective-permute-start(bf16[54,864]{1,0:T(8,128)(2,1)S(1)} %get-tuple-element.59), channel_id=1, source_target_pairs={{0,2},{1,3},{2,0},{3,1},{4,6},{5,7},{6,4},{7,5},{8,10},{9,11},{10,... | collective-permute-start | bytes 279944 | tf_op jit(solution)/shard_map/ppermute | solution.py:336
  75.9 8.4 %collective-permute-start.17 = (bf16[54,864]{1,0:T(8,128)(2,1)S(1)}, bf16[54,864]{1,0:T(8,128)(2,1)S(1)}, u32[]{:S(2)}, u32[]{:S(2)}) collective-permute-start(bf16[54,864]{1,0:T(8,128)(2,1)S(1)} %get-tuple-element.60), channel_id=1, source_target_pairs={{0,14},{1,15},{2,12},{3,13},{4,10},{5,11},{6,8},{7,9},{8,6},{9,7},... | collective-permute-start | bytes 279944 | tf_op jit(solution)/shard_map/ppermute | solution.py:336
  78.3 13.9 %collective-permute-start.16 = (bf16[54,864]{1,0:T(8,128)(2,1)S(1)}, bf16[54,864]{1,0:T(8,128)(2,1)S(1)}, u32[]{:S(2)}, u32[]{:S(2)}) collective-permute-start(bf16[54,864]{1,0:T(8,128)(2,1)S(1)} %get-tuple-element.61), channel_id=1, source_target_pairs={{0,12},{1,13},{2,14},{3,15},{4,8},{5,9},{6,10},{7,11},{8,4},{9,5},... | collective-permute-start | bytes 279944 | tf_op jit(solution)/shard_map/ppermute | solution.py:336
  80.6 15.3 %collective-permute-start.15 = (bf16[54,864]{1,0:T(8,128)(2,1)S(1)}, bf16[54,864]{1,0:T(8,128)(2,1)S(1)}, u32[]{:S(2)}, u32[]{:S(2)}) collective-permute-start(bf16[54,864]{1,0:T(8,128)(2,1)S(1)} %get-tuple-element.62), channel_id=1, source_target_pairs={{0,10},{1,11},{2,8},{3,9},{4,14},{5,15},{6,12},{7,13},{8,2},{9,3},... | collective-permute-start | bytes 279944 | tf_op jit(solution)/shard_map/ppermute | solution.py:336
  80.6 16.8 %collective-permute-start.14 = (bf16[54,864]{1,0:T(8,128)(2,1)S(1)}, bf16[54,864]{1,0:T(8,128)(2,1)S(1)}, u32[]{:S(2)}, u32[]{:S(2)}) collective-permute-start(bf16[54,864]{1,0:T(8,128)(2,1)S(1)} %get-tuple-element.63), channel_id=1, source_target_pairs={{0,8},{1,9},{2,10},{3,11},{4,12},{5,13},{6,14},{7,15},{8,0},{9,1},... | collective-permute-start | bytes 279944 | tf_op jit(solution)/shard_map/ppermute | solution.py:336
  83.6 13.9 %collective-permute-start.13 = (bf16[54,864]{1,0:T(8,128)(2,1)S(1)}, bf16[54,864]{1,0:T(8,128)(2,1)S(1)}, u32[]{:S(2)}, u32[]{:S(2)}) collective-permute-start(bf16[54,864]{1,0:T(8,128)(2,1)S(1)} %get-tuple-element.64), channel_id=1, source_target_pairs={{0,6},{1,7},{2,4},{3,5},{4,2},{5,3},{6,0},{7,1},{8,14},{9,15},{10,... | collective-permute-start | bytes 279944 | tf_op jit(solution)/shard_map/ppermute | solution.py:336
  84.3 13.9 %collective-permute-start.12 = (bf16[54,864]{1,0:T(8,128)(2,1)S(1)}, bf16[54,864]{1,0:T(8,128)(2,1)S(1)}, u32[]{:S(2)}, u32[]{:S(2)}) collective-permute-start(bf16[54,864]{1,0:T(8,128)(2,1)S(1)} %get-tuple-element.65), channel_id=1, source_target_pairs={{0,4},{1,5},{2,6},{3,7},{4,0},{5,1},{6,2},{7,3},{8,12},{9,13},{10,... | collective-permute-start | bytes 279944 | tf_op jit(solution)/shard_map/ppermute | solution.py:336
where the time goes:
time: 99.7 us; the launch traced here: 99.2 us
  starting transfers between devices  33.4 us (34%)
  Pallas kernels  23.4 us (23%)
  waiting for transfers between devices  18.2 us (18%)
  other arithmetic  15.1 us (15%)
  local copies, waits for them, and re-layouts  8.19 us (8%)
  between operations  1.04 us (1%)
    pallas_call x1, Pallas kernels, pair_moment(): pl.pallas_call(pair_kernel, out_shape=(jax.ShapeDtypeStruct((blocks // 2,...  23.4 us
    ppermute x7, starting transfers between devices, local(): lax.ppermute(parts[distance], 'space', [(d, d ^ 2 * distance) for d in ra...  16.7 us
    convert_element_type x4, other arithmetic, table_piece(): return table.astype(jnp.bfloat16).reshape(4, -1, cos_p.shape[-1])  6.85 us
    ppermute x4, starting transfers between devices, gather_ring(): from_left = lax.ppermute(from_left, 'space', ahead)  6.46 us
    ppermute x7, waiting for transfers between devices, local(): lax.ppermute(parts[distance], 'space', [(d, d ^ 2 * distance) for d in ra...  6.3 us
    all_to_all x1, starting transfers between devices, local(): lax.all_to_all(columns[NOCC:].reshape(chips, own_emp, rows), 'space', spl...  5.97 us
    ppermute x4, waiting for transfers between devices, gather_ring(): from_left = lax.ppermute(from_left, 'space', ahead)  5.15 us
    ppermute x3, waiting for transfers between devices, gather_ring(): from_right = lax.ppermute(from_right, 'space', back)  4.47 us
  transfers between devices with their start and end apart: 19, of which 12 were waited for; matrix products, arithmetic and copies ran while one was open for 18% of the time, Pallas kernels for 0%

commit v1 on v0

v1 whole, which is shorter than its diff:
```python
import functools
import math

import jax
import jax.numpy as jnp
from jax import lax
from jax.experimental import pallas as pl
from jax.experimental.pallas import tpu as pltpu
from jax.sharding import PartitionSpec as P

SIDE = 24
NG = 864
NOCC = 64
NEMP = 256
LANES = 128


def round_up(value, step):
    return -(-value // step) * step


def class_waves(mode_count, grid_side, width, zero):
    first, second = grid_side // 2, grid_side // 4
    third = mode_count // 2 // (first * second)
    shape = (4, width)
    kind = lax.broadcasted_iota(jnp.int32, shape, 0)
    column = lax.broadcasted_iota(jnp.int32, shape, 1) + zero
    a_odd, b_odd = kind // 2, kind % 2
    b_step = column % (second // 2)
    c_step = column // (second // 2) % third
    sine = column // (second // 2 * third) % 2
    a_step = column // (second // 2 * third * 2)
    a_index = 2 * a_step + (a_odd + first // 2) % 2
    b_index = 2 * b_step + (b_odd + second // 2) % 2
    return a_index - first // 2, b_index - second // 2, c_step + 1, sine, column < mode_count // 4


def table_factors(grid_side, mode_count, steps, width, zero):
    half = grid_side // 2
    a, b, c, sine, used = class_waves(mode_count, grid_side, width, zero)
    x = jnp.arange(half, dtype=jnp.int32)
    y = jnp.arange(half, dtype=jnp.int32)
    z = jnp.arange(grid_side, dtype=jnp.int32)
    unit = 2.0 * math.pi / grid_side
    scaling = math.sqrt(2.0 / grid_side**3)
    p = jnp.mod(x[:, None, None] * a, grid_side).astype(jnp.float32) * unit
    p = p.reshape(steps, half // steps, 4, width).transpose(0, 2, 1, 3)
    q = jnp.mod(y[:, None, None] * b, grid_side).astype(jnp.float32) * unit
    s = jnp.mod(z[:, None, None] * c, grid_side).astype(jnp.float32) * unit
    size = jnp.where(used, scaling, 0.0)
    q, s = q.transpose(1, 0, 2)[:, :, None, :], s.transpose(1, 0, 2)[:, None, :, :]
    inner_cos = jnp.cos(q) * jnp.cos(s) - jnp.sin(q) * jnp.sin(s)
    inner_sin = jnp.sin(q) * jnp.cos(s) + jnp.cos(q) * jnp.sin(s)
    is_sine = (sine == 1)[:, None, None, :]
    size = size[:, None, None, :]
    with_cos = jnp.where(is_sine, inner_sin, inner_cos) * size
    with_sin = jnp.where(is_sine, inner_cos, -inner_sin) * size
    flat = (4, 1, half * grid_side, width)
    return jnp.cos(p), jnp.sin(p), with_cos.reshape(flat), with_sin.reshape(flat)


def table_piece(cos_p, sin_p, with_cos, with_sin):
    table = cos_p[:, :, None, :] * with_cos + sin_p[:, :, None, :] * with_sin
    return table.astype(jnp.bfloat16).reshape(4, -1, cos_p.shape[-1])


def pair_kernel(place_ref, weight_ref, emp_own_ref, emp_other_ref, *refs):
    table, table_sem = refs[-2:]
    steps = table_sem.shape[0]
    chips = emp_own_ref.shape[0]
    occ_refs, refs = refs[:chips], refs[chips:]
    tables_hbm, refs = refs[:steps], refs[steps:]
    keep_ref, send_ref, raw_occ, occ_wide, emp_wide, first, second, rho = refs[:-2]
    width = table.shape[2]
    depth = table.shape[1] // steps
    n_occ, n_rows = raw_occ.shape[1:]
    n_emp = emp_own_ref.shape[1]
    per_group = chips // steps
    plane = SIDE * SIDE // 2
    half_pairs = first.shape[1]
    half_occ = n_occ // 2

    used = tables_hbm[0].shape[1]
    copies = [
        pltpu.make_async_copy(tables_hbm[s], table.at[:, pl.ds(s * depth, used)], table_sem.at[s])
        for s in range(steps)
    ]
    for copy in copies:
        copy.start()

    core = place_ref[chips]
    me = place_ref[chips + 1]
    for index, ref in enumerate(occ_refs):
        chip = place_ref[index]
        raw_occ[chip * 2 + core] = ref[0]
        raw_occ[chip * 2 + 1 - core] = ref[1]

    def occ_rows_of(shard):
        return raw_occ[shard].astype(jnp.float32)

    def emp_rows_of(shard):
        own = emp_own_ref[shard // 2].astype(jnp.float32)
        other = emp_other_ref[shard // 2].astype(jnp.float32)
        return jnp.where(core == shard % 2, own, other)

    def halves(rows_of, columns, group, upper):
        pieces = []
        for x in range(3):
            start = (2 * x + upper) * plane
            stop = start + plane
            while start < stop:
                shard, offset = divmod(start, n_rows)
                count = min(stop - start, n_rows - offset)
                pieces.append(rows_of(group * per_group + shard)[:, offset : offset + count])
                start += count
        pieces.append(jnp.zeros((columns, depth - 3 * plane), jnp.float32))
        return jnp.concatenate(pieces, axis=1)

    for far in range(2):
        for step in range(steps):
            lanes = slice(step * depth, (step + 1) * depth)
            for upper in range(2):
                group = far * steps + step
                occ_wide[2 * far + upper, :, lanes] = halves(occ_rows_of, n_occ, group, upper)
                emp_wide[2 * far + upper, :, lanes] = halves(emp_rows_of, n_emp, group, upper).astype(
                    jnp.bfloat16
                )
    for step in range(steps):
        table[:, step * depth + used : (step + 1) * depth, :] = jnp.zeros(
            (4, depth - used, width), jnp.bfloat16
        )

    def build(half, target, cut):
        occ_rows = [occ_wide[k, half * half_occ : (half + 1) * half_occ, cut] for k in range(4)]
        emp_rows = [emp_wide[k, :, cut] for k in range(4)]
        for i in range(half_occ):
            near_low, near_high, far_low, far_high = (
                jnp.broadcast_to(occ_rows[k][i : i + 1], (n_emp, LANES)).astype(jnp.bfloat16) * emp_rows[k]
                for k in range(4)
            )
            even_low, odd_low = near_low + far_low, near_low - far_low
            even_high, odd_high = near_high + far_high, near_high - far_high
            rows = slice(i * n_emp, (i + 1) * n_emp)
            target[0, rows, cut] = even_low + even_high
            target[1, rows, cut] = even_low - even_high
            target[2, rows, cut] = odd_low + odd_high
            target[3, rows, cut] = odd_low - odd_high

    modes = rho.shape[1]
    spacing = SIDE
    per_a = modes // spacing

    def multiply(half, source, k):
        found = jnp.dot(source[k], table[k], preferred_element_type=jnp.float32).T
        a_odd, b_odd = divmod(k, 2)
        a_first = (a_odd + SIDE // 4) % 2
        b_first = (b_odd + SIDE // 8) % 2
        for a_step in range(SIDE // 4):
            start = b_first * (SIDE // 2) + 2 * a_step + a_first
            for tile in range(half_pairs // LANES):
                rho[half * half_pairs // LANES + tile, pl.ds(start, per_a, stride=spacing), :] = found[
                    a_step * per_a : (a_step + 1) * per_a, tile * LANES : (tile + 1) * LANES
                ]

    chunks = steps * depth // LANES

    def build_first(chunk, carry):
        build(0, first, pl.ds(pl.multiple_of(chunk * LANES, LANES), LANES))
        return carry

    lax.fori_loop(0, chunks, build_first, 0)
    for copy in copies:
        copy.wait()
    for k in range(4):
        for chunk in range(k * chunks // 4, (k + 1) * chunks // 4):
            build(1, second, slice(chunk * LANES, (chunk + 1) * LANES))
        multiply(0, first, k)
    for k in range(4):
        multiply(1, second, k)

    tiles = range(rho.shape[0])
    ordered = jnp.concatenate([rho[tile].astype(jnp.bfloat16) for tile in tiles], axis=1)
    weighted = jnp.concatenate(
        [
            (rho[tile] * weight_ref[:, tile * LANES : (tile + 1) * LANES]).astype(jnp.bfloat16)
            for tile in tiles
        ],
        axis=1,
    )
    moment = lax.dot_general(
        weighted, ordered, (((1,), (1,)), ((), ())), preferred_element_type=jnp.float32
    )
    count, rows = 2 * chips, keep_ref.shape[1]
    for own_core in range(2):

        @pl.when(core == own_core)
        def _():
            for k in range(count):
                slot = jnp.bitwise_xor(me, k) // 2
                block = moment[k * rows : (k + 1) * rows]
                if k % 2 == own_core:
                    keep_ref[slot] = block
                else:
                    send_ref[slot] = block.astype(jnp.bfloat16)


def pair_moment(place, weights, occ_blocks, emp_own, emp_other, tables):
    chips, n_emp, n_rows = emp_own.shape
    n_occ = occ_blocks[0].shape[1]
    steps = len(tables)
    _, used, width = tables[0].shape
    depth = round_up(used, LANES)
    pairs = n_occ * n_emp
    blocks = 2 * chips
    rows = NG // blocks
    vmem = pl.BlockSpec(memory_space=pltpu.VMEM)
    hbm = pl.BlockSpec(memory_space=pl.ANY)
    return pl.pallas_call(
        pair_kernel,
        out_shape=(
            jax.ShapeDtypeStruct((blocks // 2, rows, NG), jnp.float32),
            jax.ShapeDtypeStruct((blocks // 2, rows, NG), jnp.bfloat16),
        ),
        in_specs=[pl.BlockSpec(memory_space=pltpu.SMEM), vmem, vmem, vmem] + [vmem] * chips + [hbm] * steps,
        out_specs=(vmem, vmem),
        scratch_shapes=[
            pltpu.VMEM((2 * chips, n_occ, n_rows), jnp.bfloat16),
            pltpu.VMEM((4, n_occ, steps * depth), jnp.float32),
            pltpu.VMEM((4, n_emp, steps * depth), jnp.bfloat16),
            pltpu.VMEM((4, pairs // 2, steps * depth), jnp.bfloat16),
            pltpu.VMEM((4, pairs // 2, steps * depth), jnp.bfloat16),
            pltpu.VMEM((pairs // LANES, NG, LANES), jnp.float32),
            pltpu.VMEM((4, steps * depth, width), jnp.bfloat16),
            pltpu.SemaphoreType.DMA((steps,)),
        ],
        compiler_params=pltpu.CompilerParams(vmem_limit_bytes=60 * 1024 * 1024),
        cost_estimate=pl.CostEstimate(
            flops=2 * steps * 4 * pairs * depth * width, bytes_accessed=16 * 2**20, transcendentals=0
        ),
        name="pair_moment",
    )(place, weights, emp_own, emp_other, *occ_blocks, *tables)


def ring_of(chips):
    return list(range(0, chips, 2)) + list(range(chips - 1, 0, -2))


def gather_ring(block, chips, between):
    ring = ring_of(chips)
    ahead, back = [], []
    for position in range(chips):
        for core in range(2):
            here = 2 * ring[position] + core
            right = 2 * ring[(position + 1) % chips] + core
            ahead.append((here, right))
            back.append((right, here))
    found, offsets, made = [block], [0], []
    from_left = from_right = block
    for hop in range(1, chips // 2 + 1):
        if hop <= len(between):
            function, arguments = between[hop - 1]
            if hop > 1:
                _, arguments = lax.optimization_barrier((from_left, arguments))
            made.append(function(*arguments))
        from_left = lax.ppermute(from_left, "space", ahead)
        found.append(from_left)
        offsets.append(-hop)
        if 2 * hop < chips:
            from_right = lax.ppermute(from_right, "space", back)
            found.append(from_right)
            offsets.append(hop)
    return found, offsets, made


def local(space, tm, orbitals, gaps, times, cos_weights):
    rows = orbitals.shape[0]
    chips = space // 2
    columns = orbitals.T
    own_occ, own_emp = NOCC // 2, NEMP // chips
    me = lax.axis_index("space")
    core, chip = me % 2, me // 2
    swap = [(d, d ^ 1) for d in range(space)]

    occ = columns[:NOCC].reshape(2, own_occ, rows)
    occ_mine = lax.dynamic_index_in_dim(occ, core, 0, keepdims=False)
    occ_theirs = lax.dynamic_index_in_dim(occ, 1 - core, 0, keepdims=False)
    occ_pair = jnp.stack([occ_mine, lax.ppermute(occ_theirs, "space", swap)])
    emp_own = lax.all_to_all(
        columns[NOCC:].reshape(chips, own_emp, rows),
        "space",
        split_axis=0,
        concat_axis=0,
        axis_index_groups=[[2 * k + c for k in range(chips)] for c in range(2)],
    )
    _, gaps, cos_weights, zero = lax.optimization_barrier((occ_pair, gaps, cos_weights, jnp.int32(0)))
    planes = 3
    steps = SIDE // 2 // planes
    width = round_up(NG // 4, 2 * LANES)
    cos_p, sin_p, with_cos, with_sin = table_factors(SIDE, NG, steps, width, zero)
    between = [(table_piece, (cos_p[k], sin_p[k], with_cos, with_sin)) for k in range(steps)]
    occ_blocks, offsets, tables = gather_ring(occ_pair, chips, between)
    emp_other = lax.ppermute(emp_own, "space", swap)

    position = jnp.where(chip % 2 == 0, chip // 2, chips - (chip + 1) // 2)
    places = (position + jnp.array(offsets, jnp.int32) + zero) % chips
    on_ring = jnp.where(places < chips // 2, 2 * places, 2 * (chips - places) - 1)
    place = jnp.concatenate([on_ring, jnp.stack([core, me])]).astype(jnp.int32)

    own_count = cos_weights.shape[0] // tm
    tm_index = lax.axis_index("tm")
    pair_weights = 0.0
    for hop in range(tm):
        source = (tm_index + hop) % tm
        their_times = times
        if hop:
            their_times = lax.ppermute(times, "tm", [((d + hop) % tm, d) for d in range(tm)])
        factors = jnp.exp(-gaps[None, :] * their_times[:, None])
        occ_factors = lax.dynamic_slice_in_dim(factors, core * own_occ, own_occ, 1) * NOCC ** (-0.5)
        emp_factors = lax.dynamic_slice_in_dim(factors, NOCC + chip * own_emp, own_emp, 1) * NEMP ** (-0.5)
        weights = lax.dynamic_slice(
            cos_weights,
            (tm_index * own_count, source * times.shape[0]),
            (own_count, times.shape[0]),
        )
        pair_weights = pair_weights + jnp.sum(
            weights[:, :, None, None] * (occ_factors[:, :, None] * emp_factors[:, None, :])[None], axis=1
        )
    pair_weights = pair_weights.reshape(own_count, 1, own_occ * own_emp)

    results = []
    for w in range(own_count):
        keep, send = pair_moment(place, pair_weights[w], occ_blocks, emp_own, emp_other, tables)
        received = lax.ppermute(send, "space", swap)
        total = keep + received.astype(jnp.float32)
        parts = total.astype(jnp.bfloat16)
        result = total[0]
        for distance in range(1, chips):
            part = lax.ppermute(
                parts[distance], "space", [(d, d ^ (2 * distance)) for d in range(space)]
            )
            result = result + part.astype(jnp.float32)
        results.append(result)
    return jnp.stack(results)


def solution(mesh):
    return jax.shard_map(
        functools.partial(local, mesh.shape["space"], mesh.shape["tm"]),
        mesh=mesh,
        in_specs=(P("space", None), P(), P("tm"), P()),
        out_specs=P("tm", "space", None),
        check_vma=False,
    )
```

time: 99.7 us -> 93.4 us (0.937)
  waiting for transfers between devices: 18.2 us -> 10.8 us
  Pallas kernels: 23.4 us -> 17.7 us
  other arithmetic: 15.1 us -> 18.7 us
  starting transfers between devices: 33.4 us -> 35.7 us
    pallas_call x1, Pallas kernels: 23.4 us -> 17.7 us  [pair_moment(): pl.pallas_call(pair_kernel, out_shape=(jax.ShapeDtypeStruct((blocks // 2,...]
    ppermute x3, waiting for transfers between devices: 4.47 us -> 0.83 us  [gather_ring(): from_right = lax.ppermute(from_right, 'space', back)]
    ppermute x4, waiting for transfers between devices: 5.15 us -> 2.62 us  [gather_ring(): from_left = lax.ppermute(from_left, 'space', ahead)]
    ppermute x7, starting transfers between devices: 16.7 us -> 18.6 us  [local(): lax.ppermute(parts[distance], 'space', [(d, d ^ 2 * distance) for d in ra...]
    convert_element_type x1 -> x0, other arithmetic: 1.66 us -> none  [column_order(): (row == jnp.arange(mode_count, dtype=jnp.int32)[None, :]).astype(jnp.bflo...]
    mul x0 -> x1, other arithmetic: none -> 1.29 us  [table_factors(): with_cos = jnp.where(is_sine, inner_sin, inner_cos) * size]
    ppermute x7, waiting for transfers between devices: 6.3 us -> 5.09 us  [local(): lax.ppermute(parts[distance], 'space', [(d, d ^ 2 * distance) for d in ra...]
    convert_element_type x4, other arithmetic: 6.85 us -> 8.04 us  [table_piece(): return table.astype(jnp.bfloat16).reshape(4, -1, cos_p.shape[-1])]
  transfers between devices with their start and end apart: 19 -> 19, of which waited for: 12 -> 8; matrix products, arithmetic and copies ran while one was open for 18% -> 25% of each run, Pallas kernels for 0% -> 0%
where the time goes in v1:
time: 93.4 us; the launch traced here: 92.9 us
  starting transfers between devices  35.7 us (38%)
  other arithmetic  18.7 us (20%)
  Pallas kernels  17.7 us (19%)
  waiting for transfers between devices  10.8 us (12%)
  local copies, waits for them, and re-layouts  9.06 us (10%)
  between operations  0.96 us (1%)
    ppermute x7, starting transfers between devices, local(): lax.ppermute(parts[distance], 'space', [(d, d ^ 2 * distance) for d in ra...  18.6 us
    pallas_call x1, Pallas kernels, pair_moment(): pl.pallas_call(pair_kernel, out_shape=(jax.ShapeDtypeStruct((blocks // 2,...  17.7 us
    convert_element_type x4, other arithmetic, table_piece(): return table.astype(jnp.bfloat16).reshape(4, -1, cos_p.shape[-1])  8.04 us
    ppermute x4, starting transfers between devices, gather_ring(): from_left = lax.ppermute(from_left, 'space', ahead)  5.95 us
    all_to_all x1, starting transfers between devices, local(): lax.all_to_all(columns[NOCC:].reshape(chips, own_emp, rows), 'space', spl...  5.83 us
    ppermute x7, waiting for transfers between devices, local(): lax.ppermute(parts[distance], 'space', [(d, d ^ 2 * distance) for d in ra...  5.09 us
    ppermute x1, starting transfers between devices, local(): lax.ppermute(times, 'tm', [((d + hop) % tm, d) for d in range(tm)])  2.94 us
    ppermute x4, waiting for transfers between devices, gather_ring(): from_left = lax.ppermute(from_left, 'space', ahead)  2.62 us
  transfers between devices with their start and end apart: 19, of which 8 were waited for; matrix products, arithmetic and copies ran while one was open for 25% of the time, Pallas kernels for 0%

profile of v1, /device:TPU:0, one launch (start us, length us, event | category | flops | bytes accessed | tf_op | source)
XLA Modules:
  0.0 92.9 jit_solution(622987750154674820)
XLA Ops:
  0.0 2.9 %collective-permute-start.1 = (f32[1]{0:T(128)}, f32[1]{0:T(128)}, u32[]{:S(2)}, u32[]{:S(2)}) collective-permute-start(f32[1]{0:T(128)} %param.7), channel_id=1, source_target_pairs={{16,0},{0,16},{17,1},{1,17},{18,2},{2,18},{19,3},{3,19},{20,4},{4,... | collective-permute-start | bytes 20 | tf_op jit(solution)/shard_map/ppermute | solution.py:316
  2.9 0.9 slice.72
  3.9 0.1 collective-permute-start
  4.0 1.8 %slice.73 = bf16[256,864]{1,0:T(8,128)(2,1)} slice(bf16[320,864]{1,0:T(8,128)(2,1)} %bitcast.110), slice={[64:320], [0:864]} | slice | bytes 884736 | tf_op jit(solution)/shard_map/slice | solution.py:289
  5.8 5.8 %all-to-all-start = ((bf16[8,32,864]{2,1,0:T(8,128)(2,1)}), bf16[8,32,864]{2,1,0:T(8,128)(2,1)}, u32[]{:S(2)}, u32[]{:S(2)}) async-start(bf16[8,32,864]{2,1,0:T(8,128)(2,1)} %bitcast.10), calls=%async_computation | async-start | bytes 917504 | tf_op jit(solution)/shard_map/all_to_all | solution.py:288
  11.6 0.5 iota_shift-right-logical_fusion
  12.2 0.5 compare_and_fusion
  13.4 0.7 pad_maximum_fusion.refs_0_
  14.1 2.1 %collective-permute-start.4 = (bf16[2,32,864]{2,1,0:T(8,128)(2,1)}, bf16[2,32,864]{2,1,0:T(8,128)(2,1)}, u32[]{:S(2)}, u32[]{:S(2)}) collective-permute-start(bf16[2,32,864]{2,1,0:T(8,128)(2,1)} %pad_maximum_fusion.refs_0_), channel_id=1, source_target_pairs={{4,0},{5,1},{8,4},{9,5},{12,8},{13,9},{14,12},{15,13},{10,14},{11,... | collective-permute-start | bytes 331784 | tf_op jit(solution)/shard_map/ppermute | solution.py:269
  16.2 0.1 collective-permute-start.3
  16.3 0.1 fusion.39
  16.4 0.3 fusion.26
  16.7 0.4 fusion.17
  17.1 0.3 multiply_add_fusion
  17.4 0.3 fusion.1
  17.7 0.0 copy-start.5
  17.7 0.0 copy-start.7
  17.7 0.0 copy-start.11
  17.8 1.3 %fusion.2 = (f32[4,288,256]{2,1,0:T(8,128)S(1)}, f32[4,288,256]{2,1,0:T(8,128)}) fusion(f32[4,12,24,256]{3,2,1,0:T(8,128)S(1)} %get-tuple-element.53, f32[4,12,24,256]{3,2,1,0:T(8,128)S(1)} %get-tuple-element.52, f32[256]{0:T(256)S(1)} %compare_select_fusion.2, pred[4,256]{1,0:T(4,128)(4,1)S(1)} %fusion.36), kind=kLoop, calls=%fused_computation.12 | loop fusion | flops 1474560 | bytes 4720640 | tf_op jit(solution)/shard_map/mul | solution.py:56
  19.1 0.1 fusion.35
  19.1 0.6 fusion.32
  19.7 0.6 slice_bitcast_fusion.9
  20.4 0.6 slice_bitcast_fusion.8
  21.0 0.6 multiply_exponential_fusion.1
  21.7 0.6 fusion.52
  22.3 0.1 dynamic-slice_multiply_fusion.1
  22.4 1.9 %multiply_add_fusion.1 = f32[32,1,32]{2,0,1:T(8,128)} fusion(f32[32]{0:T(128)S(1)} %get-tuple-element.75, f32[32]{0:T(128)S(1)} %get-tuple-element.74, f32[]{:T(128)} %bitcast.8, f32[32]{0:T(128)S(1)} %get-tuple-element.92, f32[32]{0:T(128)S(1)} %get-tuple-element.93, f32[]{:T(128)} %bitcast.6), kind=kLoop, calls=%fused_computation.70 | loop fusion | flops 5120 | bytes 4616 | tf_op jit(solution)/shard_map/add | solution.py:325
  24.3 0.5 compare_select_fusion.3
  24.8 1.4 %add.313.weight_ref = f32[1,1024]{1,0:T(1,128)} reshape(f32[32,1,32]{2,0,1:T(8,128)} %multiply_add_fusion.1) | data formatting | bytes 8192 | tf_op jit(solution)/shard_map/add | solution.py:325
  26.2 3.0 %add_convert_fusion.3 = bf16[4,3,288,256]{3,2,1,0:T(8,128)(2,1)} fusion(f32[4,288,256]{2,1,0:T(8,128)} %get-tuple-element.44, f32[4,3,256]{2,1,0:T(4,128)} %get-tuple-element.59, f32[4,288,256]{2,1,0:T(8,128)S(1)} %get-tuple-element.43, f32[4,3,256]{2,1,0:T(4,128)} %get-tuple-element.63), kind=kLoop, calls=%fused_computation.3 | loop fusion | flops 3538944 | bytes 4153344 | tf_op jit(solution)/shard_map/convert_element_type | solution.py:64
  29.3 0.7 pad_add_fusion.place_ref
  29.9 2.0 %collective-permute-start.5 = (bf16[2,32,864]{2,1,0:T(8,128)(2,1)}, bf16[2,32,864]{2,1,0:T(8,128)(2,1)S(1)}, u32[]{:S(2)}, u32[]{:S(2)}) collective-permute-start(bf16[2,32,864]{2,1,0:T(8,128)(2,1)} %collective-permute-done.3.refs_1_), channel_id=1, source_target_pairs={{0,4},{1,5},{4,8},{5,9},{8,12},{9,13},{12,14},{13,15},{14,10},{15,... | collective-permute-start | bytes 331784 | tf_op jit(solution)/shard_map/ppermute | solution.py:265
  31.9 1.7 %add_convert_fusion.2 = bf16[4,3,288,256]{3,2,1,0:T(8,128)(2,1)} fusion(f32[4,288,256]{2,1,0:T(8,128)S(1)} %bitcast.99, f32[4,3,256]{2,1,0:T(4,128)S(1)} %copy-done.4, f32[4,288,256]{2,1,0:T(8,128)S(1)} %bitcast.102, f32[4,3,256]{2,1,0:T(4,128)S(1)} %copy-done.3), kind=kLoop, calls=%fused_computation.2 | loop fusion | flops 3538944 | bytes 4153344 | tf_op jit(solution)/shard_map/convert_element_type | solution.py:64
  33.6 0.1 collective-permute-start.6
  33.6 1.3 %collective-permute-done.5.refs_3_ = bf16[2,32,864]{2,1,0:T(8,128)(2,1)S(1)} collective-permute-done((bf16[2,32,864]{2,1,0:T(8,128)(2,1)}, bf16[2,32,864]{2,1,0:T(8,128)(2,1)S(1)}, u32[]{:S(2)}, u32[]{:S(2)}) %collective-permute-start.5) | collective-permute-done | bytes 110624 | tf_op jit(solution)/shard_map/ppermute | solution.py:265
  34.9 2.0 %collective-permute-start.7 = (bf16[2,32,864]{2,1,0:T(8,128)(2,1)S(1)}, bf16[2,32,864]{2,1,0:T(8,128)(2,1)S(1)}, u32[]{:S(2)}, u32[]{:S(2)}) collective-permute-start(bf16[2,32,864]{2,1,0:T(8,128)(2,1)S(1)} %collective-permute-done.5.refs_3_), channel_id=1, source_target_pairs={{0,4},{1,5},{4,8},{5,9},{8,12},{9,13},{12,14},{13,15},{14,10},{15,... | collective-permute-start | bytes 331784 | tf_op jit(solution)/shard_map/ppermute | solution.py:265
  36.9 1.7 %add_convert_fusion.1 = bf16[4,3,288,256]{3,2,1,0:T(8,128)(2,1)} fusion(f32[4,288,256]{2,1,0:T(8,128)S(1)} %bitcast.100, f32[4,3,256]{2,1,0:T(4,128)S(1)} %copy-done.2, f32[4,288,256]{2,1,0:T(8,128)S(1)} %bitcast.103, f32[4,3,256]{2,1,0:T(4,128)S(1)} %copy-done.1), kind=kLoop, calls=%fused_computation.1 | loop fusion | flops 3538944 | bytes 4153344 | tf_op jit(solution)/shard_map/convert_element_type | solution.py:64
  38.6 0.1 collective-permute-start.8
  38.7 1.0 %collective-permute-done.7.refs_5_ = bf16[2,32,864]{2,1,0:T(8,128)(2,1)S(1)} collective-permute-done((bf16[2,32,864]{2,1,0:T(8,128)(2,1)S(1)}, bf16[2,32,864]{2,1,0:T(8,128)(2,1)S(1)}, u32[]{:S(2)}, u32[]{:S(2)}) %collective-permute-start.7) | collective-permute-done | bytes 110624 | tf_op jit(solution)/shard_map/ppermute | solution.py:265
  39.7 2.0 %collective-permute-start.9 = (bf16[2,32,864]{2,1,0:T(8,128)(2,1)S(1)}, bf16[2,32,864]{2,1,0:T(8,128)(2,1)S(1)}, u32[]{:S(2)}, u32[]{:S(2)}) collective-permute-start(bf16[2,32,864]{2,1,0:T(8,128)(2,1)S(1)} %collective-permute-done.7.refs_5_), channel_id=1, source_target_pairs={{0,4},{1,5},{4,8},{5,9},{8,12},{9,13},{12,14},{13,15},{14,10},{15,... | collective-permute-start | bytes 331784 | tf_op jit(solution)/shard_map/ppermute | solution.py:265
  41.7 1.7 %add_convert_fusion = bf16[4,3,288,256]{3,2,1,0:T(8,128)(2,1)} fusion(f32[4,288,256]{2,1,0:T(8,128)S(1)} %bitcast.101, f32[4,3,256]{2,1,0:T(4,128)S(1)} %copy-done, f32[4,288,256]{2,1,0:T(8,128)S(1)} %bitcast.104, f32[4,3,256]{2,1,0:T(4,128)S(1)} %get-tuple-element.33), kind=kLoop, calls=%fused_computation | loop fusion | flops 3538944 | bytes 4153344 | tf_op jit(solution)/shard_map/convert_element_type | solution.py:64
  43.4 0.8 collective-permute-done.8.refs_6_
  44.2 0.3 collective-permute-done.9.refs_7_
  44.5 0.3 copy-done.16
  44.8 0.3 copy-done.17
  45.2 0.2 copy-done.12
  45.3 17.7 %pair_moment.1 = (f32[8,54,864]{2,1,0:T(8,128)}, bf16[8,54,864]{2,1,0:T(8,128)(2,1)}) custom-call(s32[10]{0:T(128)} %pad_add_fusion.place_ref, f32[1,1024]{1,0:T(1,128)} %add.313.weight_ref, bf16[8,32,864]{2,1,0:T(8,128)(2,1)} %all-to-all-done.emp_own_ref, bf16[8,32,864]{2,1,0:T(8,128)(2,1)} %copy-done.12, bf16[2,32,864]{2,1,0:T(8,128)(2,1)} %pad_maximum_fusion.refs_0_, ...), custom_call_target="tpu_custom_call" | custom-call | flops 7516192768 | bytes 16777216 | tf_op jit(solution)/shard_map/pair_moment/pallas_call | solution.py:218
  63.1 1.2 %copy.7 = bf16[8,54,864]{2,0,1:T(8,128)(2,1)S(1)} copy(bf16[8,54,864]{2,1,0:T(8,128)(2,1)} %get-tuple-element.38) | data formatting | bytes 1492992 | tf_op jit(solution)/shard_map/pair_moment/pallas_call | solution.py:218
  64.3 0.1 collective-permute-start.10
  64.4 2.3 %collective-permute-done.10 = bf16[8,54,864]{2,0,1:T(8,128)(2,1)S(1)} collective-permute-done((bf16[8,54,864]{2,0,1:T(8,128)(2,1)S(1)}, bf16[8,54,864]{2,0,1:T(8,128)(2,1)S(1)}, u32[]{:S(2)}, u32[]{:S(2)}) %collective-permute-start.10) | collective-permute-done | bytes 746528 | tf_op jit(solution)/shard_map/ppermute | solution.py:333
  66.6 1.6 %fusion.51 = (bf16[8,54,864]{2,1,0:T(8,128)(2,1)S(1)}, f32[8,54,864]{2,1,0:T(8,128)S(1)}) fusion(f32[8,54,864]{2,1,0:T(8,128)} %get-tuple-element.37, bf16[8,54,864]{2,0,1:T(8,128)(2,1)S(1)} %collective-permute-done.10), kind=kLoop, calls=%fused_computation.133 | loop fusion | flops 1119744 | bytes 4478976 | tf_op jit(solution)/shard_map/convert_element_type | solution.py:335
  68.2 0.1 slice_bitcast_fusion.7
  68.3 2.0 %collective-permute-start.11 = (bf16[54,864]{1,0:T(8,128)(2,1)S(1)}, bf16[54,864]{1,0:T(8,128)(2,1)S(1)}, u32[]{:S(2)}, u32[]{:S(2)}) collective-permute-start(bf16[54,864]{1,0:T(8,128)(2,1)S(1)} %get-tuple-element.45), channel_id=1, source_target_pairs={{0,2},{1,3},{2,0},{3,1},{4,6},{5,7},{6,4},{7,5},{8,10},{9,11},{10,... | collective-permute-start | bytes 279944 | tf_op jit(solution)/shard_map/ppermute | solution.py:338
  70.3 3.3 %collective-permute-start.17 = (bf16[54,864]{1,0:T(8,128)(2,1)S(1)}, bf16[54,864]{1,0:T(8,128)(2,1)S(1)}, u32[]{:S(2)}, u32[]{:S(2)}) collective-permute-start(bf16[54,864]{1,0:T(8,128)(2,1)S(1)} %get-tuple-element.46), channel_id=1, source_target_pairs={{0,14},{1,15},{2,12},{3,13},{4,10},{5,11},{6,8},{7,9},{8,6},{9,7},... | collective-permute-start | bytes 279944 | tf_op jit(solution)/shard_map/ppermute | solution.py:338
  73.6 0.1 collective-permute-start.16
  73.6 2.0 %collective-permute-start.15 = (bf16[54,864]{1,0:T(8,128)(2,1)S(1)}, bf16[54,864]{1,0:T(8,128)(2,1)S(1)}, u32[]{:S(2)}, u32[]{:S(2)}) collective-permute-start(bf16[54,864]{1,0:T(8,128)(2,1)S(1)} %get-tuple-element.48), channel_id=1, source_target_pairs={{0,10},{1,11},{2,8},{3,9},{4,14},{5,15},{6,12},{7,13},{8,2},{9,3},... | collective-permute-start | bytes 279944 | tf_op jit(solution)/shard_map/ppermute | solution.py:338
  75.6 2.4 %collective-permute-start.14 = (bf16[54,864]{1,0:T(8,128)(2,1)S(1)}, bf16[54,864]{1,0:T(8,128)(2,1)S(1)}, u32[]{:S(2)}, u32[]{:S(2)}) collective-permute-start(bf16[54,864]{1,0:T(8,128)(2,1)S(1)} %get-tuple-element.49), channel_id=1, source_target_pairs={{0,8},{1,9},{2,10},{3,11},{4,12},{5,13},{6,14},{7,15},{8,0},{9,1},... | collective-permute-start | bytes 279944 | tf_op jit(solution)/shard_map/ppermute | solution.py:338
  78.0 0.9 collective-permute-start.13
  78.9 8.0 %collective-permute-start.12 = (bf16[54,864]{1,0:T(8,128)(2,1)S(1)}, bf16[54,864]{1,0:T(8,128)(2,1)S(1)}, u32[]{:S(2)}, u32[]{:S(2)}) collective-permute-start(bf16[54,864]{1,0:T(8,128)(2,1)S(1)} %get-tuple-element.51), channel_id=1, source_target_pairs={{0,4},{1,5},{2,6},{3,7},{4,0},{5,1},{6,2},{7,3},{8,12},{9,13},{10,... | collective-permute-start | bytes 279944 | tf_op jit(solution)/shard_map/ppermute | solution.py:338
  86.8 3.9 %collective-permute-done.15 = bf16[54,864]{1,0:T(8,128)(2,1)S(1)} collective-permute-done((bf16[54,864]{1,0:T(8,128)(2,1)S(1)}, bf16[54,864]{1,0:T(8,128)(2,1)S(1)}, u32[]{:S(2)}, u32[]{:S(2)}) %collective-permute-start.15) | collective-permute-done | bytes 93344 | tf_op jit(solution)/shard_map/ppermute | solution.py:338
  90.7 0.3 collective-permute-done.14
  91.0 1.0 %collective-permute-done.12 = bf16[54,864]{1,0:T(8,128)(2,1)S(1)} collective-permute-done((bf16[54,864]{1,0:T(8,128)(2,1)S(1)}, bf16[54,864]{1,0:T(8,128)(2,1)S(1)}, u32[]{:S(2)}, u32[]{:S(2)}) %collective-permute-start.12) | collective-permute-done | bytes 93344 | tf_op jit(solution)/shard_map/ppermute | solution.py:338
  91.9 0.1 fusion.11
  92.1 0.9 copy.9
  (54 shorter events, 0.2 us)
Async XLA Ops:
  0.0 21.0 %collective-permute-start.1 = (f32[1]{0:T(128)}, f32[1]{0:T(128)}, u32[]{:S(2)}, u32[]{:S(2)}) collective-permute-start(f32[1]{0:T(128)} %param.7), channel_id=1, source_target_pairs={{16,0},{0,16},{17,1},{1,17},{18,2},{2,18},{19,3},{3,19},{20,4},{4,... | collective-permute-start | bytes 20 | tf_op jit(solution)/shard_map/ppermute | solution.py:316
  3.9 9.5 %collective-permute-start = (bf16[32,864]{1,0:T(8,128)(2,1)S(1)}, bf16[32,864]{1,0:T(8,128)(2,1)S(1)}, u32[]{:S(2)}, u32[]{:S(2)}) collective-permute-start(bf16[32,864]{1,0:T(8,128)(2,1)S(1)} %get-tuple-element.55), channel_id=1, source_target_pairs={{0,1},{1,0},{2,3},{3,2},{4,5},{5,4},{6,7},{7,6},{8,9},{9,8},{10,11... | collective-permute-start | bytes 165896 | tf_op jit(solution)/shard_map/ppermute | solution.py:287
  5.8 31.1 %all-to-all-start = ((bf16[8,32,864]{2,1,0:T(8,128)(2,1)}), bf16[8,32,864]{2,1,0:T(8,128)(2,1)}, u32[]{:S(2)}, u32[]{:S(2)}) async-start(bf16[8,32,864]{2,1,0:T(8,128)(2,1)} %bitcast.10), calls=%async_computation | async-start | bytes 917504 | tf_op jit(solution)/shard_map/all_to_all | solution.py:288
  14.1 19.4 %collective-permute-start.4 = (bf16[2,32,864]{2,1,0:T(8,128)(2,1)}, bf16[2,32,864]{2,1,0:T(8,128)(2,1)}, u32[]{:S(2)}, u32[]{:S(2)}) collective-permute-start(bf16[2,32,864]{2,1,0:T(8,128)(2,1)} %pad_maximum_fusion.refs_0_), channel_id=1, source_target_pairs={{4,0},{5,1},{8,4},{9,5},{12,8},{13,9},{14,12},{15,13},{10,14},{11,... | collective-permute-start | bytes 331784 | tf_op jit(solution)/shard_map/ppermute | solution.py:269
  16.2 13.7 %collective-permute-start.3 = (bf16[2,32,864]{2,1,0:T(8,128)(2,1)}, bf16[2,32,864]{2,1,0:T(8,128)(2,1)}, u32[]{:S(2)}, u32[]{:S(2)}) collective-permute-start(bf16[2,32,864]{2,1,0:T(8,128)(2,1)} %pad_maximum_fusion.refs_0_), channel_id=1, source_target_pairs={{0,4},{1,5},{4,8},{5,9},{8,12},{9,13},{12,14},{13,15},{14,10},{15,... | collective-permute-start | bytes 331784 | tf_op jit(solution)/shard_map/ppermute | solution.py:265
  17.7 1.4 %copy-start.8 = (s32[4]{0:T(128)S(1)}, s32[4]{0:T(128)}, u32[]{:S(2)}) copy-start(s32[4]{0:T(128)} %get-tuple-element.96) | copy-start | bytes 52
  17.7 1.3 %copy-start.9 = (s32[4]{0:T(128)S(1)}, s32[4]{0:T(128)}, u32[]{:S(2)}) copy-start(s32[4]{0:T(128)} %get-tuple-element.97) | copy-start | bytes 52
  17.7 1.3 %copy-start.10 = (pred[4]{0:T(512)(128)(4,1)S(1)}, pred[4]{0:T(512)(128)(4,1)}, u32[]{:S(2)}) copy-start(pred[4]{0:T(512)(128)(4,1)} %get-tuple-element.79) | copy-start | bytes 16
  17.7 3.3 %copy-start.5 = (f32[320]{0:T(512)S(1)}, f32[320]{0:T(512)}, u32[]{:S(2)}) copy-start(f32[320]{0:T(512)} %param.6) | copy-start | bytes 3844
  17.7 3.9 %copy-start.7 = (f32[2,2]{1,0:T(2,128)S(1)}, f32[2,2]{1,0:T(2,128)}, u32[]{:S(2)}) copy-start(f32[2,2]{1,0:T(2,128)} %param.8) | copy-start | bytes 52
  17.7 6.5 %copy-start.11 = (s32[8]{0:T(128)S(1)}, s32[8]{0:T(128)}, u32[]{:S(2)}) copy-start(s32[8]{0:T(128)} %constant.209.clone) | copy-start | bytes 100
  26.2 3.0 %copy-start.6 = (s32[8]{0:T(128)S(1)}, s32[8]{0:T(128)}, u32[]{:S(2)}) copy-start(s32[8]{0:T(128)} %compare_select_fusion.3) | copy-start | bytes 100
  26.2 5.7 %copy-start.3 = (f32[4,3,256]{2,1,0:T(4,128)S(1)}, f32[4,3,256]{2,1,0:T(4,128)}, u32[]{:S(2)}) copy-start(f32[4,3,256]{2,1,0:T(4,128)} %get-tuple-element.25) | copy-start | bytes 36868
  26.2 5.7 %copy-start.4 = (f32[4,3,256]{2,1,0:T(4,128)S(1)}, f32[4,3,256]{2,1,0:T(4,128)}, u32[]{:S(2)}) copy-start(f32[4,3,256]{2,1,0:T(4,128)} %get-tuple-element.27) | copy-start | bytes 36868
  29.9 5.0 %collective-permute-start.5 = (bf16[2,32,864]{2,1,0:T(8,128)(2,1)}, bf16[2,32,864]{2,1,0:T(8,128)(2,1)S(1)}, u32[]{:S(2)}, u32[]{:S(2)}) collective-permute-start(bf16[2,32,864]{2,1,0:T(8,128)(2,1)} %collective-permute-done.3.refs_1_), channel_id=1, source_target_pairs={{0,4},{1,5},{4,8},{5,9},{8,12},{9,13},{12,14},{13,15},{14,10},{15,... | collective-permute-start | bytes 331784 | tf_op jit(solution)/shard_map/ppermute | solution.py:265
  31.9 5.0 %copy-start.1 = (f32[4,3,256]{2,1,0:T(4,128)S(1)}, f32[4,3,256]{2,1,0:T(4,128)}, u32[]{:S(2)}) copy-start(f32[4,3,256]{2,1,0:T(4,128)} %get-tuple-element.29) | copy-start | bytes 36868
  31.9 5.0 %copy-start.2 = (f32[4,3,256]{2,1,0:T(4,128)S(1)}, f32[4,3,256]{2,1,0:T(4,128)}, u32[]{:S(2)}) copy-start(f32[4,3,256]{2,1,0:T(4,128)} %get-tuple-element.31) | copy-start | bytes 36868
  33.6 5.0 %collective-permute-start.6 = (bf16[2,32,864]{2,1,0:T(8,128)(2,1)}, bf16[2,32,864]{2,1,0:T(8,128)(2,1)S(1)}, u32[]{:S(2)}, u32[]{:S(2)}) collective-permute-start(bf16[2,32,864]{2,1,0:T(8,128)(2,1)} %collective-permute-done.4.refs_2_), channel_id=1, source_target_pairs={{4,0},{5,1},{8,4},{9,5},{12,8},{13,9},{14,12},{15,13},{10,14},{11,... | collective-permute-start | bytes 331784 | tf_op jit(solution)/shard_map/ppermute | solution.py:269
  34.9 3.7 %copy-start.13 = (bf16[2,32,864]{2,1,0:T(8,128)(2,1)}, bf16[2,32,864]{2,1,0:T(8,128)(2,1)S(1)}, u32[]{:S(2)}) copy-start(bf16[2,32,864]{2,1,0:T(8,128)(2,1)S(1)} %collective-permute-done.5.refs_3_) | copy-start | bytes 331780
  34.9 4.8 %collective-permute-start.7 = (bf16[2,32,864]{2,1,0:T(8,128)(2,1)S(1)}, bf16[2,32,864]{2,1,0:T(8,128)(2,1)S(1)}, u32[]{:S(2)}, u32[]{:S(2)}) collective-permute-start(bf16[2,32,864]{2,1,0:T(8,128)(2,1)S(1)} %collective-permute-done.5.refs_3_), channel_id=1, source_target_pairs={{0,4},{1,5},{4,8},{5,9},{8,12},{9,13},{12,14},{13,15},{14,10},{15,... | collective-permute-start | bytes 331784 | tf_op jit(solution)/shard_map/ppermute | solution.py:265
  36.9 7.6 %collective-permute-start.2 = (bf16[8,32,864]{2,1,0:T(8,128)(2,1)}, bf16[8,32,864]{2,1,0:T(8,128)(2,1)S(1)}, u32[]{:S(2)}, u32[]{:S(2)}) collective-permute-start(bf16[8,32,864]{2,1,0:T(8,128)(2,1)} %all-to-all-done.emp_own_ref), channel_id=1, source_target_pairs={{0,1},{1,0},{2,3},{3,2},{4,5},{5,4},{6,7},{7,6},{8,9},{9,8},{10,11... | collective-permute-start | bytes 1327112 | tf_op jit(solution)/shard_map/ppermute | solution.py:302
  36.9 4.8 %copy-start = (f32[4,3,256]{2,1,0:T(4,128)S(1)}, f32[4,3,256]{2,1,0:T(4,128)}, u32[]{:S(2)}) copy-start(f32[4,3,256]{2,1,0:T(4,128)} %get-tuple-element.35) | copy-start | bytes 36868
  38.6 4.8 %copy-start.14 = (bf16[2,32,864]{2,1,0:T(8,128)(2,1)}, bf16[2,32,864]{2,1,0:T(8,128)(2,1)S(1)}, u32[]{:S(2)}) copy-start(bf16[2,32,864]{2,1,0:T(8,128)(2,1)S(1)} %collective-permute-done.6.refs_4_) | copy-start | bytes 331780
  38.6 5.6 %collective-permute-start.8 = (bf16[2,32,864]{2,1,0:T(8,128)(2,1)S(1)}, bf16[2,32,864]{2,1,0:T(8,128)(2,1)S(1)}, u32[]{:S(2)}, u32[]{:S(2)}) collective-permute-start(bf16[2,32,864]{2,1,0:T(8,128)(2,1)S(1)} %collective-permute-done.6.refs_4_), channel_id=1, source_target_pairs={{4,0},{5,1},{8,4},{9,5},{12,8},{13,9},{14,12},{15,13},{10,14},{11,... | collective-permute-start | bytes 331784 | tf_op jit(solution)/shard_map/ppermute | solution.py:269
  39.7 3.6 %copy-start.15 = (bf16[2,32,864]{2,1,0:T(8,128)(2,1)}, bf16[2,32,864]{2,1,0:T(8,128)(2,1)S(1)}, u32[]{:S(2)}) copy-start(bf16[2,32,864]{2,1,0:T(8,128)(2,1)S(1)} %collective-permute-done.7.refs_5_) | copy-start | bytes 331780
  39.7 4.8 %collective-permute-start.9 = (bf16[2,32,864]{2,1,0:T(8,128)(2,1)S(1)}, bf16[2,32,864]{2,1,0:T(8,128)(2,1)S(1)}, u32[]{:S(2)}, u32[]{:S(2)}) collective-permute-start(bf16[2,32,864]{2,1,0:T(8,128)(2,1)S(1)} %collective-permute-done.7.refs_5_), channel_id=1, source_target_pairs={{0,4},{1,5},{4,8},{5,9},{8,12},{9,13},{12,14},{13,15},{14,10},{15,... | collective-permute-start | bytes 331784 | tf_op jit(solution)/shard_map/ppermute | solution.py:265
  44.2 0.6 copy-start.16
  44.5 0.6 copy-start.17
  44.5 0.8 copy-start.12
  64.3 2.3 %collective-permute-start.10 = (bf16[8,54,864]{2,0,1:T(8,128)(2,1)S(1)}, bf16[8,54,864]{2,0,1:T(8,128)(2,1)S(1)}, u32[]{:S(2)}, u32[]{:S(2)}) collective-permute-start(bf16[8,54,864]{2,0,1:T(8,128)(2,1)S(1)} %copy.7), channel_id=1, source_target_pairs={{0,1},{1,0},{2,3},{3,2},{4,5},{5,4},{6,7},{7,6},{8,9},{9,8},{10,11... | collective-permute-start | bytes 2239496 | tf_op jit(solution)/shard_map/ppermute | solution.py:333
  68.3 9.7 %collective-permute-start.11 = (bf16[54,864]{1,0:T(8,128)(2,1)S(1)}, bf16[54,864]{1,0:T(8,128)(2,1)S(1)}, u32[]{:S(2)}, u32[]{:S(2)}) collective-permute-start(bf16[54,864]{1,0:T(8,128)(2,1)S(1)} %get-tuple-element.45), channel_id=1, source_target_pairs={{0,2},{1,3},{2,0},{3,1},{4,6},{5,7},{6,4},{7,5},{8,10},{9,11},{10,... | collective-permute-start | bytes 279944 | tf_op jit(solution)/shard_map/ppermute | solution.py:338
  70.3 8.6 %collective-permute-start.17 = (bf16[54,864]{1,0:T(8,128)(2,1)S(1)}, bf16[54,864]{1,0:T(8,128)(2,1)S(1)}, u32[]{:S(2)}, u32[]{:S(2)}) collective-permute-start(bf16[54,864]{1,0:T(8,128)(2,1)S(1)} %get-tuple-element.46), channel_id=1, source_target_pairs={{0,14},{1,15},{2,12},{3,13},{4,10},{5,11},{6,8},{7,9},{8,6},{9,7},... | collective-permute-start | bytes 279944 | tf_op jit(solution)/shard_map/ppermute | solution.py:338
  73.6 13.3 %collective-permute-start.16 = (bf16[54,864]{1,0:T(8,128)(2,1)S(1)}, bf16[54,864]{1,0:T(8,128)(2,1)S(1)}, u32[]{:S(2)}, u32[]{:S(2)}) collective-permute-start(bf16[54,864]{1,0:T(8,128)(2,1)S(1)} %get-tuple-element.47), channel_id=1, source_target_pairs={{0,12},{1,13},{2,14},{3,15},{4,8},{5,9},{6,10},{7,11},{8,4},{9,5},... | collective-permute-start | bytes 279944 | tf_op jit(solution)/shard_map/ppermute | solution.py:338
  73.6 17.1 %collective-permute-start.15 = (bf16[54,864]{1,0:T(8,128)(2,1)S(1)}, bf16[54,864]{1,0:T(8,128)(2,1)S(1)}, u32[]{:S(2)}, u32[]{:S(2)}) collective-permute-start(bf16[54,864]{1,0:T(8,128)(2,1)S(1)} %get-tuple-element.48), channel_id=1, source_target_pairs={{0,10},{1,11},{2,8},{3,9},{4,14},{5,15},{6,12},{7,13},{8,2},{9,3},... | collective-permute-start | bytes 279944 | tf_op jit(solution)/shard_map/ppermute | solution.py:338
  75.6 15.4 %collective-permute-start.14 = (bf16[54,864]{1,0:T(8,128)(2,1)S(1)}, bf16[54,864]{1,0:T(8,128)(2,1)S(1)}, u32[]{:S(2)}, u32[]{:S(2)}) collective-permute-start(bf16[54,864]{1,0:T(8,128)(2,1)S(1)} %get-tuple-element.49), channel_id=1, source_target_pairs={{0,8},{1,9},{2,10},{3,11},{4,12},{5,13},{6,14},{7,15},{8,0},{9,1},... | collective-permute-start | bytes 279944 | tf_op jit(solution)/shard_map/ppermute | solution.py:338
  78.0 13.0 %collective-permute-start.13 = (bf16[54,864]{1,0:T(8,128)(2,1)S(1)}, bf16[54,864]{1,0:T(8,128)(2,1)S(1)}, u32[]{:S(2)}, u32[]{:S(2)}) collective-permute-start(bf16[54,864]{1,0:T(8,128)(2,1)S(1)} %get-tuple-element.50), channel_id=1, source_target_pairs={{0,6},{1,7},{2,4},{3,5},{4,2},{5,3},{6,0},{7,1},{8,14},{9,15},{10,... | collective-permute-start | bytes 279944 | tf_op jit(solution)/shard_map/ppermute | solution.py:338
  78.9 13.1 %collective-permute-start.12 = (bf16[54,864]{1,0:T(8,128)(2,1)S(1)}, bf16[54,864]{1,0:T(8,128)(2,1)S(1)}, u32[]{:S(2)}, u32[]{:S(2)}) collective-permute-start(bf16[54,864]{1,0:T(8,128)(2,1)S(1)} %get-tuple-element.51), channel_id=1, source_target_pairs={{0,4},{1,5},{2,6},{3,7},{4,0},{5,1},{6,2},{7,3},{8,12},{9,13},{10,... | collective-permute-start | bytes 279944 | tf_op jit(solution)/shard_map/ppermute | solution.py:338

commit v2 on v1

v2 whole, which is shorter than its diff:
```python
import functools
import math

import jax
import jax.numpy as jnp
from jax import lax
from jax.experimental import pallas as pl
from jax.experimental.pallas import tpu as pltpu
from jax.sharding import PartitionSpec as P

SIDE = 24
NG = 864
NOCC = 64
NEMP = 256
LANES = 128
PLANES = 3


def round_up(value, step):
    return -(-value // step) * step


def pair_weights(tm, n_occ, n_emp, own_count, times_refs, gaps_ref, cos_ref, out_ref):
    me = lax.axis_index("space")
    tm_index = lax.axis_index("tm")
    core, own_chip = me % 2, me // 2
    shape = out_ref.shape[1:]
    pair = lax.broadcasted_iota(jnp.int32, shape, 0) * LANES + lax.broadcasted_iota(jnp.int32, shape, 1)
    emp_number = lax.rem(pair, n_emp)
    occ_gap = jnp.zeros(shape, jnp.float32)
    emp_gap = jnp.zeros(shape, jnp.float32)
    for i in range(n_occ):
        occ_gap = jnp.where(pair >= i * n_emp, gaps_ref[core * n_occ + i], occ_gap)
    for j in range(n_emp):
        emp_gap = jnp.where(emp_number == j, gaps_ref[NOCC + own_chip * n_emp + j], emp_gap)
    for w in range(own_count):
        weights = jnp.zeros(shape, jnp.float32)
        for hop, times_ref in enumerate(times_refs):
            source = lax.rem(tm_index + hop, tm)
            for k in range(times_ref.shape[0]):
                occ_factor = jnp.exp(-occ_gap * times_ref[k]) * NOCC ** (-0.5)
                emp_factor = jnp.exp(-emp_gap * times_ref[k]) * NEMP ** (-0.5)
                share = cos_ref[tm_index * own_count + w, source * times_ref.shape[0] + k]
                weights = weights + share * (occ_factor * emp_factor)
        out_ref[w] = weights


def table_kernel(held_ref, out_ref, with_cos, with_sin):
    kind = pl.program_id(0) + held_ref[0]
    a_odd, b_odd = kind // 2, kind % 2
    half = SIDE // 2
    a_waves, b_waves, c_waves = SIDE // 4, SIDE // 8, NG // (SIDE // 2 * (SIDE // 4) * 2)
    width = out_ref.shape[2]

    def parts(value, size):
        whole = jnp.floor((value + 0.5) * (1.0 / size))
        return whole, value - size * whole

    column = lax.broadcasted_iota(jnp.int32, (SIDE, width), 1).astype(jnp.float32)
    row = lax.broadcasted_iota(jnp.int32, (SIDE, width), 0).astype(jnp.float32)
    a_step, rest = parts(column, 2 * c_waves * b_waves)
    sine, rest = parts(rest, c_waves * b_waves)
    c_step, b_step = parts(rest, b_waves)
    a = 2.0 * a_step + ((a_odd + a_waves) % 2 - a_waves).astype(jnp.float32)
    b = 2.0 * b_step + ((b_odd + b_waves) % 2 - b_waves).astype(jnp.float32)
    c = c_step + 1.0
    unit = 2.0 * math.pi / SIDE
    size = jnp.where(a_step < a_waves, math.sqrt(2.0 / SIDE**3), 0.0)

    def factors(wave):
        angle = parts(wave * row, SIDE)[1] * unit
        return jnp.cos(angle), jnp.sin(angle)

    cos_p, sin_p = factors(a)
    cos_q, sin_q = factors(b)
    cos_s, sin_s = factors(c)
    is_sine = sine > 0.5
    for y in range(half):
        inner_cos = cos_q[y : y + 1] * cos_s - sin_q[y : y + 1] * sin_s
        inner_sin = sin_q[y : y + 1] * cos_s + cos_q[y : y + 1] * sin_s
        rows = slice(y * SIDE, (y + 1) * SIDE)
        with_cos[rows] = jnp.where(is_sine, inner_sin, inner_cos) * size
        with_sin[rows] = jnp.where(is_sine, inner_cos, -inner_sin) * size
    plane = half * SIDE
    depth = round_up(PLANES * plane, LANES)
    for x in range(half):
        start = x // PLANES * depth + x % PLANES * plane
        table = cos_p[x : x + 1] * with_cos[...] + sin_p[x : x + 1] * with_sin[...]
        out_ref[0, start : start + plane] = table.astype(jnp.bfloat16)
    for step in range(half // PLANES):
        out_ref[0, step * depth + PLANES * plane : (step + 1) * depth] = jnp.zeros(
            (depth - PLANES * plane, width), jnp.bfloat16
        )


def prepare_kernel(tm, n_occ, n_emp, own_count, held_ref, *refs):
    times_refs, (gaps_ref, cos_ref, table_ref, weight_ref, with_cos, with_sin) = refs[:tm], refs[tm:]

    @pl.when(pl.program_id(0) == 0)
    def _():
        pair_weights(tm, n_occ, n_emp, own_count, times_refs, gaps_ref, cos_ref, weight_ref)

    table_kernel(held_ref, table_ref, with_cos, with_sin)


def prepare(held, every_time, gaps, cos_weights, n_occ, n_emp):
    plane = SIDE * SIDE // 2
    depth = SIDE // 2 // PLANES * round_up(PLANES * plane, LANES)
    width = round_up(NG // 4, 2 * LANES)
    tm = len(every_time)
    own_count = cos_weights.shape[0] // tm
    weight_shape = (own_count, n_occ * n_emp // LANES, LANES)
    return pl.pallas_call(
        functools.partial(prepare_kernel, tm, n_occ, n_emp, own_count),
        grid=(4,),
        out_shape=(
            jax.ShapeDtypeStruct((4, depth, width), jnp.bfloat16),
            jax.ShapeDtypeStruct(weight_shape, jnp.float32),
        ),
        in_specs=[pl.BlockSpec(memory_space=pltpu.SMEM)] * (tm + 3),
        out_specs=(
            pl.BlockSpec((1, depth, width), lambda k: (k, 0, 0)),
            pl.BlockSpec(weight_shape, lambda k: (0, 0, 0)),
        ),
        scratch_shapes=[pltpu.VMEM((plane, width), jnp.float32), pltpu.VMEM((plane, width), jnp.float32)],
        compiler_params=pltpu.CompilerParams(vmem_limit_bytes=60 * 1024 * 1024),
        cost_estimate=pl.CostEstimate(
            flops=64 * depth * width, bytes_accessed=8 * depth * width, transcendentals=0
        ),
        name="prepare",
    )(held, *every_time, gaps, cos_weights)


def ring_place(chip, chips):
    return jnp.where(chip % 2 == 0, chip // 2, chips - (chip + 1) // 2)


def ring_chip(place, chips):
    place = lax.rem(place + chips, chips)
    return jnp.where(place < chips // 2, 2 * place, 2 * (chips - place) - 1)


def far_slots(chips):
    return [chips // 2, chips // 2 + 1]


def pair_kernel(offsets, weight_ref, emp_own_ref, emp_other_ref, *refs):
    chips = emp_own_ref.shape[0]
    occ_refs, refs = refs[:chips], refs[chips:]
    table_hbm, keep_far, send_far, keep_near, send_near = refs[:5]
    raw_occ, occ_wide, emp_wide, first, second, rho, blocks, table, table_sem = refs[5:]
    depth = round_up(PLANES * SIDE * SIDE // 2, LANES)
    steps = table.shape[1] // depth
    n_occ, n_rows = raw_occ.shape[1:]
    n_emp = emp_own_ref.shape[1]
    per_group = chips // steps
    plane = SIDE * SIDE // 2
    half_pairs = first.shape[1]
    half_occ = n_occ // 2

    copies = [pltpu.make_async_copy(table_hbm.at[k], table.at[k], table_sem.at[k]) for k in range(4)]
    for copy in copies:
        copy.start()

    me = lax.axis_index("space")
    core, own_chip = me % 2, me // 2
    place = ring_place(own_chip, chips)
    for offset, ref in zip(offsets, occ_refs, strict=True):
        chip = ring_chip(place + offset, chips)
        raw_occ[chip * 2 + core] = ref[0]
        raw_occ[chip * 2 + 1 - core] = ref[1]

    def occ_rows_of(shard):
        return raw_occ[shard].astype(jnp.float32)

    def emp_rows_of(shard):
        own = emp_own_ref[shard // 2].astype(jnp.float32)
        other = emp_other_ref[shard // 2].astype(jnp.float32)
        return jnp.where(core == shard % 2, own, other)

    def halves(rows_of, columns, group, upper):
        pieces = []
        for x in range(PLANES):
            start = (2 * x + upper) * plane
            stop = start + plane
            while start < stop:
                shard, offset = divmod(start, n_rows)
                count = min(stop - start, n_rows - offset)
                pieces.append(rows_of(group * per_group + shard)[:, offset : offset + count])
                start += count
        pieces.append(jnp.zeros((columns, depth - PLANES * plane), jnp.float32))
        return jnp.concatenate(pieces, axis=1)

    for far in range(2):
        for step in range(steps):
            lanes = slice(step * depth, (step + 1) * depth)
            for upper in range(2):
                group = far * steps + step
                occ_wide[2 * far + upper, :, lanes] = halves(occ_rows_of, n_occ, group, upper)
                emp_wide[2 * far + upper, :, lanes] = halves(emp_rows_of, n_emp, group, upper).astype(
                    jnp.bfloat16
                )
    def build(half, target, cut):
        occ_rows = [occ_wide[k, half * half_occ : (half + 1) * half_occ, cut] for k in range(4)]
        emp_rows = [emp_wide[k, :, cut] for k in range(4)]
        for i in range(half_occ):
            near_low, near_high, far_low, far_high = (
                jnp.broadcast_to(occ_rows[k][i : i + 1], (n_emp, LANES)).astype(jnp.bfloat16) * emp_rows[k]
                for k in range(4)
            )
            even_low, odd_low = near_low + far_low, near_low - far_low
            even_high, odd_high = near_high + far_high, near_high - far_high
            rows = slice(i * n_emp, (i + 1) * n_emp)
            target[0, rows, cut] = even_low + even_high
            target[1, rows, cut] = even_low - even_high
            target[2, rows, cut] = odd_low + odd_high
            target[3, rows, cut] = odd_low - odd_high

    modes = rho.shape[1]
    spacing = SIDE
    per_a = modes // spacing

    def multiply(half, source, k):
        found = jnp.dot(source[k], table[k], preferred_element_type=jnp.float32).T
        a_odd, b_odd = divmod(k, 2)
        a_first = (a_odd + SIDE // 4) % 2
        b_first = (b_odd + SIDE // 8) % 2
        for a_step in range(SIDE // 4):
            start = b_first * (SIDE // 2) + 2 * a_step + a_first
            for tile in range(half_pairs // LANES):
                rho[half * half_pairs // LANES + tile, pl.ds(start, per_a, stride=spacing), :] = found[
                    a_step * per_a : (a_step + 1) * per_a, tile * LANES : (tile + 1) * LANES
                ]

    chunks = steps * depth // LANES

    def build_first(chunk, carry):
        build(0, first, pl.ds(pl.multiple_of(chunk * LANES, LANES), LANES))
        return carry

    lax.fori_loop(0, chunks, build_first, 0)
    for k in range(4):
        copies[k].wait()
        for chunk in range(k * chunks // 4, (k + 1) * chunks // 4):
            build(1, second, slice(chunk * LANES, (chunk + 1) * LANES))
        multiply(0, first, k)
    for k in range(4):
        multiply(1, second, k)

    tiles = range(rho.shape[0])
    ordered = jnp.concatenate([rho[tile].astype(jnp.bfloat16) for tile in tiles], axis=1)
    weighted = jnp.concatenate(
        [
            (rho[tile] * weight_ref[tile : tile + 1]).astype(jnp.bfloat16) for tile in tiles
        ],
        axis=1,
    )
    moment = lax.dot_general(
        weighted, ordered, (((1,), (1,)), ((), ())), preferred_element_type=jnp.float32
    )
    rows = blocks.shape[1]
    for k in range(2 * chips):
        blocks[k] = moment[k * rows : (k + 1) * rows]
    far = far_slots(chips)
    near = [slot for slot in range(chips) if slot not in far]
    for slots, keep, send in ((far, keep_far, send_far), (near, keep_near, send_near)):
        for index, slot in enumerate(slots):
            chip = ring_chip(place + slot, chips)
            start = index * round_up(rows, 16)
            keep[start : start + rows, :NG] = blocks[2 * chip + core]
            send[start : start + rows, :NG] = blocks[2 * chip + 1 - core].astype(jnp.bfloat16)


def pair_moment(weights, occ_blocks, offsets, emp_own, emp_other, tables):
    chips, n_emp, n_rows = emp_own.shape
    n_occ = occ_blocks[0].shape[1]
    _, depth, width = tables.shape
    pairs = n_occ * n_emp
    rows = NG // (2 * chips)
    far_rows, near_rows = 2 * round_up(rows, 16), (chips - 2) * round_up(rows, 16)
    vmem = pl.BlockSpec(memory_space=pltpu.VMEM)
    return pl.pallas_call(
        functools.partial(pair_kernel, offsets),
        out_shape=tuple(
            jax.ShapeDtypeStruct((count, round_up(NG, LANES)), dtype)
            for count in (far_rows, near_rows)
            for dtype in (jnp.float32, jnp.bfloat16)
        ),
        in_specs=[vmem] * (3 + chips) + [pl.BlockSpec(memory_space=pl.ANY)],
        out_specs=(vmem, vmem, vmem, vmem),
        scratch_shapes=[
            pltpu.VMEM((2 * chips, n_occ, n_rows), jnp.bfloat16),
            pltpu.VMEM((4, n_occ, depth), jnp.float32),
            pltpu.VMEM((4, n_emp, depth), jnp.bfloat16),
            pltpu.VMEM((4, pairs // 2, depth), jnp.bfloat16),
            pltpu.VMEM((4, pairs // 2, depth), jnp.bfloat16),
            pltpu.VMEM((pairs // LANES, NG, LANES), jnp.float32),
            pltpu.VMEM((2 * chips, rows, NG), jnp.float32),
            pltpu.VMEM((4, depth, width), jnp.bfloat16),
            pltpu.SemaphoreType.DMA((4,)),
        ],
        compiler_params=pltpu.CompilerParams(vmem_limit_bytes=60 * 1024 * 1024),
        cost_estimate=pl.CostEstimate(
            flops=8 * pairs * depth * width, bytes_accessed=16 * 2**20, transcendentals=0
        ),
        name="pair_moment",
    )(weights, emp_own, emp_other, *occ_blocks, tables)


def ring_steps(chips):
    ring = list(range(0, chips, 2)) + list(range(chips - 1, 0, -2))
    ahead = [
        (2 * ring[k] + core, 2 * ring[(k + 1) % chips] + core) for k in range(chips) for core in range(2)
    ]
    return ahead, [(to, start) for start, to in ahead]


def hold(value, until):
    return lax.optimization_barrier((value, until))[0]


def gather_ring(block, chips, work, beside):
    ahead, back = ring_steps(chips)
    found, offsets = [block], [0]
    from_left = from_right = block
    for hop in range(1, chips // 2 + 1):
        if hop == 3:
            from_left, from_right, made, beside = lax.optimization_barrier(
                (from_left, from_right, made, beside)
            )
        elif hop > 1:
            from_left, from_right = lax.optimization_barrier((from_left, from_right))
        from_left = lax.ppermute(from_left, "space", ahead)
        found.append(from_left)
        offsets.append(-hop)
        if 2 * hop < chips:
            from_right = lax.ppermute(from_right, "space", back)
            found.append(from_right)
            offsets.append(hop)
        if hop == 1:
            made = work(from_left)
    return found, offsets, made, beside


def reduce_ring(totals, chips):
    ahead, back = ring_steps(chips)
    farthest = chips // 2
    from_left, from_right = totals[farthest], totals[farthest + 1]
    for hop in range(1, farthest + 1):
        from_left = lax.ppermute(from_left.astype(jnp.bfloat16), "space", ahead).astype(jnp.float32)
        if hop < farthest:
            from_right = lax.ppermute(from_right.astype(jnp.bfloat16), "space", back).astype(jnp.float32)
            from_left = from_left + totals[farthest - hop]
        if hop < farthest - 1:
            from_right = from_right + totals[farthest + 1 + hop]
    return (totals[0] + from_left + from_right)[:, :NG]


def local(space, tm, orbitals, gaps, times, cos_weights):
    rows = orbitals.shape[0]
    chips = space // 2
    columns = orbitals.T
    own_occ, own_emp = NOCC // 2, NEMP // chips
    core = lax.axis_index("space") % 2
    swap = [(d, d ^ 1) for d in range(space)]

    occ = columns[:NOCC].reshape(2, own_occ, rows)
    occ_mine = lax.dynamic_index_in_dim(occ, core, 0, keepdims=False)
    occ_theirs = lax.dynamic_index_in_dim(occ, 1 - core, 0, keepdims=False)
    occ_pair = jnp.stack([occ_mine, lax.ppermute(occ_theirs, "space", swap)])
    emp_own = lax.all_to_all(
        columns[NOCC:].reshape(chips, own_emp, rows),
        "space",
        split_axis=0,
        concat_axis=0,
        axis_index_groups=[[2 * k + c for k in range(chips)] for c in range(2)],
    )
    every_time = [times] + [
        lax.ppermute(times, "tm", [((d + hop) % tm, d) for d in range(tm)]) for hop in range(1, tm)
    ]

    def work(block):
        held = hold(jnp.zeros((1,), jnp.int32), block)
        return prepare(held, every_time, gaps, cos_weights, own_occ, own_emp)

    occ_blocks, offsets, (tables, weights), emp_own = gather_ring(occ_pair, chips, work, emp_own)
    emp_other = lax.ppermute(emp_own, "space", swap)

    results = []
    own_count = cos_weights.shape[0] // tm
    part_rows = NG // space
    for w in range(own_count):
        keep_far, send_far, keep_near, send_near = pair_moment(
            weights[w], occ_blocks, offsets, emp_own, emp_other, tables
        )
        far_total = keep_far + lax.ppermute(send_far, "space", swap).astype(jnp.float32)
        near_total = keep_near + lax.ppermute(send_near, "space", swap).astype(jnp.float32)
        far = far_slots(chips)
        near = [slot for slot in range(chips) if slot not in far]
        totals = {}
        for slots, total in ((far, far_total), (near, near_total)):
            for index, slot in enumerate(slots):
                start = index * round_up(part_rows, 16)
                totals[slot] = total[start : start + part_rows]
        results.append(reduce_ring(totals, chips))
    return jnp.stack(results)


def solution(mesh):
    return jax.shard_map(
        functools.partial(local, mesh.shape["space"], mesh.shape["tm"]),
        mesh=mesh,
        in_specs=(P("space", None), P(), P("tm"), P()),
        out_specs=P("tm", "space", None),
        check_vma=False,
    )
```

time: 93.4 us -> 94.3 us (level)
  waiting for transfers between devices: 10.8 us -> 32.2 us
  other arithmetic: 18.7 us -> 2.73 us
  Pallas kernels: 17.7 us -> 27.9 us
  starting transfers between devices: 35.7 us -> 25.7 us
  local copies, waits for them, and re-layouts: 9.06 us -> 4.47 us
    ppermute x8 -> x9, starting transfers between devices: 18.6 us -> 7.18 us  [the longest x3 5.4 us: reduce_ring(): lax.ppermute(from_right.astype(jnp.bfloat16), 'space', back)]
    pallas_call x1 -> x2, Pallas kernels: 17.7 us -> 27.9 us  [the longest x1 21.7 us: pair_moment(): pl.pallas_call(functools.partial(pair_kernel, offsets), out_shape=tuple((...]
    convert_element_type x5 -> x3, other arithmetic: 9.63 us -> 0.12 us  [reduce_ring(): from_left.astype(jnp.bfloat16)]
    ppermute x3, waiting for transfers between devices: 0.83 us -> 8.45 us  [gather_ring(): from_right = lax.ppermute(from_right, 'space', back)]
    ppermute x8 -> x9, waiting for transfers between devices: 7.35 us -> 13 us  [the longest x4 11.1 us: reduce_ring(): lax.ppermute(from_left.astype(jnp.bfloat16), 'space', ahead)]
    ppermute x4, waiting for transfers between devices: 2.62 us -> 7.93 us  [gather_ring(): from_left = lax.ppermute(from_left, 'space', ahead)]
    mul x4 -> x0, other arithmetic: 1.64 us -> none  [the longest x1 1.29 us: table_factors(): with_cos = jnp.where(is_sine, inner_sin, inner_cos) * size]
    ppermute x1, waiting for transfers between devices: 0.01 us -> 1.6 us  [local(): lax.ppermute(times, 'tm', [((d + hop) % tm, d) for d in range(tm)])]
  transfers between devices with their start and end apart: 19 -> 20, of which waited for: 8 -> 13; matrix products, arithmetic and copies ran while one was open for 25% -> 4% of each run, Pallas kernels for 0% -> 7%
where the time goes in v2:
time: 94.3 us; the launch traced here: 93.9 us
  waiting for transfers between devices  32.2 us (34%)
  Pallas kernels  27.9 us (30%)
  starting transfers between devices  25.7 us (27%)
  local copies, waits for them, and re-layouts  4.47 us (5%)
  other arithmetic  2.73 us (3%)
    pallas_call x1, Pallas kernels, pair_moment(): pl.pallas_call(functools.partial(pair_kernel, offsets), out_shape=tuple((...  21.7 us
    ppermute x4, waiting for transfers between devices, reduce_ring(): lax.ppermute(from_left.astype(jnp.bfloat16), 'space', ahead)  11.1 us
    ppermute x3, waiting for transfers between devices, gather_ring(): from_right = lax.ppermute(from_right, 'space', back)  8.45 us
    ppermute x4, waiting for transfers between devices, gather_ring(): from_left = lax.ppermute(from_left, 'space', ahead)  7.93 us
    ppermute x4, starting transfers between devices, gather_ring(): from_left = lax.ppermute(from_left, 'space', ahead)  7.48 us
    all_to_all x1, starting transfers between devices, local(): lax.all_to_all(columns[NOCC:].reshape(chips, own_emp, rows), 'space', spl...  7.28 us
    pallas_call x1, Pallas kernels, prepare(): pl.pallas_call(functools.partial(prepare_kernel, tm, n_occ, n_emp, own_co...  6.21 us
    ppermute x3, starting transfers between devices, reduce_ring(): lax.ppermute(from_right.astype(jnp.bfloat16), 'space', back)  5.4 us
  transfers between devices with their start and end apart: 20, of which 13 were waited for; matrix products, arithmetic and copies ran while one was open for 4% of the time, Pallas kernels for 7%

profile of v2, /device:TPU:0, one launch (start us, length us, event | category | flops | bytes accessed | tf_op | source)
XLA Modules:
  0.0 93.9 jit_solution(8815597353129559140)
XLA Ops:
  0.0 1.9 %slice.47 = bf16[256,864]{1,0:T(8,128)(2,1)} slice(bf16[320,864]{1,0:T(8,128)(2,1)} %bitcast.9), slice={[64:320], [0:864]} | slice | bytes 884736 | tf_op jit(solution)/shard_map/slice | solution.py:372
  1.9 7.3 %all-to-all-start = ((bf16[8,32,864]{2,1,0:T(8,128)(2,1)}), bf16[8,32,864]{2,1,0:T(8,128)(2,1)S(1)}, u32[]{:S(2)}, u32[]{:S(2)}) async-start(bf16[8,32,864]{2,1,0:T(8,128)(2,1)} %bitcast.4), calls=%async_computation | async-start | bytes 917504 | tf_op jit(solution)/shard_map/all_to_all | solution.py:371
  9.1 0.9 slice.46
  10.1 0.1 collective-permute-start
  10.2 1.2 %collective-permute-done = bf16[32,864]{1,0:T(8,128)(2,1)S(1)} collective-permute-done((bf16[32,864]{1,0:T(8,128)(2,1)S(1)}, bf16[32,864]{1,0:T(8,128)(2,1)S(1)}, u32[]{:S(2)}, u32[]{:S(2)}) %collective-permute-start) | collective-permute-done | bytes 55328 | tf_op jit(solution)/shard_map/ppermute | solution.py:370
  11.4 0.0 copy-start.1
  11.4 2.1 %collective-permute-start.2 = (bf16[2,32,864]{2,1,0:T(8,128)(2,1)S(1)}, bf16[2,32,864]{2,1,0:T(8,128)(2,1)S(1)}, u32[]{:S(2)}, u32[]{:S(2)}) collective-permute-start(bf16[2,32,864]{2,1,0:T(8,128)(2,1)S(1)} %pad_maximum_fusion.refs_0_), channel_id=1, source_target_pairs={{4,0},{5,1},{8,4},{9,5},{12,8},{13,9},{14,12},{15,13},{10,14},{11,... | collective-permute-start | bytes 331784 | tf_op jit(solution)/shard_map/ppermute | solution.py:337
  13.5 0.1 collective-permute-start.1
  13.6 6.7 %collective-permute-done.2.refs_2_ = bf16[2,32,864]{2,1,0:T(8,128)(2,1)S(1)} collective-permute-done((bf16[2,32,864]{2,1,0:T(8,128)(2,1)S(1)}, bf16[2,32,864]{2,1,0:T(8,128)(2,1)S(1)}, u32[]{:S(2)}, u32[]{:S(2)}) %collective-permute-start.2) | collective-permute-done | bytes 110624 | tf_op jit(solution)/shard_map/ppermute | solution.py:337
  20.3 0.0 copy-start.3
  20.3 0.0 collective-permute-done.1.refs_1_
  20.3 0.0 copy-start.4
  20.3 5.0 %collective-permute-start.3 = (bf16[2,32,864]{2,1,0:T(8,128)(2,1)S(1)}, bf16[2,32,864]{2,1,0:T(8,128)(2,1)S(1)}, u32[]{:S(2)}, u32[]{:S(2)}) collective-permute-start(bf16[2,32,864]{2,1,0:T(8,128)(2,1)S(1)} %collective-permute-done.1.refs_1_), channel_id=1, source_target_pairs={{0,4},{1,5},{4,8},{5,9},{8,12},{9,13},{12,14},{13,15},{14,10},{15,... | collective-permute-start | bytes 331784 | tf_op jit(solution)/shard_map/ppermute | solution.py:333
  25.3 0.0 collective-permute-start.4
  25.3 1.5 %collective-permute-start.5 = (f32[1]{0:T(128)}, f32[1]{0:T(128)}, u32[]{:S(2)}, u32[]{:S(2)}) collective-permute-start(f32[1]{0:T(128)} %param.6), channel_id=1, source_target_pairs={{16,0},{0,16},{17,1},{1,17},{18,2},{2,18},{19,3},{3,19},{20,4},{4,... | collective-permute-start | bytes 20 | tf_op jit(solution)/shard_map/ppermute | solution.py:379
  27.5 1.6 %collective-permute-done.5.refs_1_ = f32[1]{0:T(128)} collective-permute-done((f32[1]{0:T(128)}, f32[1]{0:T(128)}, u32[]{:S(2)}, u32[]{:S(2)}) %collective-permute-start.5) | collective-permute-done | bytes 36 | tf_op jit(solution)/shard_map/ppermute | solution.py:379
  29.1 6.2 %prepare.1 = (bf16[4,3584,256]{2,1,0:T(8,128)(2,1)}, f32[1,8,128]{2,1,0:T(8,128)}) custom-call(s32[1]{0:T(128)} %constant.27.clone.1.held_ref, f32[1]{0:T(128)S(6)} %copy.6.refs_0_, f32[1]{0:T(128)} %collective-permute-done.5.refs_1_, f32[320]{0:T(512)} %refs_2_.1, f32[2,2]{1,0:T(2,128)} %refs_3_.1), custom_call_target="tpu_custom_call" | custom-call | flops 58720256 | bytes 7340032 | tf_op jit(solution)/shard_map/prepare/pallas_call | solution.py:113
  35.3 0.0 collective-permute-done.3.refs_3_
  35.3 0.0 copy-start.5
  35.3 0.0 collective-permute-done.4.refs_4_
  35.3 0.0 copy-start.6
  35.3 0.0 all-to-all-done.emp_own_ref
  35.3 0.0 copy-start
  35.3 0.1 collective-permute-start.6
  35.4 2.1 %collective-permute-start.7 = (bf16[2,32,864]{2,1,0:T(8,128)(2,1)S(1)}, bf16[2,32,864]{2,1,0:T(8,128)(2,1)S(1)}, u32[]{:S(2)}, u32[]{:S(2)}) collective-permute-start(bf16[2,32,864]{2,1,0:T(8,128)(2,1)S(1)} %collective-permute-done.3.refs_3_), channel_id=1, source_target_pairs={{0,4},{1,5},{4,8},{5,9},{8,12},{9,13},{12,14},{13,15},{14,10},{15,... | collective-permute-start | bytes 331784 | tf_op jit(solution)/shard_map/ppermute | solution.py:333
  37.5 0.0 collective-permute-start.8
  37.5 3.5 %collective-permute-done.7.refs_5_ = bf16[2,32,864]{2,1,0:T(8,128)(2,1)S(1)} collective-permute-done((bf16[2,32,864]{2,1,0:T(8,128)(2,1)S(1)}, bf16[2,32,864]{2,1,0:T(8,128)(2,1)S(1)}, u32[]{:S(2)}, u32[]{:S(2)}) %collective-permute-start.7) | collective-permute-done | bytes 110624 | tf_op jit(solution)/shard_map/ppermute | solution.py:333
  41.0 1.7 %collective-permute-done.8.refs_6_ = bf16[2,32,864]{2,1,0:T(8,128)(2,1)S(1)} collective-permute-done((bf16[2,32,864]{2,1,0:T(8,128)(2,1)S(1)}, bf16[2,32,864]{2,1,0:T(8,128)(2,1)S(1)}, u32[]{:S(2)}, u32[]{:S(2)}) %collective-permute-start.8) | collective-permute-done | bytes 110624 | tf_op jit(solution)/shard_map/ppermute | solution.py:337
  42.7 0.3 collective-permute-start.9
  43.0 4.5 %collective-permute-done.9.refs_7_ = bf16[2,32,864]{2,1,0:T(8,128)(2,1)S(1)} collective-permute-done((bf16[2,32,864]{2,1,0:T(8,128)(2,1)S(1)}, bf16[2,32,864]{2,1,0:T(8,128)(2,1)S(1)}, u32[]{:S(2)}, u32[]{:S(2)}) %collective-permute-start.9) | collective-permute-done | bytes 110624 | tf_op jit(solution)/shard_map/ppermute | solution.py:333
  47.5 0.0 collective-permute-done.6.emp_other_ref
  47.5 0.0 copy-done.1
  47.5 0.0 copy-done.3
  47.5 0.0 copy-done.4
  47.5 0.0 copy-done.5
  47.5 0.0 copy-done.6
  47.5 0.0 copy-done
  47.6 0.0 copy-done.7
  47.6 0.0 copy-done.8
  47.6 0.6 copy-done.9
  48.1 0.2 copy-done.2
  48.3 21.7 %pair_moment.1 = (f32[128,896]{1,0:T(8,128)}, bf16[128,896]{1,0:T(8,128)(2,1)}, f32[384,896]{1,0:T(8,128)}, bf16[384,896]{1,0:T(8,128)(2,1)}) custom-call(f32[8,128]{1,0:T(8,128)} %bitcast.13, bf16[8,32,864]{2,1,0:T(8,128)(2,1)} %copy-done, bf16[8,32,864]{2,1,0:T(8,128)(2,1)} %copy-done.2, bf16[2,32,864]{2,1,0:T(8,128)(2,1)} %copy-done.1, ...), custom_call_target="tpu_custom_call" | custom-call | flops 7516192768 | bytes 16777216 | tf_op jit(solution)/shard_map/pair_moment/pallas_call | solution.py:282
  70.1 0.1 collective-permute-start.11
  70.2 0.5 collective-permute-start.10
  70.7 1.2 %collective-permute-done.11 = bf16[128,896]{1,0:T(8,128)(2,1)S(1)} collective-permute-done((bf16[128,896]{1,0:T(8,128)(2,1)}, bf16[128,896]{1,0:T(8,128)(2,1)S(1)}, u32[]{:S(2)}, u32[]{:S(2)}) %collective-permute-start.11) | collective-permute-done | bytes 229408 | tf_op jit(solution)/shard_map/ppermute | solution.py:396
  71.9 1.1 %add_convert_fusion = bf16[128,896]{1,0:T(8,128)(2,1)S(1)} fusion(f32[128,896]{1,0:T(8,128)} %get-tuple-element.33, bf16[128,896]{1,0:T(8,128)(2,1)S(1)} %collective-permute-done.11), kind=kLoop, calls=%fused_computation.1 | loop fusion | flops 344064 | bytes 917504 | tf_op jit(solution)/shard_map/convert.1
  73.0 0.4 collective-permute-start.12
  73.3 1.7 %collective-permute-start.16 = (bf16[54,896]{1,0:T(8,128)(2,1)S(1)}, bf16[54,896]{1,0:T(8,128)(2,1)S(1)}, u32[]{:S(2)}, u32[]{:S(2)}) collective-permute-start(bf16[54,896]{1,0:T(8,128)(2,1)S(1)} %get-tuple-element.41), channel_id=1, source_target_pairs={{4,0},{5,1},{8,4},{9,5},{12,8},{13,9},{14,12},{15,13},{10,14},{11,... | collective-permute-start | bytes 290312 | tf_op jit(solution)/shard_map/ppermute | solution.py:352
  75.0 0.0 collective-permute-done.10
  75.0 1.5 %convert_add_fusion = f32[384,896]{1,0:T(8,128)S(1)} fusion(f32[384,896]{1,0:T(8,128)} %get-tuple-element.31, bf16[384,896]{1,0:T(8,128)(2,1)S(1)} %collective-permute-done.10), kind=kLoop, calls=%fused_computation | loop fusion | flops 688128 | bytes 3440640 | tf_op jit(solution)/shard_map/add | solution.py:397
  76.5 1.4 %collective-permute-done.12 = bf16[54,896]{1,0:T(8,128)(2,1)S(1)} collective-permute-done((bf16[54,896]{1,0:T(8,128)(2,1)S(1)}, bf16[54,896]{1,0:T(8,128)(2,1)S(1)}, u32[]{:S(2)}, u32[]{:S(2)}) %collective-permute-start.12) | collective-permute-done | bytes 96800 | tf_op jit(solution)/shard_map/ppermute | solution.py:350
  77.9 0.4 collective-permute-start.13
  78.3 0.0 collective-permute-done.16
  78.3 4.3 %collective-permute-done.13 = bf16[54,896]{1,0:T(8,128)(2,1)S(1)} collective-permute-done((bf16[54,896]{1,0:T(8,128)(2,1)S(1)}, bf16[54,896]{1,0:T(8,128)(2,1)S(1)}, u32[]{:S(2)}, u32[]{:S(2)}) %collective-permute-start.13) | collective-permute-done | bytes 96800 | tf_op jit(solution)/shard_map/ppermute | solution.py:350
  82.6 0.4 collective-permute-start.14
  83.0 1.7 %collective-permute-start.17 = (bf16[54,896]{1,0:T(8,128)(2,1)S(1)}, bf16[54,896]{1,0:T(8,128)(2,1)S(1)}, u32[]{:S(2)}, u32[]{:S(2)}) collective-permute-start(bf16[54,896]{1,0:T(8,128)(2,1)S(1)} %get-tuple-element.39), channel_id=1, source_target_pairs={{4,0},{5,1},{8,4},{9,5},{12,8},{13,9},{14,12},{15,13},{10,14},{11,... | collective-permute-start | bytes 290312 | tf_op jit(solution)/shard_map/ppermute | solution.py:352
  84.7 2.9 %collective-permute-done.14 = bf16[54,896]{1,0:T(8,128)(2,1)S(1)} collective-permute-done((bf16[54,896]{1,0:T(8,128)(2,1)S(1)}, bf16[54,896]{1,0:T(8,128)(2,1)S(1)}, u32[]{:S(2)}, u32[]{:S(2)}) %collective-permute-start.14) | collective-permute-done | bytes 96800 | tf_op jit(solution)/shard_map/ppermute | solution.py:350
  87.6 0.6 collective-permute-done.17
  88.2 0.1 fusion.4
  88.3 0.1 collective-permute-start.15
  88.3 2.0 %collective-permute-start.18 = (bf16[54,896]{1,0:T(8,128)(2,1)S(1)}, bf16[54,896]{1,0:T(8,128)(2,1)S(1)}, u32[]{:S(2)}, u32[]{:S(2)}) collective-permute-start(bf16[54,896]{1,0:T(8,128)(2,1)S(1)} %get-tuple-element.36), channel_id=1, source_target_pairs={{4,0},{5,1},{8,4},{9,5},{12,8},{13,9},{14,12},{15,13},{10,14},{11,... | collective-permute-start | bytes 290312 | tf_op jit(solution)/shard_map/ppermute | solution.py:352
  90.3 2.6 %collective-permute-done.15 = bf16[54,896]{1,0:T(8,128)(2,1)S(1)} collective-permute-done((bf16[54,896]{1,0:T(8,128)(2,1)S(1)}, bf16[54,896]{1,0:T(8,128)(2,1)S(1)}, u32[]{:S(2)}, u32[]{:S(2)}) %collective-permute-start.15) | collective-permute-done | bytes 96800 | tf_op jit(solution)/shard_map/ppermute | solution.py:350
  93.0 0.1 collective-permute-done.18
  93.1 0.9 copy.5
  (10 shorter events, 0.2 us)
Async XLA Ops:
  1.9 33.5 %all-to-all-start = ((bf16[8,32,864]{2,1,0:T(8,128)(2,1)}), bf16[8,32,864]{2,1,0:T(8,128)(2,1)S(1)}, u32[]{:S(2)}, u32[]{:S(2)}) async-start(bf16[8,32,864]{2,1,0:T(8,128)(2,1)} %bitcast.4), calls=%async_computation | async-start | bytes 917504 | tf_op jit(solution)/shard_map/all_to_all | solution.py:371
  10.1 1.3 %collective-permute-start = (bf16[32,864]{1,0:T(8,128)(2,1)S(1)}, bf16[32,864]{1,0:T(8,128)(2,1)S(1)}, u32[]{:S(2)}, u32[]{:S(2)}) collective-permute-start(bf16[32,864]{1,0:T(8,128)(2,1)S(1)} %get-tuple-element.43), channel_id=1, source_target_pairs={{0,1},{1,0},{2,3},{3,2},{4,5},{5,4},{6,7},{7,6},{8,9},{9,8},{10,11... | collective-permute-start | bytes 165896 | tf_op jit(solution)/shard_map/ppermute | solution.py:370
  11.4 36.1 %copy-start.1 = (bf16[2,32,864]{2,1,0:T(8,128)(2,1)}, bf16[2,32,864]{2,1,0:T(8,128)(2,1)S(1)}, u32[]{:S(2)}) copy-start(bf16[2,32,864]{2,1,0:T(8,128)(2,1)S(1)} %pad_maximum_fusion.refs_0_) | copy-start | bytes 331780
  11.4 8.8 %collective-permute-start.2 = (bf16[2,32,864]{2,1,0:T(8,128)(2,1)S(1)}, bf16[2,32,864]{2,1,0:T(8,128)(2,1)S(1)}, u32[]{:S(2)}, u32[]{:S(2)}) collective-permute-start(bf16[2,32,864]{2,1,0:T(8,128)(2,1)S(1)} %pad_maximum_fusion.refs_0_), channel_id=1, source_target_pairs={{4,0},{5,1},{8,4},{9,5},{12,8},{13,9},{14,12},{15,13},{10,14},{11,... | collective-permute-start | bytes 331784 | tf_op jit(solution)/shard_map/ppermute | solution.py:337
  13.5 6.8 %collective-permute-start.1 = (bf16[2,32,864]{2,1,0:T(8,128)(2,1)S(1)}, bf16[2,32,864]{2,1,0:T(8,128)(2,1)S(1)}, u32[]{:S(2)}, u32[]{:S(2)}) collective-permute-start(bf16[2,32,864]{2,1,0:T(8,128)(2,1)S(1)} %pad_maximum_fusion.refs_0_), channel_id=1, source_target_pairs={{0,4},{1,5},{4,8},{5,9},{8,12},{9,13},{12,14},{13,15},{14,10},{15,... | collective-permute-start | bytes 331784 | tf_op jit(solution)/shard_map/ppermute | solution.py:333
  20.3 27.2 %copy-start.3 = (bf16[2,32,864]{2,1,0:T(8,128)(2,1)}, bf16[2,32,864]{2,1,0:T(8,128)(2,1)S(1)}, u32[]{:S(2)}) copy-start(bf16[2,32,864]{2,1,0:T(8,128)(2,1)S(1)} %collective-permute-done.2.refs_2_) | copy-start | bytes 331780
  20.3 27.2 %copy-start.4 = (bf16[2,32,864]{2,1,0:T(8,128)(2,1)}, bf16[2,32,864]{2,1,0:T(8,128)(2,1)S(1)}, u32[]{:S(2)}) copy-start(bf16[2,32,864]{2,1,0:T(8,128)(2,1)S(1)} %collective-permute-done.1.refs_1_) | copy-start | bytes 331780
  20.3 15.0 %collective-permute-start.3 = (bf16[2,32,864]{2,1,0:T(8,128)(2,1)S(1)}, bf16[2,32,864]{2,1,0:T(8,128)(2,1)S(1)}, u32[]{:S(2)}, u32[]{:S(2)}) collective-permute-start(bf16[2,32,864]{2,1,0:T(8,128)(2,1)S(1)} %collective-permute-done.1.refs_1_), channel_id=1, source_target_pairs={{0,4},{1,5},{4,8},{5,9},{8,12},{9,13},{12,14},{13,15},{14,10},{15,... | collective-permute-start | bytes 331784 | tf_op jit(solution)/shard_map/ppermute | solution.py:333
  25.3 10.0 %collective-permute-start.4 = (bf16[2,32,864]{2,1,0:T(8,128)(2,1)S(1)}, bf16[2,32,864]{2,1,0:T(8,128)(2,1)S(1)}, u32[]{:S(2)}, u32[]{:S(2)}) collective-permute-start(bf16[2,32,864]{2,1,0:T(8,128)(2,1)S(1)} %collective-permute-done.2.refs_2_), channel_id=1, source_target_pairs={{4,0},{5,1},{8,4},{9,5},{12,8},{13,9},{14,12},{15,13},{10,14},{11,... | collective-permute-start | bytes 331784 | tf_op jit(solution)/shard_map/ppermute | solution.py:337
  25.3 3.8 %collective-permute-start.5 = (f32[1]{0:T(128)}, f32[1]{0:T(128)}, u32[]{:S(2)}, u32[]{:S(2)}) collective-permute-start(f32[1]{0:T(128)} %param.6), channel_id=1, source_target_pairs={{16,0},{0,16},{17,1},{1,17},{18,2},{2,18},{19,3},{3,19},{20,4},{4,... | collective-permute-start | bytes 20 | tf_op jit(solution)/shard_map/ppermute | solution.py:379
  35.3 12.2 %copy-start.5 = (bf16[2,32,864]{2,1,0:T(8,128)(2,1)}, bf16[2,32,864]{2,1,0:T(8,128)(2,1)S(1)}, u32[]{:S(2)}) copy-start(bf16[2,32,864]{2,1,0:T(8,128)(2,1)S(1)} %collective-permute-done.3.refs_3_) | copy-start | bytes 331780
  35.3 12.2 %copy-start.6 = (bf16[2,32,864]{2,1,0:T(8,128)(2,1)}, bf16[2,32,864]{2,1,0:T(8,128)(2,1)S(1)}, u32[]{:S(2)}) copy-start(bf16[2,32,864]{2,1,0:T(8,128)(2,1)S(1)} %collective-permute-done.4.refs_4_) | copy-start | bytes 331780
  35.3 12.2 %copy-start = (bf16[8,32,864]{2,1,0:T(8,128)(2,1)}, bf16[8,32,864]{2,1,0:T(8,128)(2,1)S(1)}, u32[]{:S(2)}) copy-start(bf16[8,32,864]{2,1,0:T(8,128)(2,1)S(1)} %all-to-all-done.emp_own_ref) | copy-start | bytes 1327108
  35.3 12.2 %collective-permute-start.6 = (bf16[8,32,864]{2,1,0:T(8,128)(2,1)S(1)}, bf16[8,32,864]{2,1,0:T(8,128)(2,1)S(1)}, u32[]{:S(2)}, u32[]{:S(2)}) collective-permute-start(bf16[8,32,864]{2,1,0:T(8,128)(2,1)S(1)} %all-to-all-done.emp_own_ref), channel_id=1, source_target_pairs={{0,1},{1,0},{2,3},{3,2},{4,5},{5,4},{6,7},{7,6},{8,9},{9,8},{10,11... | collective-permute-start | bytes 1327112 | tf_op jit(solution)/shard_map/ppermute | solution.py:387
  35.4 5.5 %collective-permute-start.7 = (bf16[2,32,864]{2,1,0:T(8,128)(2,1)S(1)}, bf16[2,32,864]{2,1,0:T(8,128)(2,1)S(1)}, u32[]{:S(2)}, u32[]{:S(2)}) collective-permute-start(bf16[2,32,864]{2,1,0:T(8,128)(2,1)S(1)} %collective-permute-done.3.refs_3_), channel_id=1, source_target_pairs={{0,4},{1,5},{4,8},{5,9},{8,12},{9,13},{12,14},{13,15},{14,10},{15,... | collective-permute-start | bytes 331784 | tf_op jit(solution)/shard_map/ppermute | solution.py:333
  37.5 5.2 %collective-permute-start.8 = (bf16[2,32,864]{2,1,0:T(8,128)(2,1)S(1)}, bf16[2,32,864]{2,1,0:T(8,128)(2,1)S(1)}, u32[]{:S(2)}, u32[]{:S(2)}) collective-permute-start(bf16[2,32,864]{2,1,0:T(8,128)(2,1)S(1)} %collective-permute-done.4.refs_4_), channel_id=1, source_target_pairs={{4,0},{5,1},{8,4},{9,5},{12,8},{13,9},{14,12},{15,13},{10,14},{11,... | collective-permute-start | bytes 331784 | tf_op jit(solution)/shard_map/ppermute | solution.py:337
  41.0 6.6 %copy-start.7 = (bf16[2,32,864]{2,1,0:T(8,128)(2,1)}, bf16[2,32,864]{2,1,0:T(8,128)(2,1)S(1)}, u32[]{:S(2)}) copy-start(bf16[2,32,864]{2,1,0:T(8,128)(2,1)S(1)} %collective-permute-done.7.refs_5_) | copy-start | bytes 331780
  42.7 4.9 %copy-start.8 = (bf16[2,32,864]{2,1,0:T(8,128)(2,1)}, bf16[2,32,864]{2,1,0:T(8,128)(2,1)S(1)}, u32[]{:S(2)}) copy-start(bf16[2,32,864]{2,1,0:T(8,128)(2,1)S(1)} %collective-permute-done.8.refs_6_) | copy-start | bytes 331780
  42.7 4.8 %collective-permute-start.9 = (bf16[2,32,864]{2,1,0:T(8,128)(2,1)S(1)}, bf16[2,32,864]{2,1,0:T(8,128)(2,1)S(1)}, u32[]{:S(2)}, u32[]{:S(2)}) collective-permute-start(bf16[2,32,864]{2,1,0:T(8,128)(2,1)S(1)} %collective-permute-done.7.refs_5_), channel_id=1, source_target_pairs={{0,4},{1,5},{4,8},{5,9},{8,12},{9,13},{12,14},{13,15},{14,10},{15,... | collective-permute-start | bytes 331784 | tf_op jit(solution)/shard_map/ppermute | solution.py:333
  47.5 0.7 copy-start.9
  47.5 0.8 copy-start.2
  70.1 1.8 %collective-permute-start.11 = (bf16[128,896]{1,0:T(8,128)(2,1)}, bf16[128,896]{1,0:T(8,128)(2,1)S(1)}, u32[]{:S(2)}, u32[]{:S(2)}) collective-permute-start(bf16[128,896]{1,0:T(8,128)(2,1)} %get-tuple-element.34), channel_id=1, source_target_pairs={{0,1},{1,0},{2,3},{3,2},{4,5},{5,4},{6,7},{7,6},{8,9},{9,8},{10,11... | collective-permute-start | bytes 688136 | tf_op jit(solution)/shard_map/ppermute | solution.py:396
  70.2 4.9 %collective-permute-start.10 = (bf16[384,896]{1,0:T(8,128)(2,1)}, bf16[384,896]{1,0:T(8,128)(2,1)S(1)}, u32[]{:S(2)}, u32[]{:S(2)}) collective-permute-start(bf16[384,896]{1,0:T(8,128)(2,1)} %get-tuple-element.32), channel_id=1, source_target_pairs={{0,1},{1,0},{2,3},{3,2},{4,5},{5,4},{6,7},{7,6},{8,9},{9,8},{10,11... | collective-permute-start | bytes 2064392 | tf_op jit(solution)/shard_map/ppermute | solution.py:397
  73.0 4.9 %collective-permute-start.12 = (bf16[54,896]{1,0:T(8,128)(2,1)S(1)}, bf16[54,896]{1,0:T(8,128)(2,1)S(1)}, u32[]{:S(2)}, u32[]{:S(2)}) collective-permute-start(bf16[54,896]{1,0:T(8,128)(2,1)S(1)} %get-tuple-element.40), channel_id=1, source_target_pairs={{0,4},{1,5},{4,8},{5,9},{8,12},{9,13},{12,14},{13,15},{14,10},{15,... | collective-permute-start | bytes 290312 | tf_op jit(solution)/shard_map/ppermute | solution.py:350
  73.3 5.0 %collective-permute-start.16 = (bf16[54,896]{1,0:T(8,128)(2,1)S(1)}, bf16[54,896]{1,0:T(8,128)(2,1)S(1)}, u32[]{:S(2)}, u32[]{:S(2)}) collective-permute-start(bf16[54,896]{1,0:T(8,128)(2,1)S(1)} %get-tuple-element.41), channel_id=1, source_target_pairs={{4,0},{5,1},{8,4},{9,5},{12,8},{13,9},{14,12},{15,13},{10,14},{11,... | collective-permute-start | bytes 290312 | tf_op jit(solution)/shard_map/ppermute | solution.py:352
  77.9 4.7 %collective-permute-start.13 = (bf16[54,896]{1,0:T(8,128)(2,1)S(1)}, bf16[54,896]{1,0:T(8,128)(2,1)S(1)}, u32[]{:S(2)}, u32[]{:S(2)}) collective-permute-start(bf16[54,896]{1,0:T(8,128)(2,1)S(1)} %fusion.6), channel_id=1, source_target_pairs={{0,4},{1,5},{4,8},{5,9},{8,12},{9,13},{12,14},{13,15},{14,10},{15,... | collective-permute-start | bytes 290312 | tf_op jit(solution)/shard_map/ppermute | solution.py:350
  82.6 4.9 %collective-permute-start.14 = (bf16[54,896]{1,0:T(8,128)(2,1)S(1)}, bf16[54,896]{1,0:T(8,128)(2,1)S(1)}, u32[]{:S(2)}, u32[]{:S(2)}) collective-permute-start(bf16[54,896]{1,0:T(8,128)(2,1)S(1)} %get-tuple-element.38), channel_id=1, source_target_pairs={{0,4},{1,5},{4,8},{5,9},{8,12},{9,13},{12,14},{13,15},{14,10},{15,... | collective-permute-start | bytes 290312 | tf_op jit(solution)/shard_map/ppermute | solution.py:350
  83.0 5.2 %collective-permute-start.17 = (bf16[54,896]{1,0:T(8,128)(2,1)S(1)}, bf16[54,896]{1,0:T(8,128)(2,1)S(1)}, u32[]{:S(2)}, u32[]{:S(2)}) collective-permute-start(bf16[54,896]{1,0:T(8,128)(2,1)S(1)} %get-tuple-element.39), channel_id=1, source_target_pairs={{4,0},{5,1},{8,4},{9,5},{12,8},{13,9},{14,12},{15,13},{10,14},{11,... | collective-permute-start | bytes 290312 | tf_op jit(solution)/shard_map/ppermute | solution.py:352
  88.3 4.7 %collective-permute-start.15 = (bf16[54,896]{1,0:T(8,128)(2,1)S(1)}, bf16[54,896]{1,0:T(8,128)(2,1)S(1)}, u32[]{:S(2)}, u32[]{:S(2)}) collective-permute-start(bf16[54,896]{1,0:T(8,128)(2,1)S(1)} %get-tuple-element.35), channel_id=1, source_target_pairs={{0,4},{1,5},{4,8},{5,9},{8,12},{9,13},{12,14},{13,15},{14,10},{15,... | collective-permute-start | bytes 290312 | tf_op jit(solution)/shard_map/ppermute | solution.py:350
  88.3 4.7 %collective-permute-start.18 = (bf16[54,896]{1,0:T(8,128)(2,1)S(1)}, bf16[54,896]{1,0:T(8,128)(2,1)S(1)}, u32[]{:S(2)}, u32[]{:S(2)}) collective-permute-start(bf16[54,896]{1,0:T(8,128)(2,1)S(1)} %get-tuple-element.36), channel_id=1, source_target_pairs={{4,0},{5,1},{8,4},{9,5},{12,8},{13,9},{14,12},{15,13},{10,14},{11,... | collective-permute-start | bytes 290312 | tf_op jit(solution)/shard_map/ppermute | solution.py:352

commit v3 on v2

v3 whole, which is shorter than its diff:
```python
import functools
import math

import jax
import jax.numpy as jnp
from jax import lax
from jax.experimental import pallas as pl
from jax.experimental.pallas import tpu as pltpu
from jax.sharding import PartitionSpec as P

SIDE = 24
NG = 864
NOCC = 64
NEMP = 256
LANES = 128
PLANES = 3


def round_up(value, step):
    return -(-value // step) * step


def pair_weights(tm, own_count, time_count, n_occ, n_emp, place_ref, scalar_ref, out_ref):
    me, tm_index = place_ref[0], place_ref[1]
    core, own_chip = lax.rem(me, 2), lax.div(me, 2)
    shape = out_ref.shape[1:]
    pair = lax.broadcasted_iota(jnp.int32, shape, 0) * LANES + lax.broadcasted_iota(jnp.int32, shape, 1)
    occ_number = lax.rem(pair, n_occ)
    occ_gap = jnp.zeros(shape, jnp.float32)
    emp_gap = jnp.zeros(shape, jnp.float32)
    for i in range(n_occ):
        occ_gap = jnp.where(occ_number == i, scalar_ref[core * n_occ + i], occ_gap)
    for j in range(n_emp):
        emp_gap = jnp.where(pair >= j * n_occ, scalar_ref[NOCC + own_chip * n_emp + j], emp_gap)
    first_time = NOCC + NEMP
    first_share = first_time + time_count
    weights = [jnp.zeros(shape, jnp.float32) for _ in range(own_count)]
    for k in range(time_count):
        hop, number = divmod(k, time_count // tm)
        source = lax.rem(tm_index + hop, tm) * (time_count // tm) + number
        time = scalar_ref[first_time + k]
        occ_factor = jnp.exp(-occ_gap * time) * NOCC ** (-0.5)
        emp_factor = jnp.exp(-emp_gap * time) * NEMP ** (-0.5)
        for w in range(own_count):
            share = scalar_ref[first_share + (tm_index * own_count + w) * time_count + source]
            weights[w] = weights[w] + share * (occ_factor * emp_factor)
    for w in range(own_count):
        out_ref[w] = weights[w]


def table_kernel(out_ref, with_cos, with_sin):
    kind = pl.program_id(0)
    a_odd, b_odd = kind // 2, kind % 2
    half = SIDE // 2
    a_waves, b_waves, c_waves = SIDE // 4, SIDE // 8, NG // (SIDE // 2 * (SIDE // 4) * 2)
    width = out_ref.shape[2]

    def parts(value, size):
        whole = jnp.floor((value + 0.5) * (1.0 / size))
        return whole, value - size * whole

    column = lax.broadcasted_iota(jnp.int32, (SIDE, width), 1).astype(jnp.float32)
    row = lax.broadcasted_iota(jnp.int32, (SIDE, width), 0).astype(jnp.float32)
    a_step, rest = parts(column, 2 * c_waves * b_waves)
    sine, rest = parts(rest, c_waves * b_waves)
    c_step, b_step = parts(rest, b_waves)
    a = 2.0 * a_step + ((a_odd + a_waves) % 2 - a_waves).astype(jnp.float32)
    b = 2.0 * b_step + ((b_odd + b_waves) % 2 - b_waves).astype(jnp.float32)
    c = c_step + 1.0
    unit = 2.0 * math.pi / SIDE
    size = jnp.where(a_step < a_waves, math.sqrt(2.0 / SIDE**3), 0.0)

    def factors(wave):
        angle = parts(wave * row, SIDE)[1] * unit
        return jnp.cos(angle), jnp.sin(angle)

    cos_p, sin_p = factors(a)
    cos_q, sin_q = factors(b)
    cos_s, sin_s = factors(c)
    is_sine = sine > 0.5
    for y in range(half):
        inner_cos = cos_q[y : y + 1] * cos_s - sin_q[y : y + 1] * sin_s
        inner_sin = sin_q[y : y + 1] * cos_s + cos_q[y : y + 1] * sin_s
        rows = slice(y * SIDE, (y + 1) * SIDE)
        with_cos[rows] = jnp.where(is_sine, inner_sin, inner_cos) * size
        with_sin[rows] = jnp.where(is_sine, inner_cos, -inner_sin) * size
    plane = half * SIDE
    depth = round_up(PLANES * plane, LANES)
    for x in range(half):
        start = x // PLANES * depth + x % PLANES * plane
        table = cos_p[x : x + 1] * with_cos[...] + sin_p[x : x + 1] * with_sin[...]
        out_ref[0, start : start + plane] = table.astype(jnp.bfloat16)
    for step in range(half // PLANES):
        out_ref[0, step * depth + PLANES * plane : (step + 1) * depth] = jnp.zeros(
            (depth - PLANES * plane, width), jnp.bfloat16
        )


def prepare_kernel(
    tm, own_count, time_count, n_occ, n_emp, place_ref, scalar_ref, table_ref, weight_ref, with_cos, with_sin
):
    @pl.when(pl.program_id(0) == 0)
    def _():
        pair_weights(tm, own_count, time_count, n_occ, n_emp, place_ref, scalar_ref, weight_ref)

    table_kernel(table_ref, with_cos, with_sin)


def prepare(place, scalars, tm, own_count, time_count, n_occ, n_emp):
    plane = SIDE * SIDE // 2
    depth = SIDE // 2 // PLANES * round_up(PLANES * plane, LANES)
    width = round_up(NG // 4, 2 * LANES)
    weight_shape = (own_count, n_occ * n_emp // LANES, LANES)
    return pl.pallas_call(
        functools.partial(prepare_kernel, tm, own_count, time_count, n_occ, n_emp),
        grid=(4,),
        out_shape=(
            jax.ShapeDtypeStruct((4, depth, width), jnp.bfloat16),
            jax.ShapeDtypeStruct(weight_shape, jnp.float32),
        ),
        in_specs=[pl.BlockSpec(memory_space=pltpu.SMEM)] * 2,
        out_specs=(
            pl.BlockSpec((1, depth, width), lambda k: (k, 0, 0)),
            pl.BlockSpec(weight_shape, lambda k: (0, 0, 0)),
        ),
        scratch_shapes=[pltpu.VMEM((plane, width), jnp.float32), pltpu.VMEM((plane, width), jnp.float32)],
        compiler_params=pltpu.CompilerParams(vmem_limit_bytes=60 * 1024 * 1024),
        cost_estimate=pl.CostEstimate(
            flops=64 * depth * width, bytes_accessed=8 * depth * width, transcendentals=0
        ),
        name="prepare",
    )(place, scalars)


def ring_place(chip, chips):
    return jnp.where(chip % 2 == 0, chip // 2, chips - (chip + 1) // 2)


def ring_chip(place, chips):
    place = lax.rem(place + chips, chips)
    return jnp.where(place < chips // 2, 2 * place, 2 * (chips - place) - 1)


def far_slots(chips):
    return [chips // 2, chips // 2 + 1]


def pair_kernel(offsets, place_ref, weight_ref, emp_own_ref, emp_other_ref, *refs):
    chips, n_emp, n_rows = emp_own_ref.shape
    shards = 2 * chips
    occ_refs, refs = refs[:chips], refs[chips:]
    table_hbm, keep_far, send_far, keep_near, send_near = refs[:5]
    occ_wide, emp_wide, rho, table, table_sem, raw_sem = refs[5:]
    depth = round_up(PLANES * SIDE * SIDE // 2, LANES)
    steps = table.shape[1] // depth
    n_occ = occ_wide.shape[1]
    per_group = chips // steps
    plane = SIDE * SIDE // 2
    half_emp = n_emp // 2
    half_pairs = half_emp * n_occ

    copy = pltpu.make_async_copy(table_hbm, table, table_sem)
    copy.start()

    me = place_ref[0]
    core, own_chip = lax.rem(me, 2), lax.div(me, 2)
    place = ring_place(own_chip, chips)

    def low_and_high(raw, rows, target):
        for far in range(2):
            for step in range(steps):
                group = far * steps + step
                shard_rows = [
                    raw[group * per_group + shard, rows].astype(jnp.float32) for shard in range(per_group)
                ]
                for upper in range(2):
                    pieces = []
                    for x in range(PLANES):
                        start = (2 * x + upper) * plane
                        stop = start + plane
                        while start < stop:
                            shard, offset = divmod(start, n_rows)
                            count = min(stop - start, n_rows - offset)
                            pieces.append(shard_rows[shard][:, offset : offset + count])
                            start += count
                    pieces.append(jnp.zeros((pieces[0].shape[0], depth - PLANES * plane), jnp.float32))
                    lanes = slice(step * depth, (step + 1) * depth)
                    target[2 * far + upper, rows, lanes] = jnp.concatenate(pieces, axis=1).astype(target.dtype)

    def arrange(raw_occ, raw_emp):
        copies = []
        for index, (offset, ref) in enumerate(zip(offsets, occ_refs, strict=True)):
            chip = ring_chip(place + offset, chips)
            copies += [
                pltpu.make_async_copy(ref.at[0], raw_occ.at[chip * 2 + core], raw_sem.at[4 * index]),
                pltpu.make_async_copy(ref.at[1], raw_occ.at[chip * 2 + 1 - core], raw_sem.at[4 * index + 1]),
                pltpu.make_async_copy(
                    emp_own_ref.at[index], raw_emp.at[index * 2 + core], raw_sem.at[4 * index + 2]
                ),
                pltpu.make_async_copy(
                    emp_other_ref.at[index], raw_emp.at[index * 2 + 1 - core], raw_sem.at[4 * index + 3]
                ),
            ]
        for raw_copy in copies:
            raw_copy.start()
        for raw_copy in copies:
            raw_copy.wait()

        def sixteen(raw, target):
            def rows(part, carry):
                low_and_high(raw, pl.ds(pl.multiple_of(part * 16, 16), 16), target)
                return carry

            lax.fori_loop(0, raw.shape[1] // 16, rows, 0)

        sixteen(raw_occ, occ_wide)
        sixteen(raw_emp, emp_wide)

    pl.run_scoped(
        arrange,
        pltpu.VMEM((shards, n_occ, n_rows), jnp.bfloat16),
        pltpu.VMEM((shards, n_emp, n_rows), jnp.bfloat16),
    )

    def build(half, target, cut):
        emp_rows = [emp_wide[k, half * half_emp : (half + 1) * half_emp, cut] for k in range(4)]
        for i in range(half_emp):
            emp_row = [
                jnp.broadcast_to(emp_rows[k][i : i + 1], (16, LANES)).astype(jnp.bfloat16) for k in range(4)
            ]
            for part in range(0, n_occ, 16):
                near_low, near_high, far_low, far_high = (
                    emp_row[k] * occ_wide[k, part : part + 16, cut] for k in range(4)
                )
                even_low, odd_low = near_low + far_low, near_low - far_low
                even_high, odd_high = near_high + far_high, near_high - far_high
                rows = slice(i * n_occ + part, i * n_occ + part + 16)
                target[0, rows, cut] = even_low + even_high
                target[1, rows, cut] = even_low - even_high
                target[2, rows, cut] = odd_low + odd_high
                target[3, rows, cut] = odd_low - odd_high

    modes = rho.shape[1]
    spacing = SIDE
    per_a = modes // spacing

    def multiply(half, source, k):
        found = jnp.dot(source[k], table[k], preferred_element_type=jnp.float32).T
        a_odd, b_odd = divmod(k, 2)
        a_first = (a_odd + SIDE // 4) % 2
        b_first = (b_odd + SIDE // 8) % 2
        for a_step in range(SIDE // 4):
            start = b_first * (SIDE // 2) + 2 * a_step + a_first
            for tile in range(half_pairs // LANES):
                rho[half * half_pairs // LANES + tile, pl.ds(start, per_a, stride=spacing), :] = found[
                    a_step * per_a : (a_step + 1) * per_a, tile * LANES : (tile + 1) * LANES
                ]

    chunks = steps * depth // LANES

    def transform(first, second):
        def build_first(chunk, carry):
            build(0, first, pl.ds(pl.multiple_of(chunk * LANES, LANES), LANES))
            return carry

        lax.fori_loop(0, chunks, build_first, 0)
        copy.wait()
        for k in range(4):
            for chunk in range(k * chunks // 4, (k + 1) * chunks // 4):
                build(1, second, slice(chunk * LANES, (chunk + 1) * LANES))
            multiply(0, first, k)
        for k in range(4):
            multiply(1, second, k)

    product = pltpu.VMEM((4, half_pairs, steps * depth), jnp.bfloat16)
    pl.run_scoped(transform, product, product)

    rows = NG // shards

    def combine(blocks):
        tiles = range(rho.shape[0])
        ordered = jnp.concatenate([rho[tile].astype(jnp.bfloat16) for tile in tiles], axis=1)
        per_part = shards // 4
        for part in range(4):
            cut = slice(part * per_part * rows, (part + 1) * per_part * rows)
            weighted = jnp.concatenate(
                [(rho[tile, cut] * weight_ref[tile : tile + 1]).astype(jnp.bfloat16) for tile in tiles], axis=1
            )
            moment = lax.dot_general(
                weighted, ordered, (((1,), (1,)), ((), ())), preferred_element_type=jnp.float32
            )
            for k in range(per_part):
                blocks[part * per_part + k] = moment[k * rows : (k + 1) * rows]
        far = far_slots(chips)
        near = [slot for slot in range(chips) if slot not in far]
        for slots, keep, send in ((far, keep_far, send_far), (near, keep_near, send_near)):
            for index, slot in enumerate(slots):
                chip = ring_chip(place + slot, chips)
                start = index * round_up(rows, 16)
                keep[start : start + rows, :NG] = blocks[2 * chip + core]
                send[start : start + rows, :NG] = blocks[2 * chip + 1 - core].astype(jnp.bfloat16)

    pl.run_scoped(combine, pltpu.VMEM((shards, rows, NG), jnp.float32))


def pair_moment(place, weights, occ_blocks, offsets, emp_own, emp_other, tables):
    chips, n_emp, _ = emp_own.shape
    n_occ = occ_blocks[0].shape[1]
    _, depth, width = tables.shape
    pairs = n_occ * n_emp
    rows = NG // (2 * chips)
    far_rows, near_rows = 2 * round_up(rows, 16), (chips - 2) * round_up(rows, 16)
    smem = pl.BlockSpec(memory_space=pltpu.SMEM)
    vmem = pl.BlockSpec(memory_space=pltpu.VMEM)
    hbm = pl.BlockSpec(memory_space=pl.ANY)
    return pl.pallas_call(
        functools.partial(pair_kernel, offsets),
        out_shape=tuple(
            jax.ShapeDtypeStruct((count, round_up(NG, LANES)), dtype)
            for count in (far_rows, near_rows)
            for dtype in (jnp.float32, jnp.bfloat16)
        ),
        in_specs=[smem, vmem] + [hbm] * (chips + 3),
        out_specs=(vmem, vmem, vmem, vmem),
        scratch_shapes=[
            pltpu.VMEM((4, n_occ, depth), jnp.bfloat16),
            pltpu.VMEM((4, n_emp, depth), jnp.float32),
            pltpu.VMEM((pairs // LANES, NG, LANES), jnp.float32),
            pltpu.VMEM((4, depth, width), jnp.bfloat16),
            pltpu.SemaphoreType.DMA,
            pltpu.SemaphoreType.DMA((4 * chips,)),
        ],
        compiler_params=pltpu.CompilerParams(vmem_limit_bytes=60 * 1024 * 1024),
        cost_estimate=pl.CostEstimate(
            flops=8 * pairs * depth * width, bytes_accessed=16 * 2**20, transcendentals=0
        ),
        name="pair_moment",
    )(place, weights, emp_own, emp_other, *occ_blocks, tables)


def ring_steps(chips):
    ring = list(range(0, chips, 2)) + list(range(chips - 1, 0, -2))
    ahead = [
        (2 * ring[k] + core, 2 * ring[(k + 1) % chips] + core) for k in range(chips) for core in range(2)
    ]
    return ahead, [(to, start) for start, to in ahead]


def hold(value, until):
    return lax.optimization_barrier((value, until))[0]


def gather_ring(block, chips, second, third):
    ahead, back = ring_steps(chips)
    found, offsets = [block], [0]
    from_left = from_right = block
    for hop in range(1, chips // 2 + 1):
        if hop == 2:
            from_left, from_right, second = lax.optimization_barrier((from_left, from_right, second))
        elif hop == 3:
            from_left, from_right, third = lax.optimization_barrier((from_left, from_right, third))
        elif hop > 3:
            from_left, from_right = lax.optimization_barrier((from_left, from_right))
        from_left = lax.ppermute(from_left, "space", ahead)
        found.append(from_left)
        offsets.append(-hop)
        if 2 * hop < chips:
            from_right = lax.ppermute(from_right, "space", back)
            found.append(from_right)
            offsets.append(hop)
    return found, offsets, second, third


def reduce_ring(totals, chips):
    ahead, back = ring_steps(chips)
    farthest = chips // 2
    from_left, from_right = totals[farthest], totals[farthest + 1]
    for hop in range(1, farthest + 1):
        from_left = lax.ppermute(from_left.astype(jnp.bfloat16), "space", ahead).astype(jnp.float32)
        if hop < farthest:
            from_right = lax.ppermute(from_right.astype(jnp.bfloat16), "space", back).astype(jnp.float32)
            from_left = from_left + totals[farthest - hop]
        if hop < farthest - 1:
            from_right = from_right + totals[farthest + 1 + hop]
    return (totals[0] + from_left + from_right)[:, :NG]


def local(space, tm, orbitals, gaps, times, cos_weights):
    rows = orbitals.shape[0]
    chips = space // 2
    columns = orbitals.T
    own_occ, own_emp = NOCC // 2, NEMP // chips
    own_count, time_count = cos_weights.shape[0] // tm, cos_weights.shape[1]
    me = lax.axis_index("space")
    core = me % 2
    swap = [(d, d ^ 1) for d in range(space)]

    every_time = [times] + [
        lax.ppermute(times, "tm", [((d + hop) % tm, d) for d in range(tm)]) for hop in range(1, tm)
    ]
    scalars = jnp.concatenate([gaps] + every_time + [cos_weights.reshape(-1)])
    place = jnp.stack([me, lax.axis_index("tm")]).astype(jnp.int32)

    occ = columns[:NOCC].reshape(2, own_occ, rows)
    occ_mine = lax.dynamic_index_in_dim(occ, core, 0, keepdims=False)
    occ_theirs = lax.dynamic_index_in_dim(occ, 1 - core, 0, keepdims=False)
    occ_pair = jnp.stack([occ_mine, lax.ppermute(occ_theirs, "space", swap)])
    emp_own = lax.all_to_all(
        columns[NOCC:].reshape(chips, own_emp, rows),
        "space",
        split_axis=0,
        concat_axis=0,
        axis_index_groups=[[2 * k + c for k in range(chips)] for c in range(2)],
    )
    made = prepare(place, hold(scalars, occ_pair), tm, own_count, time_count, own_occ, own_emp)
    occ_blocks, offsets, (tables, weights), emp_own = gather_ring(occ_pair, chips, made, emp_own)
    emp_other = lax.ppermute(emp_own, "space", swap)

    results = []
    part_rows = NG // space
    for w in range(own_count):
        keep_far, send_far, keep_near, send_near = pair_moment(
            place, weights[w], occ_blocks, offsets, emp_own, emp_other, tables
        )
        far_total = keep_far + lax.ppermute(send_far, "space", swap).astype(jnp.float32)
        near_total = keep_near + lax.ppermute(send_near, "space", swap).astype(jnp.float32)
        far = far_slots(chips)
        near = [slot for slot in range(chips) if slot not in far]
        totals = {}
        for slots, total in ((far, far_total), (near, near_total)):
            for index, slot in enumerate(slots):
                start = index * round_up(part_rows, 16)
                totals[slot] = total[start : start + part_rows]
        results.append(reduce_ring(totals, chips))
    return jnp.stack(results)


def solution(mesh):
    return jax.shard_map(
        functools.partial(local, mesh.shape["space"], mesh.shape["tm"]),
        mesh=mesh,
        in_specs=(P("space", None), P(), P("tm"), P()),
        out_specs=P("tm", "space", None),
        check_vma=False,
    )
```

time: 94.3 us -> 87.3 us (0.926)
  waiting for transfers between devices: 32.2 us -> 25.7 us
  Pallas kernels: 27.9 us -> 25.4 us
  other arithmetic: 2.73 us -> 4.48 us
    ppermute x3, waiting for transfers between devices: 8.45 us -> 2.43 us  [gather_ring(): from_right = lax.ppermute(from_right, 'space', back)]
    ppermute x4, starting transfers between devices: 1.21 us -> 5.38 us  [reduce_ring(): lax.ppermute(from_left.astype(jnp.bfloat16), 'space', ahead)]
    ppermute x3, starting transfers between devices: 5.4 us -> 2.14 us  [reduce_ring(): lax.ppermute(from_right.astype(jnp.bfloat16), 'space', back)]
    ppermute x4, starting transfers between devices: 7.48 us -> 5 us  [gather_ring(): from_left = lax.ppermute(from_left, 'space', ahead)]
    ppermute x3, waiting for transfers between devices: 0.7 us -> 2.71 us  [reduce_ring(): lax.ppermute(from_right.astype(jnp.bfloat16), 'space', back)]
    pallas_call x1, Pallas kernels: 21.7 us -> 19.8 us  [pair_moment(): pl.pallas_call(functools.partial(pair_kernel, offsets), out_shape=tuple((...]
    ppermute x3, starting transfers between devices: 2.08 us -> 3.87 us  [gather_ring(): from_right = lax.ppermute(from_right, 'space', back)]
    ppermute x1, waiting for transfers between devices: 1.6 us -> 0.01 us  [local(): lax.ppermute(times, 'tm', [((d + hop) % tm, d) for d in range(tm)])]
  transfers between devices with their start and end apart: 20 -> 20, of which waited for: 13 -> 11; matrix products, arithmetic and copies ran while one was open for 4% -> 6% of each run, Pallas kernels for 7% -> 6%
where the time goes in v3:
time: 87.3 us; the launch traced here: 86.9 us
  starting transfers between devices  25.9 us (30%)
  waiting for transfers between devices  25.7 us (29%)
  Pallas kernels  25.4 us (29%)
  local copies, waits for them, and re-layouts  4.57 us (5%)
  other arithmetic  4.48 us (5%)
    pallas_call x1, Pallas kernels, pair_moment(): pl.pallas_call(functools.partial(pair_kernel, offsets), out_shape=tuple((...  19.8 us
    ppermute x4, waiting for transfers between devices, reduce_ring(): lax.ppermute(from_left.astype(jnp.bfloat16), 'space', ahead)  9.99 us
    ppermute x4, waiting for transfers between devices, gather_ring(): from_left = lax.ppermute(from_left, 'space', ahead)  9.4 us
    all_to_all x1, starting transfers between devices, local(): lax.all_to_all(columns[NOCC:].reshape(chips, own_emp, rows), 'space', spl...  7.28 us
    pallas_call x1, Pallas kernels, prepare(): pl.pallas_call(functools.partial(prepare_kernel, tm, own_count, time_coun...  5.55 us
    ppermute x4, starting transfers between devices, reduce_ring(): lax.ppermute(from_left.astype(jnp.bfloat16), 'space', ahead)  5.38 us
    ppermute x4, starting transfers between devices, gather_ring(): from_left = lax.ppermute(from_left, 'space', ahead)  5 us
    ppermute x3, starting transfers between devices, gather_ring(): from_right = lax.ppermute(from_right, 'space', back)  3.87 us
  transfers between devices with their start and end apart: 20, of which 11 were waited for; matrix products, arithmetic and copies ran while one was open for 6% of the time, Pallas kernels for 6%

profile of v3, /device:TPU:0, one launch (start us, length us, event | category | flops | bytes accessed | tf_op | source)
XLA Modules:
  0.0 86.9 jit_solution(744750772721349787)
XLA Ops:
  0.0 1.9 %slice.47 = bf16[256,864]{1,0:T(8,128)(2,1)} slice(bf16[320,864]{1,0:T(8,128)(2,1)} %bitcast.11), slice={[64:320], [0:864]} | slice | bytes 884736 | tf_op jit(solution)/shard_map/slice | solution.py:409
  1.9 7.3 %all-to-all-start = ((bf16[8,32,864]{2,1,0:T(8,128)(2,1)}), bf16[8,32,864]{2,1,0:T(8,128)(2,1)S(1)}, u32[]{:S(2)}, u32[]{:S(2)}) async-start(bf16[8,32,864]{2,1,0:T(8,128)(2,1)} %bitcast.7), calls=%async_computation | async-start | bytes 917504 | tf_op jit(solution)/shard_map/all_to_all | solution.py:408
  9.2 1.5 %collective-permute-start.3 = (f32[1]{0:T(128)}, f32[1]{0:T(128)}, u32[]{:S(2)}, u32[]{:S(2)}) collective-permute-start(f32[1]{0:T(128)} %param.6), channel_id=1, source_target_pairs={{16,0},{0,16},{17,1},{1,17},{18,2},{2,18},{19,3},{3,19},{20,4},{4,... | collective-permute-start | bytes 20 | tf_op jit(solution)/shard_map/ppermute | solution.py:399
  10.7 0.9 %slice.46 = bf16[64,864]{1,0:T(8,128)(2,1)S(1)} slice(bf16[320,864]{1,0:T(8,128)(2,1)} %bitcast.12), slice={[0:64], [0:864]} | slice | bytes 221184 | tf_op jit(solution)/shard_map/slice | solution.py:404
  11.6 0.1 collective-permute-start
  11.7 0.6 pad_add_fusion.place_ref
  12.9 0.0 copy-done.11
  12.9 0.1 reshape.10
  13.0 0.0 collective-permute-done
  13.0 0.0 copy-start.1
  13.0 2.1 %collective-permute-start.2 = (bf16[2,32,864]{2,1,0:T(8,128)(2,1)S(1)}, bf16[2,32,864]{2,1,0:T(8,128)(2,1)S(1)}, u32[]{:S(2)}, u32[]{:S(2)}) collective-permute-start(bf16[2,32,864]{2,1,0:T(8,128)(2,1)S(1)} %pad_maximum_fusion.refs_0_), channel_id=1, source_target_pairs={{4,0},{5,1},{8,4},{9,5},{12,8},{13,9},{14,12},{15,13},{10,14},{11,... | collective-permute-start | bytes 331784 | tf_op jit(solution)/shard_map/ppermute | solution.py:368
  15.1 0.1 collective-permute-start.1
  15.2 0.0 collective-permute-done.3
  15.2 0.0 copy-done.2
  15.2 1.2 %pad_maximum_fusion.1.scalar_ref = f32[326]{0:T(512)} fusion(f32[4]{0:T(128)S(1)} %reshape.10, f32[1]{0:T(128)} %collective-permute-done.3, f32[1]{0:T(128)S(6)} %copy.6, f32[320]{0:T(512)S(1)} %copy-done.2), kind=kLoop, calls=%fused_computation.17 | loop fusion | flops 978 | bytes 2608 | tf_op jit(solution)/shard_map/concatenate | solution.py:401
  16.4 5.6 %prepare.1 = (bf16[4,3584,256]{2,1,0:T(8,128)(2,1)}, f32[1,8,128]{2,1,0:T(8,128)}) custom-call(s32[2]{0:T(128)} %pad_add_fusion.place_ref, f32[326]{0:T(512)} %pad_maximum_fusion.1.scalar_ref), custom_call_target="tpu_custom_call" | custom-call | flops 58720256 | bytes 7340032 | tf_op jit(solution)/shard_map/prepare/pallas_call | solution.py:114
  21.9 0.0 collective-permute-done.2.refs_2_
  21.9 0.0 collective-permute-done.1.refs_1_
  21.9 0.0 copy-start.5
  22.0 3.4 %collective-permute-start.4 = (bf16[2,32,864]{2,1,0:T(8,128)(2,1)S(1)}, bf16[2,32,864]{2,1,0:T(8,128)(2,1)S(1)}, u32[]{:S(2)}, u32[]{:S(2)}) collective-permute-start(bf16[2,32,864]{2,1,0:T(8,128)(2,1)S(1)} %collective-permute-done.1.refs_1_), channel_id=1, source_target_pairs={{0,4},{1,5},{4,8},{5,9},{8,12},{9,13},{12,14},{13,15},{14,10},{15,... | collective-permute-start | bytes 331784 | tf_op jit(solution)/shard_map/ppermute | solution.py:364
  25.3 0.0 collective-permute-start.5
  25.3 2.4 %collective-permute-done.4.refs_3_ = bf16[2,32,864]{2,1,0:T(8,128)(2,1)S(1)} collective-permute-done((bf16[2,32,864]{2,1,0:T(8,128)(2,1)S(1)}, bf16[2,32,864]{2,1,0:T(8,128)(2,1)S(1)}, u32[]{:S(2)}, u32[]{:S(2)}) %collective-permute-start.4) | collective-permute-done | bytes 110624 | tf_op jit(solution)/shard_map/ppermute | solution.py:364
  27.7 2.4 %collective-permute-done.5.refs_4_ = bf16[2,32,864]{2,1,0:T(8,128)(2,1)S(1)} collective-permute-done((bf16[2,32,864]{2,1,0:T(8,128)(2,1)S(1)}, bf16[2,32,864]{2,1,0:T(8,128)(2,1)S(1)}, u32[]{:S(2)}, u32[]{:S(2)}) %collective-permute-start.5) | collective-permute-done | bytes 110624 | tf_op jit(solution)/shard_map/ppermute | solution.py:368
  30.1 0.0 all-to-all-done.emp_own_ref
  30.1 0.1 collective-permute-start.6
  30.2 0.3 collective-permute-start.7
  30.5 1.8 %collective-permute-start.8 = (bf16[2,32,864]{2,1,0:T(8,128)(2,1)S(1)}, bf16[2,32,864]{2,1,0:T(8,128)(2,1)S(1)}, u32[]{:S(2)}, u32[]{:S(2)}) collective-permute-start(bf16[2,32,864]{2,1,0:T(8,128)(2,1)S(1)} %collective-permute-done.5.refs_4_), channel_id=1, source_target_pairs={{4,0},{5,1},{8,4},{9,5},{12,8},{13,9},{14,12},{15,13},{10,14},{11,... | collective-permute-start | bytes 331784 | tf_op jit(solution)/shard_map/ppermute | solution.py:368
  32.3 3.5 %collective-permute-done.7.refs_5_ = bf16[2,32,864]{2,1,0:T(8,128)(2,1)S(1)} collective-permute-done((bf16[2,32,864]{2,1,0:T(8,128)(2,1)S(1)}, bf16[2,32,864]{2,1,0:T(8,128)(2,1)S(1)}, u32[]{:S(2)}, u32[]{:S(2)}) %collective-permute-start.7) | collective-permute-done | bytes 110624 | tf_op jit(solution)/shard_map/ppermute | solution.py:364
  35.8 0.0 collective-permute-done.8.refs_6_
  35.8 1.3 %collective-permute-start.9 = (bf16[2,32,864]{2,1,0:T(8,128)(2,1)S(1)}, bf16[2,32,864]{2,1,0:T(8,128)(2,1)S(1)}, u32[]{:S(2)}, u32[]{:S(2)}) collective-permute-start(bf16[2,32,864]{2,1,0:T(8,128)(2,1)S(1)} %collective-permute-done.7.refs_5_), channel_id=1, source_target_pairs={{0,4},{1,5},{4,8},{5,9},{8,12},{9,13},{12,14},{13,15},{14,10},{15,... | collective-permute-start | bytes 331784 | tf_op jit(solution)/shard_map/ppermute | solution.py:364
  37.0 3.6 %collective-permute-done.9.refs_7_ = bf16[2,32,864]{2,1,0:T(8,128)(2,1)S(1)} collective-permute-done((bf16[2,32,864]{2,1,0:T(8,128)(2,1)S(1)}, bf16[2,32,864]{2,1,0:T(8,128)(2,1)S(1)}, u32[]{:S(2)}, u32[]{:S(2)}) %collective-permute-start.9) | collective-permute-done | bytes 110624 | tf_op jit(solution)/shard_map/ppermute | solution.py:364
  40.6 0.0 collective-permute-done.6.emp_other_ref
  40.6 0.0 copy-done.1
  40.6 0.0 copy-done.4
  40.6 0.0 copy-done.5
  40.6 0.0 copy-done.6
  40.6 0.0 copy-done.7
  40.7 0.0 copy-done
  40.7 0.0 copy-done.8
  40.7 0.6 copy-done.10
  41.2 0.2 copy-done.3
  41.4 19.8 %pair_moment.1 = (f32[128,896]{1,0:T(8,128)}, bf16[128,896]{1,0:T(8,128)(2,1)}, f32[384,896]{1,0:T(8,128)}, bf16[384,896]{1,0:T(8,128)(2,1)}) custom-call(s32[2]{0:T(128)} %pad_add_fusion.place_ref, f32[8,128]{1,0:T(8,128)} %bitcast.15, bf16[8,32,864]{2,1,0:T(8,128)(2,1)} %copy-done, bf16[8,32,864]{2,1,0:T(8,128)(2,1)} %copy-done.3, ...), custom_call_target="tpu_custom_call" | custom-call | flops 7516192768 | bytes 16777216 | tf_op jit(solution)/shard_map/pair_moment/pallas_call | solution.py:316
  61.3 0.1 collective-permute-start.11
  61.3 0.5 collective-permute-start.10
  61.8 1.2 %collective-permute-done.11 = bf16[128,896]{1,0:T(8,128)(2,1)S(1)} collective-permute-done((bf16[128,896]{1,0:T(8,128)(2,1)}, bf16[128,896]{1,0:T(8,128)(2,1)S(1)}, u32[]{:S(2)}, u32[]{:S(2)}) %collective-permute-start.11) | collective-permute-done | bytes 229408 | tf_op jit(solution)/shard_map/ppermute | solution.py:425
  63.0 1.1 %add_convert_fusion = bf16[128,896]{1,0:T(8,128)(2,1)S(1)} fusion(f32[128,896]{1,0:T(8,128)} %get-tuple-element.33, bf16[128,896]{1,0:T(8,128)(2,1)S(1)} %collective-permute-done.11), kind=kLoop, calls=%fused_computation.1 | loop fusion | flops 344064 | bytes 917504 | tf_op jit(solution)/shard_map/convert.1
  64.1 1.3 %collective-permute-start.12 = (bf16[54,896]{1,0:T(8,128)(2,1)S(1)}, bf16[54,896]{1,0:T(8,128)(2,1)S(1)}, u32[]{:S(2)}, u32[]{:S(2)}) collective-permute-start(bf16[54,896]{1,0:T(8,128)(2,1)S(1)} %get-tuple-element.40), channel_id=1, source_target_pairs={{0,4},{1,5},{4,8},{5,9},{8,12},{9,13},{12,14},{13,15},{14,10},{15,... | collective-permute-start | bytes 290312 | tf_op jit(solution)/shard_map/ppermute | solution.py:379
  65.4 0.8 collective-permute-start.16
  66.2 0.0 collective-permute-done.10
  66.2 1.5 %convert_add_fusion = f32[384,896]{1,0:T(8,128)S(1)} fusion(f32[384,896]{1,0:T(8,128)} %get-tuple-element.31, bf16[384,896]{1,0:T(8,128)(2,1)S(1)} %collective-permute-done.10), kind=kLoop, calls=%fused_computation | loop fusion | flops 688128 | bytes 3440640 | tf_op jit(solution)/shard_map/add | solution.py:426
  67.7 1.4 %collective-permute-done.12 = bf16[54,896]{1,0:T(8,128)(2,1)S(1)} collective-permute-done((bf16[54,896]{1,0:T(8,128)(2,1)S(1)}, bf16[54,896]{1,0:T(8,128)(2,1)S(1)}, u32[]{:S(2)}, u32[]{:S(2)}) %collective-permute-start.12) | collective-permute-done | bytes 96800 | tf_op jit(solution)/shard_map/ppermute | solution.py:379
  69.1 1.3 %collective-permute-start.13 = (bf16[54,896]{1,0:T(8,128)(2,1)S(1)}, bf16[54,896]{1,0:T(8,128)(2,1)S(1)}, u32[]{:S(2)}, u32[]{:S(2)}) collective-permute-start(bf16[54,896]{1,0:T(8,128)(2,1)S(1)} %fusion.6), channel_id=1, source_target_pairs={{0,4},{1,5},{4,8},{5,9},{8,12},{9,13},{12,14},{13,15},{14,10},{15,... | collective-permute-start | bytes 290312 | tf_op jit(solution)/shard_map/ppermute | solution.py:379
  70.4 0.0 collective-permute-done.16
  70.4 3.4 %collective-permute-done.13 = bf16[54,896]{1,0:T(8,128)(2,1)S(1)} collective-permute-done((bf16[54,896]{1,0:T(8,128)(2,1)S(1)}, bf16[54,896]{1,0:T(8,128)(2,1)S(1)}, u32[]{:S(2)}, u32[]{:S(2)}) %collective-permute-start.13) | collective-permute-done | bytes 96800 | tf_op jit(solution)/shard_map/ppermute | solution.py:379
  73.8 1.3 %collective-permute-start.14 = (bf16[54,896]{1,0:T(8,128)(2,1)S(1)}, bf16[54,896]{1,0:T(8,128)(2,1)S(1)}, u32[]{:S(2)}, u32[]{:S(2)}) collective-permute-start(bf16[54,896]{1,0:T(8,128)(2,1)S(1)} %get-tuple-element.38), channel_id=1, source_target_pairs={{0,4},{1,5},{4,8},{5,9},{8,12},{9,13},{12,14},{13,15},{14,10},{15,... | collective-permute-start | bytes 290312 | tf_op jit(solution)/shard_map/ppermute | solution.py:379
  75.1 0.8 collective-permute-start.17
  75.9 2.6 %collective-permute-done.14 = bf16[54,896]{1,0:T(8,128)(2,1)S(1)} collective-permute-done((bf16[54,896]{1,0:T(8,128)(2,1)S(1)}, bf16[54,896]{1,0:T(8,128)(2,1)S(1)}, u32[]{:S(2)}, u32[]{:S(2)}) %collective-permute-start.14) | collective-permute-done | bytes 96800 | tf_op jit(solution)/shard_map/ppermute | solution.py:379
  78.5 1.2 %collective-permute-done.17 = bf16[54,896]{1,0:T(8,128)(2,1)S(1)} collective-permute-done((bf16[54,896]{1,0:T(8,128)(2,1)S(1)}, bf16[54,896]{1,0:T(8,128)(2,1)S(1)}, u32[]{:S(2)}, u32[]{:S(2)}) %collective-permute-start.17) | collective-permute-done | bytes 96800 | tf_op jit(solution)/shard_map/ppermute | solution.py:381
  79.7 0.1 fusion.4
  79.8 1.5 %collective-permute-start.15 = (bf16[54,896]{1,0:T(8,128)(2,1)S(1)}, bf16[54,896]{1,0:T(8,128)(2,1)S(1)}, u32[]{:S(2)}, u32[]{:S(2)}) collective-permute-start(bf16[54,896]{1,0:T(8,128)(2,1)S(1)} %get-tuple-element.35), channel_id=1, source_target_pairs={{0,4},{1,5},{4,8},{5,9},{8,12},{9,13},{12,14},{13,15},{14,10},{15,... | collective-permute-start | bytes 290312 | tf_op jit(solution)/shard_map/ppermute | solution.py:379
  81.3 0.5 collective-permute-start.18
  81.9 2.6 %collective-permute-done.15 = bf16[54,896]{1,0:T(8,128)(2,1)S(1)} collective-permute-done((bf16[54,896]{1,0:T(8,128)(2,1)S(1)}, bf16[54,896]{1,0:T(8,128)(2,1)S(1)}, u32[]{:S(2)}, u32[]{:S(2)}) %collective-permute-start.15) | collective-permute-done | bytes 96800 | tf_op jit(solution)/shard_map/ppermute | solution.py:379
  84.5 1.5 %collective-permute-done.18 = bf16[54,896]{1,0:T(8,128)(2,1)S(1)} collective-permute-done((bf16[54,896]{1,0:T(8,128)(2,1)S(1)}, bf16[54,896]{1,0:T(8,128)(2,1)S(1)}, u32[]{:S(2)}, u32[]{:S(2)}) %collective-permute-start.18) | collective-permute-done | bytes 96800 | tf_op jit(solution)/shard_map/ppermute | solution.py:381
  86.0 0.9 %copy.5 = f32[1,54,864]{2,0,1:T(1,128)} copy(f32[1,54,864]{2,1,0:T(8,128)S(1)} %fusion.1) | data formatting | bytes 373248 | tf_op jit(solution)/shard_map/stack | solution.py:435
  (17 shorter events, 0.2 us)
Async XLA Ops:
  0.0 12.9 %copy-start.11 = (f32[2,2]{1,0:T(2,128)S(1)}, f32[2,2]{1,0:T(2,128)}, u32[]{:S(2)}) copy-start(f32[2,2]{1,0:T(2,128)} %param.7) | copy-start | bytes 52
  0.0 15.2 %copy-start.2 = (f32[320]{0:T(512)S(1)}, f32[320]{0:T(512)}, u32[]{:S(2)}) copy-start(f32[320]{0:T(512)} %param.5) | copy-start | bytes 3844
  1.9 28.2 %all-to-all-start = ((bf16[8,32,864]{2,1,0:T(8,128)(2,1)}), bf16[8,32,864]{2,1,0:T(8,128)(2,1)S(1)}, u32[]{:S(2)}, u32[]{:S(2)}) async-start(bf16[8,32,864]{2,1,0:T(8,128)(2,1)} %bitcast.7), calls=%async_computation | async-start | bytes 917504 | tf_op jit(solution)/shard_map/all_to_all | solution.py:408
  9.2 6.0 %collective-permute-start.3 = (f32[1]{0:T(128)}, f32[1]{0:T(128)}, u32[]{:S(2)}, u32[]{:S(2)}) collective-permute-start(f32[1]{0:T(128)} %param.6), channel_id=1, source_target_pairs={{16,0},{0,16},{17,1},{1,17},{18,2},{2,18},{19,3},{3,19},{20,4},{4,... | collective-permute-start | bytes 20 | tf_op jit(solution)/shard_map/ppermute | solution.py:399
  11.6 1.4 %collective-permute-start = (bf16[32,864]{1,0:T(8,128)(2,1)S(1)}, bf16[32,864]{1,0:T(8,128)(2,1)S(1)}, u32[]{:S(2)}, u32[]{:S(2)}) collective-permute-start(bf16[32,864]{1,0:T(8,128)(2,1)S(1)} %get-tuple-element.43), channel_id=1, source_target_pairs={{0,1},{1,0},{2,3},{3,2},{4,5},{5,4},{6,7},{7,6},{8,9},{9,8},{10,11... | collective-permute-start | bytes 165896 | tf_op jit(solution)/shard_map/ppermute | solution.py:407
  13.0 27.6 %copy-start.1 = (bf16[2,32,864]{2,1,0:T(8,128)(2,1)}, bf16[2,32,864]{2,1,0:T(8,128)(2,1)S(1)}, u32[]{:S(2)}) copy-start(bf16[2,32,864]{2,1,0:T(8,128)(2,1)S(1)} %pad_maximum_fusion.refs_0_) | copy-start | bytes 331780
  13.0 8.9 %collective-permute-start.2 = (bf16[2,32,864]{2,1,0:T(8,128)(2,1)S(1)}, bf16[2,32,864]{2,1,0:T(8,128)(2,1)S(1)}, u32[]{:S(2)}, u32[]{:S(2)}) collective-permute-start(bf16[2,32,864]{2,1,0:T(8,128)(2,1)S(1)} %pad_maximum_fusion.refs_0_), channel_id=1, source_target_pairs={{4,0},{5,1},{8,4},{9,5},{12,8},{13,9},{14,12},{15,13},{10,14},{11,... | collective-permute-start | bytes 331784 | tf_op jit(solution)/shard_map/ppermute | solution.py:368
  15.1 6.8 %collective-permute-start.1 = (bf16[2,32,864]{2,1,0:T(8,128)(2,1)S(1)}, bf16[2,32,864]{2,1,0:T(8,128)(2,1)S(1)}, u32[]{:S(2)}, u32[]{:S(2)}) collective-permute-start(bf16[2,32,864]{2,1,0:T(8,128)(2,1)S(1)} %pad_maximum_fusion.refs_0_), channel_id=1, source_target_pairs={{0,4},{1,5},{4,8},{5,9},{8,12},{9,13},{12,14},{13,15},{14,10},{15,... | collective-permute-start | bytes 331784 | tf_op jit(solution)/shard_map/ppermute | solution.py:364
  21.9 18.7 %copy-start.4 = (bf16[2,32,864]{2,1,0:T(8,128)(2,1)}, bf16[2,32,864]{2,1,0:T(8,128)(2,1)S(1)}, u32[]{:S(2)}) copy-start(bf16[2,32,864]{2,1,0:T(8,128)(2,1)S(1)} %collective-permute-done.2.refs_2_) | copy-start | bytes 331780
  21.9 18.7 %copy-start.5 = (bf16[2,32,864]{2,1,0:T(8,128)(2,1)}, bf16[2,32,864]{2,1,0:T(8,128)(2,1)S(1)}, u32[]{:S(2)}) copy-start(bf16[2,32,864]{2,1,0:T(8,128)(2,1)S(1)} %collective-permute-done.1.refs_1_) | copy-start | bytes 331780
  22.0 5.7 %collective-permute-start.4 = (bf16[2,32,864]{2,1,0:T(8,128)(2,1)S(1)}, bf16[2,32,864]{2,1,0:T(8,128)(2,1)S(1)}, u32[]{:S(2)}, u32[]{:S(2)}) collective-permute-start(bf16[2,32,864]{2,1,0:T(8,128)(2,1)S(1)} %collective-permute-done.1.refs_1_), channel_id=1, source_target_pairs={{0,4},{1,5},{4,8},{5,9},{8,12},{9,13},{12,14},{13,15},{14,10},{15,... | collective-permute-start | bytes 331784 | tf_op jit(solution)/shard_map/ppermute | solution.py:364
  25.3 4.8 %collective-permute-start.5 = (bf16[2,32,864]{2,1,0:T(8,128)(2,1)S(1)}, bf16[2,32,864]{2,1,0:T(8,128)(2,1)S(1)}, u32[]{:S(2)}, u32[]{:S(2)}) collective-permute-start(bf16[2,32,864]{2,1,0:T(8,128)(2,1)S(1)} %collective-permute-done.2.refs_2_), channel_id=1, source_target_pairs={{4,0},{5,1},{8,4},{9,5},{12,8},{13,9},{14,12},{15,13},{10,14},{11,... | collective-permute-start | bytes 331784 | tf_op jit(solution)/shard_map/ppermute | solution.py:368
  27.7 12.9 %copy-start.6 = (bf16[2,32,864]{2,1,0:T(8,128)(2,1)}, bf16[2,32,864]{2,1,0:T(8,128)(2,1)S(1)}, u32[]{:S(2)}) copy-start(bf16[2,32,864]{2,1,0:T(8,128)(2,1)S(1)} %collective-permute-done.4.refs_3_) | copy-start | bytes 331780
  30.1 10.5 %copy-start.7 = (bf16[2,32,864]{2,1,0:T(8,128)(2,1)}, bf16[2,32,864]{2,1,0:T(8,128)(2,1)S(1)}, u32[]{:S(2)}) copy-start(bf16[2,32,864]{2,1,0:T(8,128)(2,1)S(1)} %collective-permute-done.5.refs_4_) | copy-start | bytes 331780
  30.1 10.5 %copy-start = (bf16[8,32,864]{2,1,0:T(8,128)(2,1)}, bf16[8,32,864]{2,1,0:T(8,128)(2,1)S(1)}, u32[]{:S(2)}) copy-start(bf16[8,32,864]{2,1,0:T(8,128)(2,1)S(1)} %all-to-all-done.emp_own_ref) | copy-start | bytes 1327108
  30.1 10.5 %collective-permute-start.6 = (bf16[8,32,864]{2,1,0:T(8,128)(2,1)S(1)}, bf16[8,32,864]{2,1,0:T(8,128)(2,1)S(1)}, u32[]{:S(2)}, u32[]{:S(2)}) collective-permute-start(bf16[8,32,864]{2,1,0:T(8,128)(2,1)S(1)} %all-to-all-done.emp_own_ref), channel_id=1, source_target_pairs={{0,1},{1,0},{2,3},{3,2},{4,5},{5,4},{6,7},{7,6},{8,9},{9,8},{10,11... | collective-permute-start | bytes 1327112 | tf_op jit(solution)/shard_map/ppermute | solution.py:417
  30.2 5.5 %collective-permute-start.7 = (bf16[2,32,864]{2,1,0:T(8,128)(2,1)S(1)}, bf16[2,32,864]{2,1,0:T(8,128)(2,1)S(1)}, u32[]{:S(2)}, u32[]{:S(2)}) collective-permute-start(bf16[2,32,864]{2,1,0:T(8,128)(2,1)S(1)} %collective-permute-done.4.refs_3_), channel_id=1, source_target_pairs={{0,4},{1,5},{4,8},{5,9},{8,12},{9,13},{12,14},{13,15},{14,10},{15,... | collective-permute-start | bytes 331784 | tf_op jit(solution)/shard_map/ppermute | solution.py:364
  30.5 5.3 %collective-permute-start.8 = (bf16[2,32,864]{2,1,0:T(8,128)(2,1)S(1)}, bf16[2,32,864]{2,1,0:T(8,128)(2,1)S(1)}, u32[]{:S(2)}, u32[]{:S(2)}) collective-permute-start(bf16[2,32,864]{2,1,0:T(8,128)(2,1)S(1)} %collective-permute-done.5.refs_4_), channel_id=1, source_target_pairs={{4,0},{5,1},{8,4},{9,5},{12,8},{13,9},{14,12},{15,13},{10,14},{11,... | collective-permute-start | bytes 331784 | tf_op jit(solution)/shard_map/ppermute | solution.py:368
  35.8 4.9 %copy-start.8 = (bf16[2,32,864]{2,1,0:T(8,128)(2,1)}, bf16[2,32,864]{2,1,0:T(8,128)(2,1)S(1)}, u32[]{:S(2)}) copy-start(bf16[2,32,864]{2,1,0:T(8,128)(2,1)S(1)} %collective-permute-done.7.refs_5_) | copy-start | bytes 331780
  35.8 4.9 %copy-start.9 = (bf16[2,32,864]{2,1,0:T(8,128)(2,1)}, bf16[2,32,864]{2,1,0:T(8,128)(2,1)S(1)}, u32[]{:S(2)}) copy-start(bf16[2,32,864]{2,1,0:T(8,128)(2,1)S(1)} %collective-permute-done.8.refs_6_) | copy-start | bytes 331780
  35.8 4.8 %collective-permute-start.9 = (bf16[2,32,864]{2,1,0:T(8,128)(2,1)S(1)}, bf16[2,32,864]{2,1,0:T(8,128)(2,1)S(1)}, u32[]{:S(2)}, u32[]{:S(2)}) collective-permute-start(bf16[2,32,864]{2,1,0:T(8,128)(2,1)S(1)} %collective-permute-done.7.refs_5_), channel_id=1, source_target_pairs={{0,4},{1,5},{4,8},{5,9},{8,12},{9,13},{12,14},{13,15},{14,10},{15,... | collective-permute-start | bytes 331784 | tf_op jit(solution)/shard_map/ppermute | solution.py:364
  40.6 0.6 copy-start.10
  40.6 0.8 copy-start.3
  61.3 1.8 %collective-permute-start.11 = (bf16[128,896]{1,0:T(8,128)(2,1)}, bf16[128,896]{1,0:T(8,128)(2,1)S(1)}, u32[]{:S(2)}, u32[]{:S(2)}) collective-permute-start(bf16[128,896]{1,0:T(8,128)(2,1)} %get-tuple-element.34), channel_id=1, source_target_pairs={{0,1},{1,0},{2,3},{3,2},{4,5},{5,4},{6,7},{7,6},{8,9},{9,8},{10,11... | collective-permute-start | bytes 688136 | tf_op jit(solution)/shard_map/ppermute | solution.py:425
  61.3 4.9 %collective-permute-start.10 = (bf16[384,896]{1,0:T(8,128)(2,1)}, bf16[384,896]{1,0:T(8,128)(2,1)S(1)}, u32[]{:S(2)}, u32[]{:S(2)}) collective-permute-start(bf16[384,896]{1,0:T(8,128)(2,1)} %get-tuple-element.32), channel_id=1, source_target_pairs={{0,1},{1,0},{2,3},{3,2},{4,5},{5,4},{6,7},{7,6},{8,9},{9,8},{10,11... | collective-permute-start | bytes 2064392 | tf_op jit(solution)/shard_map/ppermute | solution.py:426
  64.1 4.9 %collective-permute-start.12 = (bf16[54,896]{1,0:T(8,128)(2,1)S(1)}, bf16[54,896]{1,0:T(8,128)(2,1)S(1)}, u32[]{:S(2)}, u32[]{:S(2)}) collective-permute-start(bf16[54,896]{1,0:T(8,128)(2,1)S(1)} %get-tuple-element.40), channel_id=1, source_target_pairs={{0,4},{1,5},{4,8},{5,9},{8,12},{9,13},{12,14},{13,15},{14,10},{15,... | collective-permute-start | bytes 290312 | tf_op jit(solution)/shard_map/ppermute | solution.py:379
  65.4 5.0 %collective-permute-start.16 = (bf16[54,896]{1,0:T(8,128)(2,1)S(1)}, bf16[54,896]{1,0:T(8,128)(2,1)S(1)}, u32[]{:S(2)}, u32[]{:S(2)}) collective-permute-start(bf16[54,896]{1,0:T(8,128)(2,1)S(1)} %get-tuple-element.41), channel_id=1, source_target_pairs={{4,0},{5,1},{8,4},{9,5},{12,8},{13,9},{14,12},{15,13},{10,14},{11,... | collective-permute-start | bytes 290312 | tf_op jit(solution)/shard_map/ppermute | solution.py:381
  69.1 4.7 %collective-permute-start.13 = (bf16[54,896]{1,0:T(8,128)(2,1)S(1)}, bf16[54,896]{1,0:T(8,128)(2,1)S(1)}, u32[]{:S(2)}, u32[]{:S(2)}) collective-permute-start(bf16[54,896]{1,0:T(8,128)(2,1)S(1)} %fusion.6), channel_id=1, source_target_pairs={{0,4},{1,5},{4,8},{5,9},{8,12},{9,13},{12,14},{13,15},{14,10},{15,... | collective-permute-start | bytes 290312 | tf_op jit(solution)/shard_map/ppermute | solution.py:379
  73.8 4.7 %collective-permute-start.14 = (bf16[54,896]{1,0:T(8,128)(2,1)S(1)}, bf16[54,896]{1,0:T(8,128)(2,1)S(1)}, u32[]{:S(2)}, u32[]{:S(2)}) collective-permute-start(bf16[54,896]{1,0:T(8,128)(2,1)S(1)} %get-tuple-element.38), channel_id=1, source_target_pairs={{0,4},{1,5},{4,8},{5,9},{8,12},{9,13},{12,14},{13,15},{14,10},{15,... | collective-permute-start | bytes 290312 | tf_op jit(solution)/shard_map/ppermute | solution.py:379
  75.1 4.6 %collective-permute-start.17 = (bf16[54,896]{1,0:T(8,128)(2,1)S(1)}, bf16[54,896]{1,0:T(8,128)(2,1)S(1)}, u32[]{:S(2)}, u32[]{:S(2)}) collective-permute-start(bf16[54,896]{1,0:T(8,128)(2,1)S(1)} %get-tuple-element.39), channel_id=1, source_target_pairs={{4,0},{5,1},{8,4},{9,5},{12,8},{13,9},{14,12},{15,13},{10,14},{11,... | collective-permute-start | bytes 290312 | tf_op jit(solution)/shard_map/ppermute | solution.py:381
  79.8 4.7 %collective-permute-start.15 = (bf16[54,896]{1,0:T(8,128)(2,1)S(1)}, bf16[54,896]{1,0:T(8,128)(2,1)S(1)}, u32[]{:S(2)}, u32[]{:S(2)}) collective-permute-start(bf16[54,896]{1,0:T(8,128)(2,1)S(1)} %get-tuple-element.35), channel_id=1, source_target_pairs={{0,4},{1,5},{4,8},{5,9},{8,12},{9,13},{12,14},{13,15},{14,10},{15,... | collective-permute-start | bytes 290312 | tf_op jit(solution)/shard_map/ppermute | solution.py:379
  81.3 4.6 %collective-permute-start.18 = (bf16[54,896]{1,0:T(8,128)(2,1)S(1)}, bf16[54,896]{1,0:T(8,128)(2,1)S(1)}, u32[]{:S(2)}, u32[]{:S(2)}) collective-permute-start(bf16[54,896]{1,0:T(8,128)(2,1)S(1)} %get-tuple-element.36), channel_id=1, source_target_pairs={{4,0},{5,1},{8,4},{9,5},{12,8},{13,9},{14,12},{15,13},{10,14},{11,... | collective-permute-start | bytes 290312 | tf_op jit(solution)/shard_map/ppermute | solution.py:381

commit v4 on v3

--- a/solution.py
+++ b/solution.py
@@ -48,8 +48,8 @@
         out_ref[w] = weights[w]
 
 
-def table_kernel(out_ref, with_cos, with_sin):
-    kind = pl.program_id(0)
+def table_kernel(held_ref, out_ref, with_cos, with_sin):
+    kind = pl.program_id(0) + held_ref[0]
     a_odd, b_odd = kind // 2, kind % 2
     half = SIDE // 2
     a_waves, b_waves, c_waves = SIDE // 4, SIDE // 8, NG // (SIDE // 2 * (SIDE // 4) * 2)
@@ -96,39 +96,34 @@
         )
 
 
-def prepare_kernel(
-    tm, own_count, time_count, n_occ, n_emp, place_ref, scalar_ref, table_ref, weight_ref, with_cos, with_sin
-):
-    @pl.when(pl.program_id(0) == 0)
-    def _():
-        pair_weights(tm, own_count, time_count, n_occ, n_emp, place_ref, scalar_ref, weight_ref)
-
-    table_kernel(table_ref, with_cos, with_sin)
-
-
-def prepare(place, scalars, tm, own_count, time_count, n_occ, n_emp):
+def class_tables(held):
     plane = SIDE * SIDE // 2
     depth = SIDE // 2 // PLANES * round_up(PLANES * plane, LANES)
     width = round_up(NG // 4, 2 * LANES)
-    weight_shape = (own_count, n_occ * n_emp // LANES, LANES)
     return pl.pallas_call(
-        functools.partial(prepare_kernel, tm, own_count, time_count, n_occ, n_emp),
+        table_kernel,
         grid=(4,),
-        out_shape=(
-            jax.ShapeDtypeStruct((4, depth, width), jnp.bfloat16),
-            jax.ShapeDtypeStruct(weight_shape, jnp.float32),
-        ),
-        in_specs=[pl.BlockSpec(memory_space=pltpu.SMEM)] * 2,
-        out_specs=(
-            pl.BlockSpec((1, depth, width), lambda k: (k, 0, 0)),
-            pl.BlockSpec(weight_shape, lambda k: (0, 0, 0)),
-        ),
+        out_shape=jax.ShapeDtypeStruct((4, depth, width), jnp.bfloat16),
+        in_specs=[pl.BlockSpec(memory_space=pltpu.SMEM)],
+        out_specs=pl.BlockSpec((1, depth, width), lambda k: (k, 0, 0)),
         scratch_shapes=[pltpu.VMEM((plane, width), jnp.float32), pltpu.VMEM((plane, width), jnp.float32)],
         compiler_params=pltpu.CompilerParams(vmem_limit_bytes=60 * 1024 * 1024),
         cost_estimate=pl.CostEstimate(
             flops=64 * depth * width, bytes_accessed=8 * depth * width, transcendentals=0
         ),
-        name="prepare",
+        name="class_tables",
+    )(held)
+
+
+def all_pair_weights(place, scalars, tm, own_count, time_count, n_occ, n_emp):
+    smem = pl.BlockSpec(memory_space=pltpu.SMEM)
+    return pl.pallas_call(
+        functools.partial(pair_weights, tm, own_count, time_count, n_occ, n_emp),
+        out_shape=jax.ShapeDtypeStruct((own_count, n_occ * n_emp // LANES, LANES), jnp.float32),
+        in_specs=[smem, smem],
+        out_specs=pl.BlockSpec(memory_space=pltpu.VMEM),
+        cost_estimate=pl.CostEstimate(flops=2**24, bytes_accessed=2**20, transcendentals=0),
+        name="pair_weights",
     )(place, scalars)
 
 
@@ -145,8 +140,10 @@
     return [chips // 2, chips // 2 + 1]
 
 
-def pair_kernel(offsets, place_ref, weight_ref, emp_own_ref, emp_other_ref, *refs):
-    chips, n_emp, n_rows = emp_own_ref.shape
+def pair_kernel(offsets, splits, place_ref, weight_ref, *refs):
+    emp_refs, refs = refs[: 2 * splits], refs[2 * splits :]
+    chips, part_emp, n_rows = emp_refs[0].shape
+    n_emp = splits * part_emp
     shards = 2 * chips
     occ_refs, refs = refs[:chips], refs[chips:]
     table_hbm, keep_far, send_far, keep_near, send_near = refs[:5]
@@ -160,8 +157,6 @@
     half_pairs = half_emp * n_occ
 
     copy = pltpu.make_async_copy(table_hbm, table, table_sem)
-    copy.start()
-
     me = place_ref[0]
     core, own_chip = lax.rem(me, 2), lax.div(me, 2)
     place = ring_place(own_chip, chips)
@@ -170,8 +165,10 @@
         for far in range(2):
             for step in range(steps):
                 group = far * steps + step
+                first_chip = group * per_group // 2
                 shard_rows = [
-                    raw[group * per_group + shard, rows].astype(jnp.float32) for shard in range(per_group)
+                    raw[first_chip + shard // 2, shard % 2, rows].astype(jnp.float32)
+                    for shard in range(per_group)
                 ]
                 for upper in range(2):
                     pieces = []
@@ -191,35 +188,34 @@
         copies = []
         for index, (offset, ref) in enumerate(zip(offsets, occ_refs, strict=True)):
             chip = ring_chip(place + offset, chips)
-            copies += [
-                pltpu.make_async_copy(ref.at[0], raw_occ.at[chip * 2 + core], raw_sem.at[4 * index]),
-                pltpu.make_async_copy(ref.at[1], raw_occ.at[chip * 2 + 1 - core], raw_sem.at[4 * index + 1]),
-                pltpu.make_async_copy(
-                    emp_own_ref.at[index], raw_emp.at[index * 2 + core], raw_sem.at[4 * index + 2]
-                ),
-                pltpu.make_async_copy(
-                    emp_other_ref.at[index], raw_emp.at[index * 2 + 1 - core], raw_sem.at[4 * index + 3]
-                ),
-            ]
+            for other in range(2):
+                target = raw_occ.at[chip, 1 - core if other else core]
+                copies.append(pltpu.make_async_copy(ref.at[other], target, raw_sem.at[2 * index + other]))
+        for index, ref in enumerate(emp_refs):
+            part, other = divmod(index, 2)
+            start = pl.multiple_of(lax.rem(place_ref[1] + part, splits) * part_emp, part_emp)
+            target = raw_emp.at[:, 1 - core if other else core, pl.ds(start, part_emp)]
+            copies.append(pltpu.make_async_copy(ref, target, raw_sem.at[shards + index]))
         for raw_copy in copies:
             raw_copy.start()
         for raw_copy in copies:
             raw_copy.wait()
+        copy.start()
 
         def sixteen(raw, target):
             def rows(part, carry):
                 low_and_high(raw, pl.ds(pl.multiple_of(part * 16, 16), 16), target)
                 return carry
 
-            lax.fori_loop(0, raw.shape[1] // 16, rows, 0)
+            lax.fori_loop(0, raw.shape[2] // 16, rows, 0)
 
         sixteen(raw_occ, occ_wide)
         sixteen(raw_emp, emp_wide)
 
     pl.run_scoped(
         arrange,
-        pltpu.VMEM((shards, n_occ, n_rows), jnp.bfloat16),
-        pltpu.VMEM((shards, n_emp, n_rows), jnp.bfloat16),
+        pltpu.VMEM((chips, 2, n_occ, n_rows), jnp.bfloat16),
+        pltpu.VMEM((chips, 2, n_emp, n_rows), jnp.bfloat16),
     )
 
     def build(half, target, cut):
@@ -280,17 +276,14 @@
     def combine(blocks):
         tiles = range(rho.shape[0])
         ordered = jnp.concatenate([rho[tile].astype(jnp.bfloat16) for tile in tiles], axis=1)
-        per_part = shards // 4
-        for part in range(4):
-            cut = slice(part * per_part * rows, (part + 1) * per_part * rows)
-            weighted = jnp.concatenate(
-                [(rho[tile, cut] * weight_ref[tile : tile + 1]).astype(jnp.bfloat16) for tile in tiles], axis=1
-            )
-            moment = lax.dot_general(
-                weighted, ordered, (((1,), (1,)), ((), ())), preferred_element_type=jnp.float32
-            )
-            for k in range(per_part):
-                blocks[part * per_part + k] = moment[k * rows : (k + 1) * rows]
+        weighted = jnp.concatenate(
+            [(rho[tile] * weight_ref[tile : tile + 1]).astype(jnp.bfloat16) for tile in tiles], axis=1
+        )
+        moment = lax.dot_general(
+            weighted, ordered, (((1,), (1,)), ((), ())), preferred_element_type=jnp.float32
+        )
+        for k in range(shards):
+            blocks[k] = moment[k * rows : (k + 1) * rows]
         far = far_slots(chips)
         near = [slot for slot in range(chips) if slot not in far]
         for slots, keep, send in ((far, keep_far, send_far), (near, keep_near, send_near)):
@@ -303,8 +296,10 @@
     pl.run_scoped(combine, pltpu.VMEM((shards, rows, NG), jnp.float32))
 
 
-def pair_moment(place, weights, occ_blocks, offsets, emp_own, emp_other, tables):
-    chips, n_emp, _ = emp_own.shape
+def pair_moment(place, weights, occ_blocks, offsets, emp_parts, tables):
+    splits = len(emp_parts) // 2
+    chips, part_emp, _ = emp_parts[0].shape
+    n_emp = splits * part_emp
     n_occ = occ_blocks[0].shape[1]
     _, depth, width = tables.shape
     pairs = n_occ * n_emp
@@ -314,13 +309,13 @@
     vmem = pl.BlockSpec(memory_space=pltpu.VMEM)
     hbm = pl.BlockSpec(memory_space=pl.ANY)
     return pl.pallas_call(
-        functools.partial(pair_kernel, offsets),
+        functools.partial(pair_kernel, offsets, splits),
         out_shape=tuple(
             jax.ShapeDtypeStruct((count, round_up(NG, LANES)), dtype)
             for count in (far_rows, near_rows)
             for dtype in (jnp.float32, jnp.bfloat16)
         ),
-        in_specs=[smem, vmem] + [hbm] * (chips + 3),
+        in_specs=[smem, vmem] + [hbm] * (2 * splits + chips + 1),
         out_specs=(vmem, vmem, vmem, vmem),
         scratch_shapes=[
             pltpu.VMEM((4, n_occ, depth), jnp.bfloat16),
@@ -328,14 +323,14 @@
             pltpu.VMEM((pairs // LANES, NG, LANES), jnp.float32),
             pltpu.VMEM((4, depth, width), jnp.bfloat16),
             pltpu.SemaphoreType.DMA,
-            pltpu.SemaphoreType.DMA((4 * chips,)),
+            pltpu.SemaphoreType.DMA((2 * chips + 2 * splits,)),
         ],
         compiler_params=pltpu.CompilerParams(vmem_limit_bytes=60 * 1024 * 1024),
         cost_estimate=pl.CostEstimate(
             flops=8 * pairs * depth * width, bytes_accessed=16 * 2**20, transcendentals=0
         ),
         name="pair_moment",
-    )(place, weights, emp_own, emp_other, *occ_blocks, tables)
+    )(place, weights, *emp_parts, *occ_blocks, tables)
 
 
 def ring_steps(chips):
@@ -348,27 +343,6 @@
 
 def hold(value, until):
     return lax.optimization_barrier((value, until))[0]
-
-
-def gather_ring(block, chips, second, third):
-    ahead, back = ring_steps(chips)
-    found, offsets = [block], [0]
-    from_left = from_right = block
-    for hop in range(1, chips // 2 + 1):
-        if hop == 2:
-            from_left, from_right, second = lax.optimization_barrier((from_left, from_right, second))
-        elif hop == 3:
-            from_left, from_right, third = lax.optimization_barrier((from_left, from_right, third))
-        elif hop > 3:
-            from_left, from_right = lax.optimization_barrier((from_left, from_right))
-        from_left = lax.ppermute(from_left, "space", ahead)
-        found.append(from_left)
-        offsets.append(-hop)
-        if 2 * hop < chips:
-            from_right = lax.ppermute(from_right, "space", back)
-            found.append(from_right)
-            offsets.append(hop)
-    return found, offsets, second, third
 
 
 def reduce_ring(totals, chips):
@@ -405,22 +379,54 @@
     occ_mine = lax.dynamic_index_in_dim(occ, core, 0, keepdims=False)
     occ_theirs = lax.dynamic_index_in_dim(occ, 1 - core, 0, keepdims=False)
     occ_pair = jnp.stack([occ_mine, lax.ppermute(occ_theirs, "space", swap)])
-    emp_own = lax.all_to_all(
-        columns[NOCC:].reshape(chips, own_emp, rows),
+    splits = tm if tm == 2 else 1
+    emp_columns = lax.dynamic_slice(
+        columns.reshape((NOCC + NEMP) // own_emp, splits, own_emp // splits, rows),
+        (NOCC // own_emp, lax.axis_index("tm") % splits, 0, 0),
+        (chips, 1, own_emp // splits, rows),
+    )
+    emp = lax.all_to_all(
+        emp_columns.reshape(chips, own_emp // splits, rows),
         "space",
         split_axis=0,
         concat_axis=0,
         axis_index_groups=[[2 * k + c for k in range(chips)] for c in range(2)],
     )
-    made = prepare(place, hold(scalars, occ_pair), tm, own_count, time_count, own_occ, own_emp)
-    occ_blocks, offsets, (tables, weights), emp_own = gather_ring(occ_pair, chips, made, emp_own)
-    emp_other = lax.ppermute(emp_own, "space", swap)
+
+    tables = class_tables(hold(jnp.zeros((1,), jnp.int32), occ_pair))
+    emp_parts = []
+    ahead, back = ring_steps(chips)
+    found, offsets = [occ_pair], [0]
+    from_left = from_right = occ_pair
+    for hop in range(1, chips // 2 + 1):
+        if hop == 2:
+            from_left, from_right, emp, tables = lax.optimization_barrier((from_left, from_right, emp, tables))
+            emp_parts += [emp, lax.ppermute(emp, "space", swap)]
+            traded = lax.ppermute(emp, "tm", [(0, 1), (1, 0)]) if splits > 1 else None
+        elif hop == 3:
+            from_left, from_right, traded = lax.optimization_barrier((from_left, from_right, traded))
+            if splits > 1:
+                emp_parts += [traded, lax.ppermute(traded, "space", swap)]
+            weights = all_pair_weights(
+                place, hold(scalars, (from_left, from_right)), tm, own_count, time_count, own_occ, own_emp
+            )
+        elif hop == 4:
+            from_left, from_right, weights = lax.optimization_barrier((from_left, from_right, weights))
+        elif hop > 4:
+            from_left, from_right = lax.optimization_barrier((from_left, from_right))
+        from_left = lax.ppermute(from_left, "space", ahead)
+        found.append(from_left)
+        offsets.append(-hop)
+        if 2 * hop < chips:
+            from_right = lax.ppermute(from_right, "space", back)
+            found.append(from_right)
+            offsets.append(hop)
 
     results = []
     part_rows = NG // space
     for w in range(own_count):
         keep_far, send_far, keep_near, send_near = pair_moment(
-            place, weights[w], occ_blocks, offsets, emp_own, emp_other, tables
+            place, weights[w], found, offsets, emp_parts, tables
         )
         far_total = keep_far + lax.ppermute(send_far, "space", swap).astype(jnp.float32)
         near_total = keep_near + lax.ppermute(send_near, "space", swap).astype(jnp.float32)

time: 87.3 us -> 83.5 us (0.956)
  Pallas kernels: 25.4 us -> 23.6 us
  waiting for transfers between devices: 25.7 us -> 24.3 us
    ppermute x8 -> x10, waiting for transfers between devices: 11.8 us -> 9.07 us  [the longest x4 5.95 us: local(): from_left = lax.ppermute(from_left, 'space', ahead)]
    slice x1 -> x0, local copies, waits for them, and re-layouts: 1.88 us -> none  [local(): columns[NOCC:].reshape(chips, own_emp, rows)]
    pallas_call x2 -> x3, Pallas kernels: 25.4 us -> 23.6 us  [the longest x1 17.4 us: pair_moment(): pl.pallas_call(functools.partial(pair_kernel, offsets, splits), out_shape...]
    reshape x0 -> x1, local copies, waits for them, and re-layouts: none -> 1.64 us  [local(): emp_columns.reshape(chips, own_emp // splits, rows)]
    ppermute x1, waiting for transfers between devices: 0.01 us -> 1.23 us  [local(): occ_pair = jnp.stack([occ_mine, lax.ppermute(occ_theirs, 'space', swap)])]
    ppermute x1, starting transfers between devices: 1.49 us -> 0.53 us  [local(): lax.ppermute(times, 'tm', [((d + hop) % tm, d) for d in range(tm)])]
    ppermute x8 -> x10, starting transfers between devices: 8.94 us -> 9.26 us  [the longest x4 4.65 us: local(): from_left = lax.ppermute(from_left, 'space', ahead)]
  transfers between devices with their start and end apart: 20 -> 22, of which waited for: 11 -> 14; matrix products, arithmetic and copies ran while one was open for 6% -> 7% of each run, Pallas kernels for 6% -> 7%
where the time goes in v4:
time: 83.5 us; the launch traced here: 83.1 us
  starting transfers between devices  25.5 us (31%)
  waiting for transfers between devices  24.3 us (29%)
  Pallas kernels  23.6 us (28%)
  other arithmetic  4.62 us (6%)
  local copies, waits for them, and re-layouts  4.23 us (5%)
  between operations  0.89 us (1%)
    pallas_call x1, Pallas kernels, pair_moment(): pl.pallas_call(functools.partial(pair_kernel, offsets, splits), out_shape...  17.4 us
    ppermute x4, waiting for transfers between devices, reduce_ring(): lax.ppermute(from_left.astype(jnp.bfloat16), 'space', ahead)  9.76 us
    all_to_all x1, starting transfers between devices, local(): lax.all_to_all(emp_columns.reshape(chips, own_emp // splits, rows), 'spac...  7.28 us
    ppermute x4, starting transfers between devices, reduce_ring(): lax.ppermute(from_left.astype(jnp.bfloat16), 'space', ahead)  6.18 us
    ppermute x4, waiting for transfers between devices, local(): from_left = lax.ppermute(from_left, 'space', ahead)  5.95 us
    pallas_call x1, Pallas kernels, class_tables(): pl.pallas_call(table_kernel, grid=(4,), out_shape=jax.ShapeDtypeStruct((4...  4.79 us
    ppermute x4, starting transfers between devices, local(): from_left = lax.ppermute(from_left, 'space', ahead)  4.65 us
    ppermute x3, waiting for transfers between devices, local(): from_right = lax.ppermute(from_right, 'space', back)  3.12 us
  transfers between devices with their start and end apart: 22, of which 14 were waited for; matrix products, arithmetic and copies ran while one was open for 7% of the time, Pallas kernels for 7%

profile of v4, /device:TPU:0, one launch (start us, length us, event | category | flops | bytes accessed | tf_op | source)
XLA Modules:
  0.0 83.1 jit_solution(2008202367449139591)
XLA Ops:
  0.0 1.6 %dynamic-slice_bitcast_fusion = bf16[8,16,864]{2,1,0:T(8,128)(2,1)} fusion(bf16[10,2,16,864]{3,2,1,0:T(8,128)(2,1)} %bitcast.17, s32[]{:T(128)S(6)} %select_n.25), kind=kLoop, calls=%fused_computation.2 | loop fusion | bytes 442372 | tf_op jit(solution)/shard_map/reshape | solution.py:389
  1.6 7.3 %all-to-all-start = ((bf16[8,16,864]{2,1,0:T(8,128)(2,1)}), bf16[8,16,864]{2,1,0:T(8,128)(2,1)S(1)}, u32[]{:S(2)}, u32[]{:S(2)}) async-start(bf16[8,16,864]{2,1,0:T(8,128)(2,1)} %dynamic-slice_bitcast_fusion), calls=%async_computation | async-start | bytes 458752 | tf_op jit(solution)/shard_map/all_to_all | solution.py:388
  8.9 0.9 %slice.42 = bf16[64,864]{1,0:T(8,128)(2,1)S(1)} slice(bf16[320,864]{1,0:T(8,128)(2,1)} %bitcast.18), slice={[0:64], [0:864]} | slice | bytes 221184 | tf_op jit(solution)/shard_map/slice | solution.py:378
  9.9 0.1 collective-permute-start
  10.0 1.2 %collective-permute-done = bf16[32,864]{1,0:T(8,128)(2,1)S(1)} collective-permute-done((bf16[32,864]{1,0:T(8,128)(2,1)S(1)}, bf16[32,864]{1,0:T(8,128)(2,1)S(1)}, u32[]{:S(2)}, u32[]{:S(2)}) %collective-permute-start) | collective-permute-done | bytes 55328 | tf_op jit(solution)/shard_map/ppermute | solution.py:381
  11.2 0.0 copy-start.1
  11.2 0.0 copy-start.13
  11.2 0.0 copy-start.2
  11.2 2.1 %collective-permute-start.2 = (bf16[2,32,864]{2,1,0:T(8,128)(2,1)S(1)}, bf16[2,32,864]{2,1,0:T(8,128)(2,1)S(1)}, u32[]{:S(2)}, u32[]{:S(2)}) collective-permute-start(bf16[2,32,864]{2,1,0:T(8,128)(2,1)S(1)} %pad_maximum_fusion.refs_4_), channel_id=1, source_target_pairs={{4,0},{5,1},{8,4},{9,5},{12,8},{13,9},{14,12},{15,13},{10,14},{11,... | collective-permute-start | bytes 331784 | tf_op jit(solution)/shard_map/ppermute | solution.py:421
  13.3 0.1 collective-permute-start.1
  13.4 4.8 %class_tables.1.refs_12_ = bf16[4,3584,256]{2,1,0:T(8,128)(2,1)} custom-call(s32[1]{0:T(128)} %constant.37.clone.1.held_ref), custom_call_target="tpu_custom_call" | custom-call | flops 58720256 | bytes 7340032 | tf_op jit(solution)/shard_map/class_tables/pallas_call | solution.py:103
  18.2 0.0 copy-done.1
  18.2 0.0 collective-permute-done.2.refs_6_
  18.2 0.3 collective-permute-done.1.refs_5_
  18.6 0.0 all-to-all-done.refs_0_
  18.6 1.6 %collective-permute-start.5 = (bf16[8,16,864]{2,1,0:T(8,128)(2,1)S(1)}, bf16[8,16,864]{2,1,0:T(8,128)(2,1)S(1)}, u32[]{:S(2)}, u32[]{:S(2)}) collective-permute-start(bf16[8,16,864]{2,1,0:T(8,128)(2,1)S(1)} %all-to-all-done.refs_0_), channel_id=1, source_target_pairs={{0,16},{16,0},{1,17},{17,1},{2,18},{18,2},{3,19},{19,3},{4,20},{20... | collective-permute-start | bytes 663560 | tf_op jit(solution)/shard_map/ppermute | solution.py:405
  20.1 0.5 collective-permute-start.8
  21.4 0.0 copy-done.13
  21.4 0.1 reshape.15
  21.4 1.6 %collective-permute-start.3 = (bf16[2,32,864]{2,1,0:T(8,128)(2,1)S(1)}, bf16[2,32,864]{2,1,0:T(8,128)(2,1)S(1)}, u32[]{:S(2)}, u32[]{:S(2)}) collective-permute-start(bf16[2,32,864]{2,1,0:T(8,128)(2,1)S(1)} %collective-permute-done.1.refs_5_), channel_id=1, source_target_pairs={{0,4},{1,5},{4,8},{5,9},{8,12},{9,13},{12,14},{13,15},{14,10},{15,... | collective-permute-start | bytes 331784 | tf_op jit(solution)/shard_map/ppermute | solution.py:417
  23.1 0.4 collective-permute-start.4
  23.5 0.6 pad_add_fusion.place_ref
  24.1 0.0 collective-permute-start.9
  24.1 2.2 %collective-permute-done.3.refs_7_ = bf16[2,32,864]{2,1,0:T(8,128)(2,1)S(1)} collective-permute-done((bf16[2,32,864]{2,1,0:T(8,128)(2,1)S(1)}, bf16[2,32,864]{2,1,0:T(8,128)(2,1)S(1)}, u32[]{:S(2)}, u32[]{:S(2)}) %collective-permute-start.3) | collective-permute-done | bytes 110624 | tf_op jit(solution)/shard_map/ppermute | solution.py:417
  26.2 1.6 %collective-permute-done.4.refs_8_ = bf16[2,32,864]{2,1,0:T(8,128)(2,1)S(1)} collective-permute-done((bf16[2,32,864]{2,1,0:T(8,128)(2,1)S(1)}, bf16[2,32,864]{2,1,0:T(8,128)(2,1)S(1)}, u32[]{:S(2)}, u32[]{:S(2)}) %collective-permute-start.4) | collective-permute-done | bytes 110624 | tf_op jit(solution)/shard_map/ppermute | solution.py:421
  27.8 0.0 collective-permute-done.5.refs_2_
  27.9 1.5 %collective-permute-start.6 = (bf16[2,32,864]{2,1,0:T(8,128)(2,1)S(1)}, bf16[2,32,864]{2,1,0:T(8,128)(2,1)S(1)}, u32[]{:S(2)}, u32[]{:S(2)}) collective-permute-start(bf16[2,32,864]{2,1,0:T(8,128)(2,1)S(1)} %collective-permute-done.3.refs_7_), channel_id=1, source_target_pairs={{0,4},{1,5},{4,8},{5,9},{8,12},{9,13},{12,14},{13,15},{14,10},{15,... | collective-permute-start | bytes 331784 | tf_op jit(solution)/shard_map/ppermute | solution.py:417
  29.4 0.6 collective-permute-start.7
  29.9 0.0 collective-permute-start.10
  29.9 0.0 collective-permute-done.8
  29.9 0.0 copy-done.2
  29.9 1.3 %pad_maximum_fusion.1.scalar_ref = f32[326]{0:T(512)} fusion(f32[4]{0:T(128)S(1)} %reshape.15, f32[1]{0:T(128)} %collective-permute-done.8, f32[1]{0:T(128)S(6)} %copy.8, f32[320]{0:T(512)S(1)} %copy-done.2), kind=kLoop, calls=%fused_computation.18 | loop fusion | flops 978 | bytes 2608 | tf_op jit(solution)/shard_map/concatenate | solution.py:375
  31.2 1.3 %pair_weights.1 = f32[1,8,128]{2,1,0:T(8,128)} custom-call(s32[2]{0:T(128)} %pad_add_fusion.place_ref, f32[326]{0:T(512)} %pad_maximum_fusion.1.scalar_ref), custom_call_target="tpu_custom_call" | custom-call | flops 16777216 | bytes 1048576 | tf_op jit(solution)/shard_map/pair_weights/pallas_call | solution.py:120
  32.6 0.1 collective-permute-done.6.refs_9_
  32.7 1.5 %collective-permute-done.7.refs_10_ = bf16[2,32,864]{2,1,0:T(8,128)(2,1)S(1)} collective-permute-done((bf16[2,32,864]{2,1,0:T(8,128)(2,1)S(1)}, bf16[2,32,864]{2,1,0:T(8,128)(2,1)S(1)}, u32[]{:S(2)}, u32[]{:S(2)}) %collective-permute-start.7) | collective-permute-done | bytes 110624 | tf_op jit(solution)/shard_map/ppermute | solution.py:421
  34.2 1.5 %collective-permute-start.11 = (bf16[2,32,864]{2,1,0:T(8,128)(2,1)S(1)}, bf16[2,32,864]{2,1,0:T(8,128)(2,1)S(1)}, u32[]{:S(2)}, u32[]{:S(2)}) collective-permute-start(bf16[2,32,864]{2,1,0:T(8,128)(2,1)S(1)} %collective-permute-done.6.refs_9_), channel_id=1, source_target_pairs={{0,4},{1,5},{4,8},{5,9},{8,12},{9,13},{12,14},{13,15},{14,10},{15,... | collective-permute-start | bytes 331784 | tf_op jit(solution)/shard_map/ppermute | solution.py:417
  35.6 0.0 collective-permute-done.9.refs_1_
  35.6 3.3 %collective-permute-done.11.refs_11_ = bf16[2,32,864]{2,1,0:T(8,128)(2,1)S(1)} collective-permute-done((bf16[2,32,864]{2,1,0:T(8,128)(2,1)S(1)}, bf16[2,32,864]{2,1,0:T(8,128)(2,1)S(1)}, u32[]{:S(2)}, u32[]{:S(2)}) %collective-permute-start.11) | collective-permute-done | bytes 110624 | tf_op jit(solution)/shard_map/ppermute | solution.py:417
  39.0 0.0 collective-permute-done.10.refs_3_
  39.0 0.6 copy-done.12
  39.6 0.1 copy-done.5
  39.7 17.4 %pair_moment.1 = (f32[128,896]{1,0:T(8,128)}, bf16[128,896]{1,0:T(8,128)(2,1)}, f32[384,896]{1,0:T(8,128)}, bf16[384,896]{1,0:T(8,128)(2,1)}) custom-call(s32[2]{0:T(128)} %pad_add_fusion.place_ref, f32[8,128]{1,0:T(8,128)} %bitcast.20, bf16[8,16,864]{2,1,0:T(8,128)(2,1)} %copy-done, bf16[8,16,864]{2,1,0:T(8,128)(2,1)} %copy-done.4, ...), custom_call_target="tpu_custom_call" | custom-call | flops 7516192768 | bytes 16777216 | tf_op jit(solution)/shard_map/pair_moment/pallas_call | solution.py:311
  57.1 0.1 collective-permute-start.13
  57.2 0.5 collective-permute-start.12
  57.7 1.2 %collective-permute-done.13 = bf16[128,896]{1,0:T(8,128)(2,1)S(1)} collective-permute-done((bf16[128,896]{1,0:T(8,128)(2,1)}, bf16[128,896]{1,0:T(8,128)(2,1)S(1)}, u32[]{:S(2)}, u32[]{:S(2)}) %collective-permute-start.13) | collective-permute-done | bytes 229408 | tf_op jit(solution)/shard_map/ppermute | solution.py:431
  58.9 1.1 %add_convert_fusion = bf16[128,896]{1,0:T(8,128)(2,1)S(1)} fusion(f32[128,896]{1,0:T(8,128)} %get-tuple-element.33, bf16[128,896]{1,0:T(8,128)(2,1)S(1)} %collective-permute-done.13), kind=kLoop, calls=%fused_computation.1 | loop fusion | flops 344064 | bytes 917504 | tf_op jit(solution)/shard_map/convert.1
  60.0 1.5 %collective-permute-start.14 = (bf16[54,896]{1,0:T(8,128)(2,1)S(1)}, bf16[54,896]{1,0:T(8,128)(2,1)S(1)}, u32[]{:S(2)}, u32[]{:S(2)}) collective-permute-start(bf16[54,896]{1,0:T(8,128)(2,1)S(1)} %get-tuple-element.40), channel_id=1, source_target_pairs={{0,4},{1,5},{4,8},{5,9},{8,12},{9,13},{12,14},{13,15},{14,10},{15,... | collective-permute-start | bytes 290312 | tf_op jit(solution)/shard_map/ppermute | solution.py:353
  61.5 0.6 collective-permute-start.18
  62.0 0.0 collective-permute-done.12
  62.1 1.5 %convert_add_fusion = f32[384,896]{1,0:T(8,128)S(1)} fusion(f32[384,896]{1,0:T(8,128)} %get-tuple-element.31, bf16[384,896]{1,0:T(8,128)(2,1)S(1)} %collective-permute-done.12), kind=kLoop, calls=%fused_computation | loop fusion | flops 688128 | bytes 3440640 | tf_op jit(solution)/shard_map/add | solution.py:432
  63.5 1.4 %collective-permute-done.14 = bf16[54,896]{1,0:T(8,128)(2,1)S(1)} collective-permute-done((bf16[54,896]{1,0:T(8,128)(2,1)S(1)}, bf16[54,896]{1,0:T(8,128)(2,1)S(1)}, u32[]{:S(2)}, u32[]{:S(2)}) %collective-permute-start.14) | collective-permute-done | bytes 96800 | tf_op jit(solution)/shard_map/ppermute | solution.py:353
  64.9 1.5 %collective-permute-start.15 = (bf16[54,896]{1,0:T(8,128)(2,1)S(1)}, bf16[54,896]{1,0:T(8,128)(2,1)S(1)}, u32[]{:S(2)}, u32[]{:S(2)}) collective-permute-start(bf16[54,896]{1,0:T(8,128)(2,1)S(1)} %fusion.6), channel_id=1, source_target_pairs={{0,4},{1,5},{4,8},{5,9},{8,12},{9,13},{12,14},{13,15},{14,10},{15,... | collective-permute-start | bytes 290312 | tf_op jit(solution)/shard_map/ppermute | solution.py:353
  66.4 0.0 collective-permute-done.18
  66.4 3.2 %collective-permute-done.15 = bf16[54,896]{1,0:T(8,128)(2,1)S(1)} collective-permute-done((bf16[54,896]{1,0:T(8,128)(2,1)S(1)}, bf16[54,896]{1,0:T(8,128)(2,1)S(1)}, u32[]{:S(2)}, u32[]{:S(2)}) %collective-permute-start.15) | collective-permute-done | bytes 96800 | tf_op jit(solution)/shard_map/ppermute | solution.py:353
  69.7 1.5 %collective-permute-start.16 = (bf16[54,896]{1,0:T(8,128)(2,1)S(1)}, bf16[54,896]{1,0:T(8,128)(2,1)S(1)}, u32[]{:S(2)}, u32[]{:S(2)}) collective-permute-start(bf16[54,896]{1,0:T(8,128)(2,1)S(1)} %get-tuple-element.38), channel_id=1, source_target_pairs={{0,4},{1,5},{4,8},{5,9},{8,12},{9,13},{12,14},{13,15},{14,10},{15,... | collective-permute-start | bytes 290312 | tf_op jit(solution)/shard_map/ppermute | solution.py:353
  71.2 0.6 collective-permute-start.19
  71.7 2.6 %collective-permute-done.16 = bf16[54,896]{1,0:T(8,128)(2,1)S(1)} collective-permute-done((bf16[54,896]{1,0:T(8,128)(2,1)S(1)}, bf16[54,896]{1,0:T(8,128)(2,1)S(1)}, u32[]{:S(2)}, u32[]{:S(2)}) %collective-permute-start.16) | collective-permute-done | bytes 96800 | tf_op jit(solution)/shard_map/ppermute | solution.py:353
  74.4 1.5 %collective-permute-done.19 = bf16[54,896]{1,0:T(8,128)(2,1)S(1)} collective-permute-done((bf16[54,896]{1,0:T(8,128)(2,1)S(1)}, bf16[54,896]{1,0:T(8,128)(2,1)S(1)}, u32[]{:S(2)}, u32[]{:S(2)}) %collective-permute-start.19) | collective-permute-done | bytes 96800 | tf_op jit(solution)/shard_map/ppermute | solution.py:355
  75.8 0.1 fusion.4
  75.9 1.6 %collective-permute-start.17 = (bf16[54,896]{1,0:T(8,128)(2,1)S(1)}, bf16[54,896]{1,0:T(8,128)(2,1)S(1)}, u32[]{:S(2)}, u32[]{:S(2)}) collective-permute-start(bf16[54,896]{1,0:T(8,128)(2,1)S(1)} %get-tuple-element.35), channel_id=1, source_target_pairs={{0,4},{1,5},{4,8},{5,9},{8,12},{9,13},{12,14},{13,15},{14,10},{15,... | collective-permute-start | bytes 290312 | tf_op jit(solution)/shard_map/ppermute | solution.py:353
  77.5 0.4 collective-permute-start.20
  78.0 2.6 %collective-permute-done.17 = bf16[54,896]{1,0:T(8,128)(2,1)S(1)} collective-permute-done((bf16[54,896]{1,0:T(8,128)(2,1)S(1)}, bf16[54,896]{1,0:T(8,128)(2,1)S(1)}, u32[]{:S(2)}, u32[]{:S(2)}) %collective-permute-start.17) | collective-permute-done | bytes 96800 | tf_op jit(solution)/shard_map/ppermute | solution.py:353
  80.6 1.6 %collective-permute-done.20 = bf16[54,896]{1,0:T(8,128)(2,1)S(1)} collective-permute-done((bf16[54,896]{1,0:T(8,128)(2,1)S(1)}, bf16[54,896]{1,0:T(8,128)(2,1)S(1)}, u32[]{:S(2)}, u32[]{:S(2)}) %collective-permute-start.20) | collective-permute-done | bytes 96800 | tf_op jit(solution)/shard_map/ppermute | solution.py:355
  82.2 0.9 %copy.6 = f32[1,54,864]{2,0,1:T(1,128)} copy(f32[1,54,864]{2,1,0:T(8,128)S(1)} %fusion.1) | data formatting | bytes 373248 | tf_op jit(solution)/shard_map/stack | solution.py:441
  (26 shorter events, 0.2 us)
Async XLA Ops:
  1.6 16.9 %all-to-all-start = ((bf16[8,16,864]{2,1,0:T(8,128)(2,1)}), bf16[8,16,864]{2,1,0:T(8,128)(2,1)S(1)}, u32[]{:S(2)}, u32[]{:S(2)}) async-start(bf16[8,16,864]{2,1,0:T(8,128)(2,1)} %dynamic-slice_bitcast_fusion), calls=%async_computation | async-start | bytes 458752 | tf_op jit(solution)/shard_map/all_to_all | solution.py:388
  9.9 1.3 %collective-permute-start = (bf16[32,864]{1,0:T(8,128)(2,1)S(1)}, bf16[32,864]{1,0:T(8,128)(2,1)S(1)}, u32[]{:S(2)}, u32[]{:S(2)}) collective-permute-start(bf16[32,864]{1,0:T(8,128)(2,1)S(1)} %get-tuple-element.43), channel_id=1, source_target_pairs={{0,1},{1,0},{2,3},{3,2},{4,5},{5,4},{6,7},{7,6},{8,9},{9,8},{10,11... | collective-permute-start | bytes 165896 | tf_op jit(solution)/shard_map/ppermute | solution.py:381
  11.2 7.0 %copy-start.1 = (bf16[2,32,864]{2,1,0:T(8,128)(2,1)}, bf16[2,32,864]{2,1,0:T(8,128)(2,1)S(1)}, u32[]{:S(2)}) copy-start(bf16[2,32,864]{2,1,0:T(8,128)(2,1)S(1)} %pad_maximum_fusion.refs_4_) | copy-start | bytes 331780
  11.2 10.1 %copy-start.13 = (f32[2,2]{1,0:T(2,128)S(1)}, f32[2,2]{1,0:T(2,128)}, u32[]{:S(2)}) copy-start(f32[2,2]{1,0:T(2,128)} %param.7) | copy-start | bytes 52
  11.2 18.7 %copy-start.2 = (f32[320]{0:T(512)S(1)}, f32[320]{0:T(512)}, u32[]{:S(2)}) copy-start(f32[320]{0:T(512)} %param.5) | copy-start | bytes 3844
  11.2 7.0 %collective-permute-start.2 = (bf16[2,32,864]{2,1,0:T(8,128)(2,1)S(1)}, bf16[2,32,864]{2,1,0:T(8,128)(2,1)S(1)}, u32[]{:S(2)}, u32[]{:S(2)}) collective-permute-start(bf16[2,32,864]{2,1,0:T(8,128)(2,1)S(1)} %pad_maximum_fusion.refs_4_), channel_id=1, source_target_pairs={{4,0},{5,1},{8,4},{9,5},{12,8},{13,9},{14,12},{15,13},{10,14},{11,... | collective-permute-start | bytes 331784 | tf_op jit(solution)/shard_map/ppermute | solution.py:421
  13.3 5.3 %collective-permute-start.1 = (bf16[2,32,864]{2,1,0:T(8,128)(2,1)S(1)}, bf16[2,32,864]{2,1,0:T(8,128)(2,1)S(1)}, u32[]{:S(2)}, u32[]{:S(2)}) collective-permute-start(bf16[2,32,864]{2,1,0:T(8,128)(2,1)S(1)} %pad_maximum_fusion.refs_4_), channel_id=1, source_target_pairs={{0,4},{1,5},{4,8},{5,9},{8,12},{9,13},{12,14},{13,15},{14,10},{15,... | collective-permute-start | bytes 331784 | tf_op jit(solution)/shard_map/ppermute | solution.py:417
  18.2 20.7 %copy-start.6 = (bf16[2,32,864]{2,1,0:T(8,128)(2,1)}, bf16[2,32,864]{2,1,0:T(8,128)(2,1)S(1)}, u32[]{:S(2)}) copy-start(bf16[2,32,864]{2,1,0:T(8,128)(2,1)S(1)} %collective-permute-done.2.refs_6_) | copy-start | bytes 331780
  18.6 20.4 %copy-start.7 = (bf16[2,32,864]{2,1,0:T(8,128)(2,1)}, bf16[2,32,864]{2,1,0:T(8,128)(2,1)S(1)}, u32[]{:S(2)}) copy-start(bf16[2,32,864]{2,1,0:T(8,128)(2,1)S(1)} %collective-permute-done.1.refs_5_) | copy-start | bytes 331780
  18.6 20.4 %copy-start = (bf16[8,16,864]{2,1,0:T(8,128)(2,1)}, bf16[8,16,864]{2,1,0:T(8,128)(2,1)S(1)}, u32[]{:S(2)}) copy-start(bf16[8,16,864]{2,1,0:T(8,128)(2,1)S(1)} %all-to-all-done.refs_0_) | copy-start | bytes 663556
  18.6 9.3 %collective-permute-start.5 = (bf16[8,16,864]{2,1,0:T(8,128)(2,1)S(1)}, bf16[8,16,864]{2,1,0:T(8,128)(2,1)S(1)}, u32[]{:S(2)}, u32[]{:S(2)}) collective-permute-start(bf16[8,16,864]{2,1,0:T(8,128)(2,1)S(1)} %all-to-all-done.refs_0_), channel_id=1, source_target_pairs={{0,16},{16,0},{1,17},{17,1},{2,18},{18,2},{3,19},{19,3},{4,20},{20... | collective-permute-start | bytes 663560 | tf_op jit(solution)/shard_map/ppermute | solution.py:405
  20.1 9.8 %collective-permute-start.8 = (f32[1]{0:T(128)}, f32[1]{0:T(128)}, u32[]{:S(2)}, u32[]{:S(2)}) collective-permute-start(f32[1]{0:T(128)} %param.6), channel_id=1, source_target_pairs={{16,0},{0,16},{17,1},{1,17},{18,2},{2,18},{19,3},{3,19},{20,4},{4,... | collective-permute-start | bytes 20 | tf_op jit(solution)/shard_map/ppermute | solution.py:373
  21.4 4.8 %collective-permute-start.3 = (bf16[2,32,864]{2,1,0:T(8,128)(2,1)S(1)}, bf16[2,32,864]{2,1,0:T(8,128)(2,1)S(1)}, u32[]{:S(2)}, u32[]{:S(2)}) collective-permute-start(bf16[2,32,864]{2,1,0:T(8,128)(2,1)S(1)} %collective-permute-done.1.refs_5_), channel_id=1, source_target_pairs={{0,4},{1,5},{4,8},{5,9},{8,12},{9,13},{12,14},{13,15},{14,10},{15,... | collective-permute-start | bytes 331784 | tf_op jit(solution)/shard_map/ppermute | solution.py:417
  23.1 4.8 %collective-permute-start.4 = (bf16[2,32,864]{2,1,0:T(8,128)(2,1)S(1)}, bf16[2,32,864]{2,1,0:T(8,128)(2,1)S(1)}, u32[]{:S(2)}, u32[]{:S(2)}) collective-permute-start(bf16[2,32,864]{2,1,0:T(8,128)(2,1)S(1)} %collective-permute-done.2.refs_6_), channel_id=1, source_target_pairs={{4,0},{5,1},{8,4},{9,5},{12,8},{13,9},{14,12},{15,13},{10,14},{11,... | collective-permute-start | bytes 331784 | tf_op jit(solution)/shard_map/ppermute | solution.py:421
  24.1 11.6 %collective-permute-start.9 = (bf16[8,16,864]{2,1,0:T(8,128)(2,1)S(1)}, bf16[8,16,864]{2,1,0:T(8,128)(2,1)S(1)}, u32[]{:S(2)}, u32[]{:S(2)}) collective-permute-start(bf16[8,16,864]{2,1,0:T(8,128)(2,1)S(1)} %all-to-all-done.refs_0_), channel_id=1, source_target_pairs={{0,1},{1,0},{2,3},{3,2},{4,5},{5,4},{6,7},{7,6},{8,9},{9,8},{10,11... | collective-permute-start | bytes 663560 | tf_op jit(solution)/shard_map/ppermute | solution.py:404
  26.2 12.8 %copy-start.8 = (bf16[2,32,864]{2,1,0:T(8,128)(2,1)}, bf16[2,32,864]{2,1,0:T(8,128)(2,1)S(1)}, u32[]{:S(2)}) copy-start(bf16[2,32,864]{2,1,0:T(8,128)(2,1)S(1)} %collective-permute-done.3.refs_7_) | copy-start | bytes 331780
  27.8 11.2 %copy-start.9 = (bf16[2,32,864]{2,1,0:T(8,128)(2,1)}, bf16[2,32,864]{2,1,0:T(8,128)(2,1)S(1)}, u32[]{:S(2)}) copy-start(bf16[2,32,864]{2,1,0:T(8,128)(2,1)S(1)} %collective-permute-done.4.refs_8_) | copy-start | bytes 331780
  27.9 11.2 %copy-start.3 = (bf16[8,16,864]{2,1,0:T(8,128)(2,1)}, bf16[8,16,864]{2,1,0:T(8,128)(2,1)S(1)}, u32[]{:S(2)}) copy-start(bf16[8,16,864]{2,1,0:T(8,128)(2,1)S(1)} %collective-permute-done.5.refs_2_) | copy-start | bytes 663556
  27.9 4.8 %collective-permute-start.6 = (bf16[2,32,864]{2,1,0:T(8,128)(2,1)S(1)}, bf16[2,32,864]{2,1,0:T(8,128)(2,1)S(1)}, u32[]{:S(2)}, u32[]{:S(2)}) collective-permute-start(bf16[2,32,864]{2,1,0:T(8,128)(2,1)S(1)} %collective-permute-done.3.refs_7_), channel_id=1, source_target_pairs={{0,4},{1,5},{4,8},{5,9},{8,12},{9,13},{12,14},{13,15},{14,10},{15,... | collective-permute-start | bytes 331784 | tf_op jit(solution)/shard_map/ppermute | solution.py:417
  29.4 4.8 %collective-permute-start.7 = (bf16[2,32,864]{2,1,0:T(8,128)(2,1)S(1)}, bf16[2,32,864]{2,1,0:T(8,128)(2,1)S(1)}, u32[]{:S(2)}, u32[]{:S(2)}) collective-permute-start(bf16[2,32,864]{2,1,0:T(8,128)(2,1)S(1)} %collective-permute-done.4.refs_8_), channel_id=1, source_target_pairs={{4,0},{5,1},{8,4},{9,5},{12,8},{13,9},{14,12},{15,13},{10,14},{11,... | collective-permute-start | bytes 331784 | tf_op jit(solution)/shard_map/ppermute | solution.py:421
  29.9 9.0 %collective-permute-start.10 = (bf16[8,16,864]{2,1,0:T(8,128)(2,1)S(1)}, bf16[8,16,864]{2,1,0:T(8,128)(2,1)S(1)}, u32[]{:S(2)}, u32[]{:S(2)}) collective-permute-start(bf16[8,16,864]{2,1,0:T(8,128)(2,1)S(1)} %collective-permute-done.5.refs_2_), channel_id=1, source_target_pairs={{0,1},{1,0},{2,3},{3,2},{4,5},{5,4},{6,7},{7,6},{8,9},{9,8},{10,11... | collective-permute-start | bytes 663560 | tf_op jit(solution)/shard_map/ppermute | solution.py:409
  32.7 6.3 %copy-start.10 = (bf16[2,32,864]{2,1,0:T(8,128)(2,1)}, bf16[2,32,864]{2,1,0:T(8,128)(2,1)S(1)}, u32[]{:S(2)}) copy-start(bf16[2,32,864]{2,1,0:T(8,128)(2,1)S(1)} %collective-permute-done.6.refs_9_) | copy-start | bytes 331780
  34.2 4.9 %copy-start.11 = (bf16[2,32,864]{2,1,0:T(8,128)(2,1)}, bf16[2,32,864]{2,1,0:T(8,128)(2,1)S(1)}, u32[]{:S(2)}) copy-start(bf16[2,32,864]{2,1,0:T(8,128)(2,1)S(1)} %collective-permute-done.7.refs_10_) | copy-start | bytes 331780
  34.2 4.8 %collective-permute-start.11 = (bf16[2,32,864]{2,1,0:T(8,128)(2,1)S(1)}, bf16[2,32,864]{2,1,0:T(8,128)(2,1)S(1)}, u32[]{:S(2)}, u32[]{:S(2)}) collective-permute-start(bf16[2,32,864]{2,1,0:T(8,128)(2,1)S(1)} %collective-permute-done.6.refs_9_), channel_id=1, source_target_pairs={{0,4},{1,5},{4,8},{5,9},{8,12},{9,13},{12,14},{13,15},{14,10},{15,... | collective-permute-start | bytes 331784 | tf_op jit(solution)/shard_map/ppermute | solution.py:417
  35.6 3.4 %copy-start.4 = (bf16[8,16,864]{2,1,0:T(8,128)(2,1)}, bf16[8,16,864]{2,1,0:T(8,128)(2,1)S(1)}, u32[]{:S(2)}) copy-start(bf16[8,16,864]{2,1,0:T(8,128)(2,1)S(1)} %collective-permute-done.9.refs_1_) | copy-start | bytes 663556
  39.0 0.7 copy-start.12
  39.0 0.7 copy-start.5
  57.1 1.8 %collective-permute-start.13 = (bf16[128,896]{1,0:T(8,128)(2,1)}, bf16[128,896]{1,0:T(8,128)(2,1)S(1)}, u32[]{:S(2)}, u32[]{:S(2)}) collective-permute-start(bf16[128,896]{1,0:T(8,128)(2,1)} %get-tuple-element.34), channel_id=1, source_target_pairs={{0,1},{1,0},{2,3},{3,2},{4,5},{5,4},{6,7},{7,6},{8,9},{9,8},{10,11... | collective-permute-start | bytes 688136 | tf_op jit(solution)/shard_map/ppermute | solution.py:431
  57.2 4.9 %collective-permute-start.12 = (bf16[384,896]{1,0:T(8,128)(2,1)}, bf16[384,896]{1,0:T(8,128)(2,1)S(1)}, u32[]{:S(2)}, u32[]{:S(2)}) collective-permute-start(bf16[384,896]{1,0:T(8,128)(2,1)} %get-tuple-element.32), channel_id=1, source_target_pairs={{0,1},{1,0},{2,3},{3,2},{4,5},{5,4},{6,7},{7,6},{8,9},{9,8},{10,11... | collective-permute-start | bytes 2064392 | tf_op jit(solution)/shard_map/ppermute | solution.py:432
  60.0 4.9 %collective-permute-start.14 = (bf16[54,896]{1,0:T(8,128)(2,1)S(1)}, bf16[54,896]{1,0:T(8,128)(2,1)S(1)}, u32[]{:S(2)}, u32[]{:S(2)}) collective-permute-start(bf16[54,896]{1,0:T(8,128)(2,1)S(1)} %get-tuple-element.40), channel_id=1, source_target_pairs={{0,4},{1,5},{4,8},{5,9},{8,12},{9,13},{12,14},{13,15},{14,10},{15,... | collective-permute-start | bytes 290312 | tf_op jit(solution)/shard_map/ppermute | solution.py:353
  61.5 5.0 %collective-permute-start.18 = (bf16[54,896]{1,0:T(8,128)(2,1)S(1)}, bf16[54,896]{1,0:T(8,128)(2,1)S(1)}, u32[]{:S(2)}, u32[]{:S(2)}) collective-permute-start(bf16[54,896]{1,0:T(8,128)(2,1)S(1)} %get-tuple-element.41), channel_id=1, source_target_pairs={{4,0},{5,1},{8,4},{9,5},{12,8},{13,9},{14,12},{15,13},{10,14},{11,... | collective-permute-start | bytes 290312 | tf_op jit(solution)/shard_map/ppermute | solution.py:355
  64.9 4.7 %collective-permute-start.15 = (bf16[54,896]{1,0:T(8,128)(2,1)S(1)}, bf16[54,896]{1,0:T(8,128)(2,1)S(1)}, u32[]{:S(2)}, u32[]{:S(2)}) collective-permute-start(bf16[54,896]{1,0:T(8,128)(2,1)S(1)} %fusion.6), channel_id=1, source_target_pairs={{0,4},{1,5},{4,8},{5,9},{8,12},{9,13},{12,14},{13,15},{14,10},{15,... | collective-permute-start | bytes 290312 | tf_op jit(solution)/shard_map/ppermute | solution.py:353
  69.7 4.7 %collective-permute-start.16 = (bf16[54,896]{1,0:T(8,128)(2,1)S(1)}, bf16[54,896]{1,0:T(8,128)(2,1)S(1)}, u32[]{:S(2)}, u32[]{:S(2)}) collective-permute-start(bf16[54,896]{1,0:T(8,128)(2,1)S(1)} %get-tuple-element.38), channel_id=1, source_target_pairs={{0,4},{1,5},{4,8},{5,9},{8,12},{9,13},{12,14},{13,15},{14,10},{15,... | collective-permute-start | bytes 290312 | tf_op jit(solution)/shard_map/ppermute | solution.py:353
  71.2 4.6 %collective-permute-start.19 = (bf16[54,896]{1,0:T(8,128)(2,1)S(1)}, bf16[54,896]{1,0:T(8,128)(2,1)S(1)}, u32[]{:S(2)}, u32[]{:S(2)}) collective-permute-start(bf16[54,896]{1,0:T(8,128)(2,1)S(1)} %get-tuple-element.39), channel_id=1, source_target_pairs={{4,0},{5,1},{8,4},{9,5},{12,8},{13,9},{14,12},{15,13},{10,14},{11,... | collective-permute-start | bytes 290312 | tf_op jit(solution)/shard_map/ppermute | solution.py:355
  75.9 4.7 %collective-permute-start.17 = (bf16[54,896]{1,0:T(8,128)(2,1)S(1)}, bf16[54,896]{1,0:T(8,128)(2,1)S(1)}, u32[]{:S(2)}, u32[]{:S(2)}) collective-permute-start(bf16[54,896]{1,0:T(8,128)(2,1)S(1)} %get-tuple-element.35), channel_id=1, source_target_pairs={{0,4},{1,5},{4,8},{5,9},{8,12},{9,13},{12,14},{13,15},{14,10},{15,... | collective-permute-start | bytes 290312 | tf_op jit(solution)/shard_map/ppermute | solution.py:353
  77.5 4.6 %collective-permute-start.20 = (bf16[54,896]{1,0:T(8,128)(2,1)S(1)}, bf16[54,896]{1,0:T(8,128)(2,1)S(1)}, u32[]{:S(2)}, u32[]{:S(2)}) collective-permute-start(bf16[54,896]{1,0:T(8,128)(2,1)S(1)} %get-tuple-element.36), channel_id=1, source_target_pairs={{4,0},{5,1},{8,4},{9,5},{12,8},{13,9},{14,12},{15,13},{10,14},{11,... | collective-permute-start | bytes 290312 | tf_op jit(solution)/shard_map/ppermute | solution.py:355

commit v5 on v4

--- a/solution.py
+++ b/solution.py
@@ -153,8 +153,9 @@
     n_occ = occ_wide.shape[1]
     per_group = chips // steps
     plane = SIDE * SIDE // 2
-    half_emp = n_emp // 2
-    half_pairs = half_emp * n_occ
+    whole_rows = max(1, LANES // n_occ)
+    first_emp = max(1, 3 * n_emp // 8 // whole_rows) * whole_rows
+    emp_cuts = (slice(0, first_emp), slice(first_emp, n_emp))
 
     copy = pltpu.make_async_copy(table_hbm, table, table_sem)
     me = place_ref[0]
@@ -167,8 +168,7 @@
                 group = far * steps + step
                 first_chip = group * per_group // 2
                 shard_rows = [
-                    raw[first_chip + shard // 2, shard % 2, rows].astype(jnp.float32)
-                    for shard in range(per_group)
+                    raw[first_chip + shard // 2, shard % 2, rows] for shard in range(per_group)
                 ]
                 for upper in range(2):
                     pieces = []
@@ -180,7 +180,7 @@
                             count = min(stop - start, n_rows - offset)
                             pieces.append(shard_rows[shard][:, offset : offset + count])
                             start += count
-                    pieces.append(jnp.zeros((pieces[0].shape[0], depth - PLANES * plane), jnp.float32))
+                    pieces.append(jnp.zeros((pieces[0].shape[0], depth - PLANES * plane), raw.dtype))
                     lanes = slice(step * depth, (step + 1) * depth)
                     target[2 * far + upper, rows, lanes] = jnp.concatenate(pieces, axis=1).astype(target.dtype)
 
@@ -219,8 +219,8 @@
     )
 
     def build(half, target, cut):
-        emp_rows = [emp_wide[k, half * half_emp : (half + 1) * half_emp, cut] for k in range(4)]
-        for i in range(half_emp):
+        emp_rows = [emp_wide[k, emp_cuts[half], cut] for k in range(4)]
+        for i in range(emp_rows[0].shape[0]):
             emp_row = [
                 jnp.broadcast_to(emp_rows[k][i : i + 1], (16, LANES)).astype(jnp.bfloat16) for k in range(4)
             ]
@@ -247,8 +247,8 @@
         b_first = (b_odd + SIDE // 8) % 2
         for a_step in range(SIDE // 4):
             start = b_first * (SIDE // 2) + 2 * a_step + a_first
-            for tile in range(half_pairs // LANES):
-                rho[half * half_pairs // LANES + tile, pl.ds(start, per_a, stride=spacing), :] = found[
+            for tile in range(source.shape[1] // LANES):
+                rho[emp_cuts[half].start * n_occ // LANES + tile, pl.ds(start, per_a, stride=spacing), :] = found[
                     a_step * per_a : (a_step + 1) * per_a, tile * LANES : (tile + 1) * LANES
                 ]
 
@@ -268,8 +268,12 @@
         for k in range(4):
             multiply(1, second, k)
 
-    product = pltpu.VMEM((4, half_pairs, steps * depth), jnp.bfloat16)
-    pl.run_scoped(transform, product, product)
+    pl.run_scoped(
+        transform,
+        *(
+            pltpu.VMEM((4, (cut.stop - cut.start) * n_occ, steps * depth), jnp.bfloat16) for cut in emp_cuts
+        ),
+    )
 
     rows = NG // shards
 
@@ -369,10 +373,6 @@
     core = me % 2
     swap = [(d, d ^ 1) for d in range(space)]
 
-    every_time = [times] + [
-        lax.ppermute(times, "tm", [((d + hop) % tm, d) for d in range(tm)]) for hop in range(1, tm)
-    ]
-    scalars = jnp.concatenate([gaps] + every_time + [cos_weights.reshape(-1)])
     place = jnp.stack([me, lax.axis_index("tm")]).astype(jnp.int32)
 
     occ = columns[:NOCC].reshape(2, own_occ, rows)
@@ -407,11 +407,16 @@
             from_left, from_right, traded = lax.optimization_barrier((from_left, from_right, traded))
             if splits > 1:
                 emp_parts += [traded, lax.ppermute(traded, "space", swap)]
+            held_times = hold(times, (from_left, from_right))
+            every_time = [times] + [
+                lax.ppermute(held_times, "tm", [((d + step) % tm, d) for d in range(tm)]) for step in range(1, tm)
+            ]
+        elif hop == 4:
+            from_left, from_right, every_time = lax.optimization_barrier((from_left, from_right, every_time))
+            scalars = jnp.concatenate([gaps] + every_time + [cos_weights.reshape(-1)])
             weights = all_pair_weights(
                 place, hold(scalars, (from_left, from_right)), tm, own_count, time_count, own_occ, own_emp
             )
-        elif hop == 4:
-            from_left, from_right, weights = lax.optimization_barrier((from_left, from_right, weights))
         elif hop > 4:
             from_left, from_right = lax.optimization_barrier((from_left, from_right))
         from_left = lax.ppermute(from_left, "space", ahead)

time: 83.5 us -> 82.4 us (0.987)
  waiting for transfers between devices: 24.3 us -> 23.1 us
    ppermute x1, waiting for transfers between devices: 0.01 us -> 3.2 us  [local(): lax.ppermute(held_times, 'tm', [((d + step) % tm, d) for d in range(tm)])]
    ppermute x4, waiting for transfers between devices: 5.95 us -> 3.12 us  [local(): from_left = lax.ppermute(from_left, 'space', ahead)]
    ppermute x3, waiting for transfers between devices: 3.12 us -> 1.66 us  [local(): from_right = lax.ppermute(from_right, 'space', back)]
  transfers between devices with their start and end apart: 22 -> 22, of which waited for: 14 -> 13; matrix products, arithmetic and copies ran while one was open for 7% -> 7% of each run, Pallas kernels for 7% -> 7%
where the time goes in v5:
time: 82.4 us; the launch traced here: 81.9 us
  starting transfers between devices  25.6 us (31%)
  Pallas kernels  23.6 us (29%)
  waiting for transfers between devices  23.1 us (28%)
  other arithmetic  4.53 us (5%)
  local copies, waits for them, and re-layouts  4.23 us (5%)
  between operations  0.87 us (1%)
    pallas_call x1, Pallas kernels, pair_moment(): pl.pallas_call(functools.partial(pair_kernel, offsets, splits), out_shape...  17.5 us
    ppermute x4, waiting for transfers between devices, reduce_ring(): lax.ppermute(from_left.astype(jnp.bfloat16), 'space', ahead)  9.76 us
    all_to_all x1, starting transfers between devices, local(): lax.all_to_all(emp_columns.reshape(chips, own_emp // splits, rows), 'spac...  7.28 us
    ppermute x4, starting transfers between devices, reduce_ring(): lax.ppermute(from_left.astype(jnp.bfloat16), 'space', ahead)  6.06 us
    pallas_call x1, Pallas kernels, class_tables(): pl.pallas_call(table_kernel, grid=(4,), out_shape=jax.ShapeDtypeStruct((4...  4.79 us
    ppermute x4, starting transfers between devices, local(): from_left = lax.ppermute(from_left, 'space', ahead)  4.7 us
    ppermute x1, waiting for transfers between devices, local(): lax.ppermute(held_times, 'tm', [((d + step) % tm, d) for d in range(tm)])  3.2 us
    ppermute x4, waiting for transfers between devices, local(): from_left = lax.ppermute(from_left, 'space', ahead)  3.12 us
  transfers between devices with their start and end apart: 22, of which 13 were waited for; matrix products, arithmetic and copies ran while one was open for 7% of the time, Pallas kernels for 7%

profile of v5, /device:TPU:0, one launch (start us, length us, event | category | flops | bytes accessed | tf_op | source)
XLA Modules:
  0.0 81.9 jit_solution(8454845793408720048)
XLA Ops:
  0.0 1.6 %dynamic-slice_bitcast_fusion = bf16[8,16,864]{2,1,0:T(8,128)(2,1)} fusion(bf16[10,2,16,864]{3,2,1,0:T(8,128)(2,1)} %bitcast.17, s32[]{:T(128)S(6)} %select_n.25), kind=kLoop, calls=%fused_computation.2 | loop fusion | bytes 442372 | tf_op jit(solution)/shard_map/reshape | solution.py:389
  1.6 7.3 %all-to-all-start = ((bf16[8,16,864]{2,1,0:T(8,128)(2,1)}), bf16[8,16,864]{2,1,0:T(8,128)(2,1)S(1)}, u32[]{:S(2)}, u32[]{:S(2)}) async-start(bf16[8,16,864]{2,1,0:T(8,128)(2,1)} %dynamic-slice_bitcast_fusion), calls=%async_computation | async-start | bytes 458752 | tf_op jit(solution)/shard_map/all_to_all | solution.py:388
  8.9 0.9 %slice.42 = bf16[64,864]{1,0:T(8,128)(2,1)S(1)} slice(bf16[320,864]{1,0:T(8,128)(2,1)} %bitcast.18), slice={[0:64], [0:864]} | slice | bytes 221184 | tf_op jit(solution)/shard_map/slice | solution.py:378
  9.9 0.1 collective-permute-start
  10.0 1.2 %collective-permute-done = bf16[32,864]{1,0:T(8,128)(2,1)S(1)} collective-permute-done((bf16[32,864]{1,0:T(8,128)(2,1)S(1)}, bf16[32,864]{1,0:T(8,128)(2,1)S(1)}, u32[]{:S(2)}, u32[]{:S(2)}) %collective-permute-start) | collective-permute-done | bytes 55328 | tf_op jit(solution)/shard_map/ppermute | solution.py:381
  11.2 0.0 copy-start.1
  11.2 0.0 copy-start.13
  11.2 0.0 copy-start.2
  11.2 2.1 %collective-permute-start.2 = (bf16[2,32,864]{2,1,0:T(8,128)(2,1)S(1)}, bf16[2,32,864]{2,1,0:T(8,128)(2,1)S(1)}, u32[]{:S(2)}, u32[]{:S(2)}) collective-permute-start(bf16[2,32,864]{2,1,0:T(8,128)(2,1)S(1)} %pad_maximum_fusion.refs_4_), channel_id=1, source_target_pairs={{4,0},{5,1},{8,4},{9,5},{12,8},{13,9},{14,12},{15,13},{10,14},{11,... | collective-permute-start | bytes 331784 | tf_op jit(solution)/shard_map/ppermute | solution.py:426
  13.3 0.1 collective-permute-start.1
  13.4 4.8 %class_tables.1.refs_12_ = bf16[4,3584,256]{2,1,0:T(8,128)(2,1)} custom-call(s32[1]{0:T(128)} %constant.37.clone.1.held_ref), custom_call_target="tpu_custom_call" | custom-call | flops 58720256 | bytes 7340032 | tf_op jit(solution)/shard_map/class_tables/pallas_call | solution.py:103
  18.2 0.0 copy-done.1
  18.2 0.0 collective-permute-done.2.refs_6_
  18.2 0.3 collective-permute-done.1.refs_5_
  18.6 0.0 all-to-all-done.refs_0_
  18.6 1.6 %collective-permute-start.5 = (bf16[8,16,864]{2,1,0:T(8,128)(2,1)S(1)}, bf16[8,16,864]{2,1,0:T(8,128)(2,1)S(1)}, u32[]{:S(2)}, u32[]{:S(2)}) collective-permute-start(bf16[8,16,864]{2,1,0:T(8,128)(2,1)S(1)} %all-to-all-done.refs_0_), channel_id=1, source_target_pairs={{0,16},{16,0},{1,17},{17,1},{2,18},{18,2},{3,19},{19,3},{4,20},{20... | collective-permute-start | bytes 663560 | tf_op jit(solution)/shard_map/ppermute | solution.py:405
  20.1 1.6 %collective-permute-start.3 = (bf16[2,32,864]{2,1,0:T(8,128)(2,1)S(1)}, bf16[2,32,864]{2,1,0:T(8,128)(2,1)S(1)}, u32[]{:S(2)}, u32[]{:S(2)}) collective-permute-start(bf16[2,32,864]{2,1,0:T(8,128)(2,1)S(1)} %collective-permute-done.1.refs_5_), channel_id=1, source_target_pairs={{0,4},{1,5},{4,8},{5,9},{8,12},{9,13},{12,14},{13,15},{14,10},{15,... | collective-permute-start | bytes 331784 | tf_op jit(solution)/shard_map/ppermute | solution.py:422
  21.7 0.4 collective-permute-start.4
  22.8 0.0 copy-done.13
  22.8 0.1 reshape.15
  22.9 0.0 collective-permute-start.9
  22.9 2.0 %collective-permute-done.3.refs_7_ = bf16[2,32,864]{2,1,0:T(8,128)(2,1)S(1)} collective-permute-done((bf16[2,32,864]{2,1,0:T(8,128)(2,1)S(1)}, bf16[2,32,864]{2,1,0:T(8,128)(2,1)S(1)}, u32[]{:S(2)}, u32[]{:S(2)}) %collective-permute-start.3) | collective-permute-done | bytes 110624 | tf_op jit(solution)/shard_map/ppermute | solution.py:422
  24.9 1.6 %collective-permute-done.4.refs_8_ = bf16[2,32,864]{2,1,0:T(8,128)(2,1)S(1)} collective-permute-done((bf16[2,32,864]{2,1,0:T(8,128)(2,1)S(1)}, bf16[2,32,864]{2,1,0:T(8,128)(2,1)S(1)}, u32[]{:S(2)}, u32[]{:S(2)}) %collective-permute-start.4) | collective-permute-done | bytes 110624 | tf_op jit(solution)/shard_map/ppermute | solution.py:426
  26.5 0.0 collective-permute-done.5.refs_2_
  26.5 1.5 %collective-permute-start.6 = (bf16[2,32,864]{2,1,0:T(8,128)(2,1)S(1)}, bf16[2,32,864]{2,1,0:T(8,128)(2,1)S(1)}, u32[]{:S(2)}, u32[]{:S(2)}) collective-permute-start(bf16[2,32,864]{2,1,0:T(8,128)(2,1)S(1)} %collective-permute-done.3.refs_7_), channel_id=1, source_target_pairs={{0,4},{1,5},{4,8},{5,9},{8,12},{9,13},{12,14},{13,15},{14,10},{15,... | collective-permute-start | bytes 331784 | tf_op jit(solution)/shard_map/ppermute | solution.py:422
  28.1 0.6 collective-permute-start.7
  28.6 0.0 collective-permute-start.10
  28.6 0.6 pad_add_fusion.place_ref
  29.2 0.6 collective-permute-start.8
  29.8 3.2 %collective-permute-done.8 = f32[1]{0:T(128)} collective-permute-done((f32[1]{0:T(128)}, f32[1]{0:T(128)}, u32[]{:S(2)}, u32[]{:S(2)}) %collective-permute-start.8) | collective-permute-done | bytes 36 | tf_op jit(solution)/shard_map/ppermute | solution.py:412
  33.0 0.0 collective-permute-done.6.refs_9_
  33.0 0.0 collective-permute-done.7.refs_10_
  33.0 0.0 copy-start.11
  33.0 1.5 %collective-permute-start.11 = (bf16[2,32,864]{2,1,0:T(8,128)(2,1)S(1)}, bf16[2,32,864]{2,1,0:T(8,128)(2,1)S(1)}, u32[]{:S(2)}, u32[]{:S(2)}) collective-permute-start(bf16[2,32,864]{2,1,0:T(8,128)(2,1)S(1)} %collective-permute-done.6.refs_9_), channel_id=1, source_target_pairs={{0,4},{1,5},{4,8},{5,9},{8,12},{9,13},{12,14},{13,15},{14,10},{15,... | collective-permute-start | bytes 331784 | tf_op jit(solution)/shard_map/ppermute | solution.py:422
  34.5 1.2 %pad_maximum_fusion.1.scalar_ref = f32[326]{0:T(512)} fusion(f32[4]{0:T(128)S(1)} %reshape.15, f32[1]{0:T(128)} %collective-permute-done.8, f32[1]{0:T(128)S(6)} %copy.8, f32[320]{0:T(512)S(1)} %copy-done.2), kind=kLoop, calls=%fused_computation.18 | loop fusion | flops 978 | bytes 2608 | tf_op jit(solution)/shard_map/concatenate | solution.py:416
  35.7 1.3 %pair_weights.1 = f32[1,8,128]{2,1,0:T(8,128)} custom-call(s32[2]{0:T(128)} %pad_add_fusion.place_ref, f32[326]{0:T(512)} %pad_maximum_fusion.1.scalar_ref), custom_call_target="tpu_custom_call" | custom-call | flops 16777216 | bytes 1048576 | tf_op jit(solution)/shard_map/pair_weights/pallas_call | solution.py:120
  37.1 0.0 collective-permute-done.9.refs_1_
  37.1 0.8 collective-permute-done.11.refs_11_
  37.9 0.0 collective-permute-done.10.refs_3_
  37.9 0.6 copy-done.12
  38.5 0.1 copy-done.5
  38.6 17.5 %pair_moment.1 = (f32[128,896]{1,0:T(8,128)}, bf16[128,896]{1,0:T(8,128)(2,1)}, f32[384,896]{1,0:T(8,128)}, bf16[384,896]{1,0:T(8,128)(2,1)}) custom-call(s32[2]{0:T(128)} %pad_add_fusion.place_ref, f32[8,128]{1,0:T(8,128)} %bitcast.20, bf16[8,16,864]{2,1,0:T(8,128)(2,1)} %copy-done, bf16[8,16,864]{2,1,0:T(8,128)(2,1)} %copy-done.4, ...), custom_call_target="tpu_custom_call" | custom-call | flops 7516192768 | bytes 16777216 | tf_op jit(solution)/shard_map/pair_moment/pallas_call | solution.py:315
  56.0 0.1 collective-permute-start.13
  56.1 0.5 collective-permute-start.12
  56.6 1.2 %collective-permute-done.13 = bf16[128,896]{1,0:T(8,128)(2,1)S(1)} collective-permute-done((bf16[128,896]{1,0:T(8,128)(2,1)}, bf16[128,896]{1,0:T(8,128)(2,1)S(1)}, u32[]{:S(2)}, u32[]{:S(2)}) %collective-permute-start.13) | collective-permute-done | bytes 229408 | tf_op jit(solution)/shard_map/ppermute | solution.py:436
  57.8 1.1 %add_convert_fusion = bf16[128,896]{1,0:T(8,128)(2,1)S(1)} fusion(f32[128,896]{1,0:T(8,128)} %get-tuple-element.37, bf16[128,896]{1,0:T(8,128)(2,1)S(1)} %collective-permute-done.13), kind=kLoop, calls=%fused_computation.1 | loop fusion | flops 344064 | bytes 917504 | tf_op jit(solution)/shard_map/convert.1
  58.9 1.5 %collective-permute-start.14 = (bf16[54,896]{1,0:T(8,128)(2,1)S(1)}, bf16[54,896]{1,0:T(8,128)(2,1)S(1)}, u32[]{:S(2)}, u32[]{:S(2)}) collective-permute-start(bf16[54,896]{1,0:T(8,128)(2,1)S(1)} %get-tuple-element.44), channel_id=1, source_target_pairs={{0,4},{1,5},{4,8},{5,9},{8,12},{9,13},{12,14},{13,15},{14,10},{15,... | collective-permute-start | bytes 290312 | tf_op jit(solution)/shard_map/ppermute | solution.py:357
  60.4 0.6 collective-permute-start.18
  61.0 0.0 collective-permute-done.12
  61.0 1.5 %convert_add_fusion = f32[384,896]{1,0:T(8,128)S(1)} fusion(f32[384,896]{1,0:T(8,128)} %get-tuple-element.35, bf16[384,896]{1,0:T(8,128)(2,1)S(1)} %collective-permute-done.12), kind=kLoop, calls=%fused_computation | loop fusion | flops 688128 | bytes 3440640 | tf_op jit(solution)/shard_map/add | solution.py:437
  62.5 1.4 %collective-permute-done.14 = bf16[54,896]{1,0:T(8,128)(2,1)S(1)} collective-permute-done((bf16[54,896]{1,0:T(8,128)(2,1)S(1)}, bf16[54,896]{1,0:T(8,128)(2,1)S(1)}, u32[]{:S(2)}, u32[]{:S(2)}) %collective-permute-start.14) | collective-permute-done | bytes 96800 | tf_op jit(solution)/shard_map/ppermute | solution.py:357
  63.9 1.5 %collective-permute-start.15 = (bf16[54,896]{1,0:T(8,128)(2,1)S(1)}, bf16[54,896]{1,0:T(8,128)(2,1)S(1)}, u32[]{:S(2)}, u32[]{:S(2)}) collective-permute-start(bf16[54,896]{1,0:T(8,128)(2,1)S(1)} %fusion.6), channel_id=1, source_target_pairs={{0,4},{1,5},{4,8},{5,9},{8,12},{9,13},{12,14},{13,15},{14,10},{15,... | collective-permute-start | bytes 290312 | tf_op jit(solution)/shard_map/ppermute | solution.py:357
  65.4 0.0 collective-permute-done.18
  65.4 3.2 %collective-permute-done.15 = bf16[54,896]{1,0:T(8,128)(2,1)S(1)} collective-permute-done((bf16[54,896]{1,0:T(8,128)(2,1)S(1)}, bf16[54,896]{1,0:T(8,128)(2,1)S(1)}, u32[]{:S(2)}, u32[]{:S(2)}) %collective-permute-start.15) | collective-permute-done | bytes 96800 | tf_op jit(solution)/shard_map/ppermute | solution.py:357
  68.6 1.5 %collective-permute-start.16 = (bf16[54,896]{1,0:T(8,128)(2,1)S(1)}, bf16[54,896]{1,0:T(8,128)(2,1)S(1)}, u32[]{:S(2)}, u32[]{:S(2)}) collective-permute-start(bf16[54,896]{1,0:T(8,128)(2,1)S(1)} %get-tuple-element.42), channel_id=1, source_target_pairs={{0,4},{1,5},{4,8},{5,9},{8,12},{9,13},{12,14},{13,15},{14,10},{15,... | collective-permute-start | bytes 290312 | tf_op jit(solution)/shard_map/ppermute | solution.py:357
  70.1 0.6 collective-permute-start.19
  70.7 2.6 %collective-permute-done.16 = bf16[54,896]{1,0:T(8,128)(2,1)S(1)} collective-permute-done((bf16[54,896]{1,0:T(8,128)(2,1)S(1)}, bf16[54,896]{1,0:T(8,128)(2,1)S(1)}, u32[]{:S(2)}, u32[]{:S(2)}) %collective-permute-start.16) | collective-permute-done | bytes 96800 | tf_op jit(solution)/shard_map/ppermute | solution.py:357
  73.3 1.5 %collective-permute-done.19 = bf16[54,896]{1,0:T(8,128)(2,1)S(1)} collective-permute-done((bf16[54,896]{1,0:T(8,128)(2,1)S(1)}, bf16[54,896]{1,0:T(8,128)(2,1)S(1)}, u32[]{:S(2)}, u32[]{:S(2)}) %collective-permute-start.19) | collective-permute-done | bytes 96800 | tf_op jit(solution)/shard_map/ppermute | solution.py:359
  74.8 0.1 fusion.4
  74.8 1.5 %collective-permute-start.17 = (bf16[54,896]{1,0:T(8,128)(2,1)S(1)}, bf16[54,896]{1,0:T(8,128)(2,1)S(1)}, u32[]{:S(2)}, u32[]{:S(2)}) collective-permute-start(bf16[54,896]{1,0:T(8,128)(2,1)S(1)} %get-tuple-element.39), channel_id=1, source_target_pairs={{0,4},{1,5},{4,8},{5,9},{8,12},{9,13},{12,14},{13,15},{14,10},{15,... | collective-permute-start | bytes 290312 | tf_op jit(solution)/shard_map/ppermute | solution.py:357
  76.3 0.6 collective-permute-start.20
  76.9 2.6 %collective-permute-done.17 = bf16[54,896]{1,0:T(8,128)(2,1)S(1)} collective-permute-done((bf16[54,896]{1,0:T(8,128)(2,1)S(1)}, bf16[54,896]{1,0:T(8,128)(2,1)S(1)}, u32[]{:S(2)}, u32[]{:S(2)}) %collective-permute-start.17) | collective-permute-done | bytes 96800 | tf_op jit(solution)/shard_map/ppermute | solution.py:357
  79.5 1.5 %collective-permute-done.20 = bf16[54,896]{1,0:T(8,128)(2,1)S(1)} collective-permute-done((bf16[54,896]{1,0:T(8,128)(2,1)S(1)}, bf16[54,896]{1,0:T(8,128)(2,1)S(1)}, u32[]{:S(2)}, u32[]{:S(2)}) %collective-permute-start.20) | collective-permute-done | bytes 96800 | tf_op jit(solution)/shard_map/ppermute | solution.py:359
  81.0 0.9 %copy.6 = f32[1,54,864]{2,0,1:T(1,128)} copy(f32[1,54,864]{2,1,0:T(8,128)S(1)} %fusion.1) | data formatting | bytes 373248 | tf_op jit(solution)/shard_map/stack | solution.py:446
  (26 shorter events, 0.2 us)
Async XLA Ops:
  1.6 16.9 %all-to-all-start = ((bf16[8,16,864]{2,1,0:T(8,128)(2,1)}), bf16[8,16,864]{2,1,0:T(8,128)(2,1)S(1)}, u32[]{:S(2)}, u32[]{:S(2)}) async-start(bf16[8,16,864]{2,1,0:T(8,128)(2,1)} %dynamic-slice_bitcast_fusion), calls=%async_computation | async-start | bytes 458752 | tf_op jit(solution)/shard_map/all_to_all | solution.py:388
  9.9 1.3 %collective-permute-start = (bf16[32,864]{1,0:T(8,128)(2,1)S(1)}, bf16[32,864]{1,0:T(8,128)(2,1)S(1)}, u32[]{:S(2)}, u32[]{:S(2)}) collective-permute-start(bf16[32,864]{1,0:T(8,128)(2,1)S(1)} %get-tuple-element.47), channel_id=1, source_target_pairs={{0,1},{1,0},{2,3},{3,2},{4,5},{5,4},{6,7},{7,6},{8,9},{9,8},{10,11... | collective-permute-start | bytes 165896 | tf_op jit(solution)/shard_map/ppermute | solution.py:381
  11.2 7.0 %copy-start.1 = (bf16[2,32,864]{2,1,0:T(8,128)(2,1)}, bf16[2,32,864]{2,1,0:T(8,128)(2,1)S(1)}, u32[]{:S(2)}) copy-start(bf16[2,32,864]{2,1,0:T(8,128)(2,1)S(1)} %pad_maximum_fusion.refs_4_) | copy-start | bytes 331780
  11.2 11.6 %copy-start.13 = (f32[2,2]{1,0:T(2,128)S(1)}, f32[2,2]{1,0:T(2,128)}, u32[]{:S(2)}) copy-start(f32[2,2]{1,0:T(2,128)} %param.7) | copy-start | bytes 52
  11.2 23.3 %copy-start.2 = (f32[320]{0:T(512)S(1)}, f32[320]{0:T(512)}, u32[]{:S(2)}) copy-start(f32[320]{0:T(512)} %param.5) | copy-start | bytes 3844
  11.2 7.0 %collective-permute-start.2 = (bf16[2,32,864]{2,1,0:T(8,128)(2,1)S(1)}, bf16[2,32,864]{2,1,0:T(8,128)(2,1)S(1)}, u32[]{:S(2)}, u32[]{:S(2)}) collective-permute-start(bf16[2,32,864]{2,1,0:T(8,128)(2,1)S(1)} %pad_maximum_fusion.refs_4_), channel_id=1, source_target_pairs={{4,0},{5,1},{8,4},{9,5},{12,8},{13,9},{14,12},{15,13},{10,14},{11,... | collective-permute-start | bytes 331784 | tf_op jit(solution)/shard_map/ppermute | solution.py:426
  13.3 5.3 %collective-permute-start.1 = (bf16[2,32,864]{2,1,0:T(8,128)(2,1)S(1)}, bf16[2,32,864]{2,1,0:T(8,128)(2,1)S(1)}, u32[]{:S(2)}, u32[]{:S(2)}) collective-permute-start(bf16[2,32,864]{2,1,0:T(8,128)(2,1)S(1)} %pad_maximum_fusion.refs_4_), channel_id=1, source_target_pairs={{0,4},{1,5},{4,8},{5,9},{8,12},{9,13},{12,14},{13,15},{14,10},{15,... | collective-permute-start | bytes 331784 | tf_op jit(solution)/shard_map/ppermute | solution.py:422
  18.2 19.6 %copy-start.6 = (bf16[2,32,864]{2,1,0:T(8,128)(2,1)}, bf16[2,32,864]{2,1,0:T(8,128)(2,1)S(1)}, u32[]{:S(2)}) copy-start(bf16[2,32,864]{2,1,0:T(8,128)(2,1)S(1)} %collective-permute-done.2.refs_6_) | copy-start | bytes 331780
  18.6 19.3 %copy-start.7 = (bf16[2,32,864]{2,1,0:T(8,128)(2,1)}, bf16[2,32,864]{2,1,0:T(8,128)(2,1)S(1)}, u32[]{:S(2)}) copy-start(bf16[2,32,864]{2,1,0:T(8,128)(2,1)S(1)} %collective-permute-done.1.refs_5_) | copy-start | bytes 331780
  18.6 19.3 %copy-start = (bf16[8,16,864]{2,1,0:T(8,128)(2,1)}, bf16[8,16,864]{2,1,0:T(8,128)(2,1)S(1)}, u32[]{:S(2)}) copy-start(bf16[8,16,864]{2,1,0:T(8,128)(2,1)S(1)} %all-to-all-done.refs_0_) | copy-start | bytes 663556
  18.6 8.0 %collective-permute-start.5 = (bf16[8,16,864]{2,1,0:T(8,128)(2,1)S(1)}, bf16[8,16,864]{2,1,0:T(8,128)(2,1)S(1)}, u32[]{:S(2)}, u32[]{:S(2)}) collective-permute-start(bf16[8,16,864]{2,1,0:T(8,128)(2,1)S(1)} %all-to-all-done.refs_0_), channel_id=1, source_target_pairs={{0,16},{16,0},{1,17},{17,1},{2,18},{18,2},{3,19},{19,3},{4,20},{20... | collective-permute-start | bytes 663560 | tf_op jit(solution)/shard_map/ppermute | solution.py:405
  20.1 4.8 %collective-permute-start.3 = (bf16[2,32,864]{2,1,0:T(8,128)(2,1)S(1)}, bf16[2,32,864]{2,1,0:T(8,128)(2,1)S(1)}, u32[]{:S(2)}, u32[]{:S(2)}) collective-permute-start(bf16[2,32,864]{2,1,0:T(8,128)(2,1)S(1)} %collective-permute-done.1.refs_5_), channel_id=1, source_target_pairs={{0,4},{1,5},{4,8},{5,9},{8,12},{9,13},{12,14},{13,15},{14,10},{15,... | collective-permute-start | bytes 331784 | tf_op jit(solution)/shard_map/ppermute | solution.py:422
  21.7 4.8 %collective-permute-start.4 = (bf16[2,32,864]{2,1,0:T(8,128)(2,1)S(1)}, bf16[2,32,864]{2,1,0:T(8,128)(2,1)S(1)}, u32[]{:S(2)}, u32[]{:S(2)}) collective-permute-start(bf16[2,32,864]{2,1,0:T(8,128)(2,1)S(1)} %collective-permute-done.2.refs_6_), channel_id=1, source_target_pairs={{4,0},{5,1},{8,4},{9,5},{12,8},{13,9},{14,12},{15,13},{10,14},{11,... | collective-permute-start | bytes 331784 | tf_op jit(solution)/shard_map/ppermute | solution.py:426
  22.9 14.2 %collective-permute-start.9 = (bf16[8,16,864]{2,1,0:T(8,128)(2,1)S(1)}, bf16[8,16,864]{2,1,0:T(8,128)(2,1)S(1)}, u32[]{:S(2)}, u32[]{:S(2)}) collective-permute-start(bf16[8,16,864]{2,1,0:T(8,128)(2,1)S(1)} %all-to-all-done.refs_0_), channel_id=1, source_target_pairs={{0,1},{1,0},{2,3},{3,2},{4,5},{5,4},{6,7},{7,6},{8,9},{9,8},{10,11... | collective-permute-start | bytes 663560 | tf_op jit(solution)/shard_map/ppermute | solution.py:404
  24.9 13.0 %copy-start.8 = (bf16[2,32,864]{2,1,0:T(8,128)(2,1)}, bf16[2,32,864]{2,1,0:T(8,128)(2,1)S(1)}, u32[]{:S(2)}) copy-start(bf16[2,32,864]{2,1,0:T(8,128)(2,1)S(1)} %collective-permute-done.3.refs_7_) | copy-start | bytes 331780
  26.5 11.4 %copy-start.9 = (bf16[2,32,864]{2,1,0:T(8,128)(2,1)}, bf16[2,32,864]{2,1,0:T(8,128)(2,1)S(1)}, u32[]{:S(2)}) copy-start(bf16[2,32,864]{2,1,0:T(8,128)(2,1)S(1)} %collective-permute-done.4.refs_8_) | copy-start | bytes 331780
  26.5 11.4 %copy-start.3 = (bf16[8,16,864]{2,1,0:T(8,128)(2,1)}, bf16[8,16,864]{2,1,0:T(8,128)(2,1)S(1)}, u32[]{:S(2)}) copy-start(bf16[8,16,864]{2,1,0:T(8,128)(2,1)S(1)} %collective-permute-done.5.refs_2_) | copy-start | bytes 663556
  26.5 6.4 %collective-permute-start.6 = (bf16[2,32,864]{2,1,0:T(8,128)(2,1)S(1)}, bf16[2,32,864]{2,1,0:T(8,128)(2,1)S(1)}, u32[]{:S(2)}, u32[]{:S(2)}) collective-permute-start(bf16[2,32,864]{2,1,0:T(8,128)(2,1)S(1)} %collective-permute-done.3.refs_7_), channel_id=1, source_target_pairs={{0,4},{1,5},{4,8},{5,9},{8,12},{9,13},{12,14},{13,15},{14,10},{15,... | collective-permute-start | bytes 331784 | tf_op jit(solution)/shard_map/ppermute | solution.py:422
  28.1 4.9 %collective-permute-start.7 = (bf16[2,32,864]{2,1,0:T(8,128)(2,1)S(1)}, bf16[2,32,864]{2,1,0:T(8,128)(2,1)S(1)}, u32[]{:S(2)}, u32[]{:S(2)}) collective-permute-start(bf16[2,32,864]{2,1,0:T(8,128)(2,1)S(1)} %collective-permute-done.4.refs_8_), channel_id=1, source_target_pairs={{4,0},{5,1},{8,4},{9,5},{12,8},{13,9},{14,12},{15,13},{10,14},{11,... | collective-permute-start | bytes 331784 | tf_op jit(solution)/shard_map/ppermute | solution.py:426
  28.6 9.2 %collective-permute-start.10 = (bf16[8,16,864]{2,1,0:T(8,128)(2,1)S(1)}, bf16[8,16,864]{2,1,0:T(8,128)(2,1)S(1)}, u32[]{:S(2)}, u32[]{:S(2)}) collective-permute-start(bf16[8,16,864]{2,1,0:T(8,128)(2,1)S(1)} %collective-permute-done.5.refs_2_), channel_id=1, source_target_pairs={{0,1},{1,0},{2,3},{3,2},{4,5},{5,4},{6,7},{7,6},{8,9},{9,8},{10,11... | collective-permute-start | bytes 663560 | tf_op jit(solution)/shard_map/ppermute | solution.py:409
  29.2 3.8 %collective-permute-start.8 = (f32[1]{0:T(128)}, f32[1]{0:T(128)}, u32[]{:S(2)}, u32[]{:S(2)}) collective-permute-start(f32[1]{0:T(128)} %param.6), channel_id=1, source_target_pairs={{16,0},{0,16},{17,1},{1,17},{18,2},{2,18},{19,3},{3,19},{20,4},{4,... | collective-permute-start | bytes 20 | tf_op jit(solution)/shard_map/ppermute | solution.py:412
  33.0 4.9 %copy-start.10 = (bf16[2,32,864]{2,1,0:T(8,128)(2,1)}, bf16[2,32,864]{2,1,0:T(8,128)(2,1)S(1)}, u32[]{:S(2)}) copy-start(bf16[2,32,864]{2,1,0:T(8,128)(2,1)S(1)} %collective-permute-done.6.refs_9_) | copy-start | bytes 331780
  33.0 4.9 %copy-start.11 = (bf16[2,32,864]{2,1,0:T(8,128)(2,1)}, bf16[2,32,864]{2,1,0:T(8,128)(2,1)S(1)}, u32[]{:S(2)}) copy-start(bf16[2,32,864]{2,1,0:T(8,128)(2,1)S(1)} %collective-permute-done.7.refs_10_) | copy-start | bytes 331780
  33.0 4.8 %collective-permute-start.11 = (bf16[2,32,864]{2,1,0:T(8,128)(2,1)S(1)}, bf16[2,32,864]{2,1,0:T(8,128)(2,1)S(1)}, u32[]{:S(2)}, u32[]{:S(2)}) collective-permute-start(bf16[2,32,864]{2,1,0:T(8,128)(2,1)S(1)} %collective-permute-done.6.refs_9_), channel_id=1, source_target_pairs={{0,4},{1,5},{4,8},{5,9},{8,12},{9,13},{12,14},{13,15},{14,10},{15,... | collective-permute-start | bytes 331784 | tf_op jit(solution)/shard_map/ppermute | solution.py:422
  37.1 0.8 %copy-start.4 = (bf16[8,16,864]{2,1,0:T(8,128)(2,1)}, bf16[8,16,864]{2,1,0:T(8,128)(2,1)S(1)}, u32[]{:S(2)}) copy-start(bf16[8,16,864]{2,1,0:T(8,128)(2,1)S(1)} %collective-permute-done.9.refs_1_) | copy-start | bytes 663556
  37.9 0.7 copy-start.12
  37.9 0.7 copy-start.5
  56.0 1.8 %collective-permute-start.13 = (bf16[128,896]{1,0:T(8,128)(2,1)}, bf16[128,896]{1,0:T(8,128)(2,1)S(1)}, u32[]{:S(2)}, u32[]{:S(2)}) collective-permute-start(bf16[128,896]{1,0:T(8,128)(2,1)} %get-tuple-element.38), channel_id=1, source_target_pairs={{0,1},{1,0},{2,3},{3,2},{4,5},{5,4},{6,7},{7,6},{8,9},{9,8},{10,11... | collective-permute-start | bytes 688136 | tf_op jit(solution)/shard_map/ppermute | solution.py:436
  56.1 4.9 %collective-permute-start.12 = (bf16[384,896]{1,0:T(8,128)(2,1)}, bf16[384,896]{1,0:T(8,128)(2,1)S(1)}, u32[]{:S(2)}, u32[]{:S(2)}) collective-permute-start(bf16[384,896]{1,0:T(8,128)(2,1)} %get-tuple-element.36), channel_id=1, source_target_pairs={{0,1},{1,0},{2,3},{3,2},{4,5},{5,4},{6,7},{7,6},{8,9},{9,8},{10,11... | collective-permute-start | bytes 2064392 | tf_op jit(solution)/shard_map/ppermute | solution.py:437
  58.9 4.9 %collective-permute-start.14 = (bf16[54,896]{1,0:T(8,128)(2,1)S(1)}, bf16[54,896]{1,0:T(8,128)(2,1)S(1)}, u32[]{:S(2)}, u32[]{:S(2)}) collective-permute-start(bf16[54,896]{1,0:T(8,128)(2,1)S(1)} %get-tuple-element.44), channel_id=1, source_target_pairs={{0,4},{1,5},{4,8},{5,9},{8,12},{9,13},{12,14},{13,15},{14,10},{15,... | collective-permute-start | bytes 290312 | tf_op jit(solution)/shard_map/ppermute | solution.py:357
  60.4 5.0 %collective-permute-start.18 = (bf16[54,896]{1,0:T(8,128)(2,1)S(1)}, bf16[54,896]{1,0:T(8,128)(2,1)S(1)}, u32[]{:S(2)}, u32[]{:S(2)}) collective-permute-start(bf16[54,896]{1,0:T(8,128)(2,1)S(1)} %get-tuple-element.45), channel_id=1, source_target_pairs={{4,0},{5,1},{8,4},{9,5},{12,8},{13,9},{14,12},{15,13},{10,14},{11,... | collective-permute-start | bytes 290312 | tf_op jit(solution)/shard_map/ppermute | solution.py:359
  63.9 4.7 %collective-permute-start.15 = (bf16[54,896]{1,0:T(8,128)(2,1)S(1)}, bf16[54,896]{1,0:T(8,128)(2,1)S(1)}, u32[]{:S(2)}, u32[]{:S(2)}) collective-permute-start(bf16[54,896]{1,0:T(8,128)(2,1)S(1)} %fusion.6), channel_id=1, source_target_pairs={{0,4},{1,5},{4,8},{5,9},{8,12},{9,13},{12,14},{13,15},{14,10},{15,... | collective-permute-start | bytes 290312 | tf_op jit(solution)/shard_map/ppermute | solution.py:357
  68.6 4.7 %collective-permute-start.16 = (bf16[54,896]{1,0:T(8,128)(2,1)S(1)}, bf16[54,896]{1,0:T(8,128)(2,1)S(1)}, u32[]{:S(2)}, u32[]{:S(2)}) collective-permute-start(bf16[54,896]{1,0:T(8,128)(2,1)S(1)} %get-tuple-element.42), channel_id=1, source_target_pairs={{0,4},{1,5},{4,8},{5,9},{8,12},{9,13},{12,14},{13,15},{14,10},{15,... | collective-permute-start | bytes 290312 | tf_op jit(solution)/shard_map/ppermute | solution.py:357
  70.1 4.6 %collective-permute-start.19 = (bf16[54,896]{1,0:T(8,128)(2,1)S(1)}, bf16[54,896]{1,0:T(8,128)(2,1)S(1)}, u32[]{:S(2)}, u32[]{:S(2)}) collective-permute-start(bf16[54,896]{1,0:T(8,128)(2,1)S(1)} %get-tuple-element.43), channel_id=1, source_target_pairs={{4,0},{5,1},{8,4},{9,5},{12,8},{13,9},{14,12},{15,13},{10,14},{11,... | collective-permute-start | bytes 290312 | tf_op jit(solution)/shard_map/ppermute | solution.py:359
  74.8 4.7 %collective-permute-start.17 = (bf16[54,896]{1,0:T(8,128)(2,1)S(1)}, bf16[54,896]{1,0:T(8,128)(2,1)S(1)}, u32[]{:S(2)}, u32[]{:S(2)}) collective-permute-start(bf16[54,896]{1,0:T(8,128)(2,1)S(1)} %get-tuple-element.39), channel_id=1, source_target_pairs={{0,4},{1,5},{4,8},{5,9},{8,12},{9,13},{12,14},{13,15},{14,10},{15,... | collective-permute-start | bytes 290312 | tf_op jit(solution)/shard_map/ppermute | solution.py:357
  76.3 4.6 %collective-permute-start.20 = (bf16[54,896]{1,0:T(8,128)(2,1)S(1)}, bf16[54,896]{1,0:T(8,128)(2,1)S(1)}, u32[]{:S(2)}, u32[]{:S(2)}) collective-permute-start(bf16[54,896]{1,0:T(8,128)(2,1)S(1)} %get-tuple-element.40), channel_id=1, source_target_pairs={{4,0},{5,1},{8,4},{9,5},{12,8},{13,9},{14,12},{15,13},{10,14},{11,... | collective-permute-start | bytes 290312 | tf_op jit(solution)/shard_map/ppermute | solution.py:359

commit v6 on v5

--- a/solution.py
+++ b/solution.py
@@ -153,9 +153,6 @@
     n_occ = occ_wide.shape[1]
     per_group = chips // steps
     plane = SIDE * SIDE // 2
-    whole_rows = max(1, LANES // n_occ)
-    first_emp = max(1, 3 * n_emp // 8 // whole_rows) * whole_rows
-    emp_cuts = (slice(0, first_emp), slice(first_emp, n_emp))
 
     copy = pltpu.make_async_copy(table_hbm, table, table_sem)
     me = place_ref[0]
@@ -218,9 +215,9 @@
         pltpu.VMEM((chips, 2, n_emp, n_rows), jnp.bfloat16),
     )
 
-    def build(half, target, cut):
-        emp_rows = [emp_wide[k, emp_cuts[half], cut] for k in range(4)]
-        for i in range(emp_rows[0].shape[0]):
+    def build(target, cut):
+        emp_rows = [emp_wide[k, :, cut] for k in range(4)]
+        for i in range(n_emp):
             emp_row = [
                 jnp.broadcast_to(emp_rows[k][i : i + 1], (16, LANES)).astype(jnp.bfloat16) for k in range(4)
             ]
@@ -240,7 +237,7 @@
     spacing = SIDE
     per_a = modes // spacing
 
-    def multiply(half, source, k):
+    def multiply(source, k):
         found = jnp.dot(source[k], table[k], preferred_element_type=jnp.float32).T
         a_odd, b_odd = divmod(k, 2)
         a_first = (a_odd + SIDE // 4) % 2
@@ -248,32 +245,23 @@
         for a_step in range(SIDE // 4):
             start = b_first * (SIDE // 2) + 2 * a_step + a_first
             for tile in range(source.shape[1] // LANES):
-                rho[emp_cuts[half].start * n_occ // LANES + tile, pl.ds(start, per_a, stride=spacing), :] = found[
+                rho[tile, pl.ds(start, per_a, stride=spacing), :] = found[
                     a_step * per_a : (a_step + 1) * per_a, tile * LANES : (tile + 1) * LANES
                 ]
 
     chunks = steps * depth // LANES
 
-    def transform(first, second):
-        def build_first(chunk, carry):
-            build(0, first, pl.ds(pl.multiple_of(chunk * LANES, LANES), LANES))
+    def transform(products):
+        def build_chunk(chunk, carry):
+            build(products, pl.ds(pl.multiple_of(chunk * LANES, LANES), LANES))
             return carry
 
-        lax.fori_loop(0, chunks, build_first, 0)
+        lax.fori_loop(0, chunks, build_chunk, 0)
         copy.wait()
         for k in range(4):
-            for chunk in range(k * chunks // 4, (k + 1) * chunks // 4):
-                build(1, second, slice(chunk * LANES, (chunk + 1) * LANES))
-            multiply(0, first, k)
-        for k in range(4):
-            multiply(1, second, k)
-
-    pl.run_scoped(
-        transform,
-        *(
-            pltpu.VMEM((4, (cut.stop - cut.start) * n_occ, steps * depth), jnp.bfloat16) for cut in emp_cuts
-        ),
-    )
+            multiply(products, k)
+
+    pl.run_scoped(transform, pltpu.VMEM((4, n_emp * n_occ, steps * depth), jnp.bfloat16))
 
     rows = NG // shards
 
@@ -401,10 +389,10 @@
     for hop in range(1, chips // 2 + 1):
         if hop == 2:
             from_left, from_right, emp, tables = lax.optimization_barrier((from_left, from_right, emp, tables))
-            emp_parts += [emp, lax.ppermute(emp, "space", swap)]
             traded = lax.ppermute(emp, "tm", [(0, 1), (1, 0)]) if splits > 1 else None
         elif hop == 3:
-            from_left, from_right, traded = lax.optimization_barrier((from_left, from_right, traded))
+            from_left, from_right, emp, traded = lax.optimization_barrier((from_left, from_right, emp, traded))
+            emp_parts += [emp, lax.ppermute(emp, "space", swap)]
             if splits > 1:
                 emp_parts += [traded, lax.ppermute(traded, "space", swap)]
             held_times = hold(times, (from_left, from_right))
@@ -412,7 +400,7 @@
                 lax.ppermute(held_times, "tm", [((d + step) % tm, d) for d in range(tm)]) for step in range(1, tm)
             ]
         elif hop == 4:
-            from_left, from_right, every_time = lax.optimization_barrier((from_left, from_right, every_time))
+            from_left, from_right = lax.optimization_barrier((from_left, from_right))
             scalars = jnp.concatenate([gaps] + every_time + [cos_weights.reshape(-1)])
             weights = all_pair_weights(
                 place, hold(scalars, (from_left, from_right)), tm, own_count, time_count, own_occ, own_emp

time: 82.4 us -> 84.6 us (1.027)
  Pallas kernels: 23.6 us -> 25.9 us
    ppermute x1, waiting for transfers between devices: 3.2 us -> 0.01 us  [local(): lax.ppermute(held_times, 'tm', [((d + step) % tm, d) for d in range(tm)])]
    pallas_call x1, Pallas kernels: 17.5 us -> 19.7 us  [pair_moment(): pl.pallas_call(functools.partial(pair_kernel, offsets, splits), out_shape...]
    ppermute x3, waiting for transfers between devices: 1.66 us -> 3.12 us  [local(): from_right = lax.ppermute(from_right, 'space', back)]
    ppermute x4, waiting for transfers between devices: 3.12 us -> 4.21 us  [local(): from_left = lax.ppermute(from_left, 'space', ahead)]
  transfers between devices with their start and end apart: 22 -> 22, of which waited for: 13 -> 14; matrix products, arithmetic and copies ran while one was open for 7% -> 6% of each run, Pallas kernels for 7% -> 7%
where the time goes in v6:
time: 84.6 us; the launch traced here: 84.1 us
  starting transfers between devices  26 us (31%)
  Pallas kernels  25.9 us (31%)
  waiting for transfers between devices  22.5 us (27%)
  other arithmetic  4.53 us (5%)
  local copies, waits for them, and re-layouts  4.31 us (5%)
  between operations  0.86 us (1%)
    pallas_call x1, Pallas kernels, pair_moment(): pl.pallas_call(functools.partial(pair_kernel, offsets, splits), out_shape...  19.7 us
    ppermute x4, waiting for transfers between devices, reduce_ring(): lax.ppermute(from_left.astype(jnp.bfloat16), 'space', ahead)  9.76 us
    all_to_all x1, starting transfers between devices, local(): lax.all_to_all(emp_columns.reshape(chips, own_emp // splits, rows), 'spac...  7.28 us
    ppermute x4, starting transfers between devices, reduce_ring(): lax.ppermute(from_left.astype(jnp.bfloat16), 'space', ahead)  6.13 us
    pallas_call x1, Pallas kernels, class_tables(): pl.pallas_call(table_kernel, grid=(4,), out_shape=jax.ShapeDtypeStruct((4...  4.79 us
    ppermute x4, starting transfers between devices, local(): from_left = lax.ppermute(from_left, 'space', ahead)  4.65 us
    ppermute x4, waiting for transfers between devices, local(): from_left = lax.ppermute(from_left, 'space', ahead)  4.21 us
    ppermute x3, waiting for transfers between devices, local(): from_right = lax.ppermute(from_right, 'space', back)  3.12 us
  transfers between devices with their start and end apart: 22, of which 14 were waited for; matrix products, arithmetic and copies ran while one was open for 6% of the time, Pallas kernels for 7%

profile of v6, /device:TPU:0, one launch (start us, length us, event | category | flops | bytes accessed | tf_op | source)
XLA Modules:
  0.0 84.1 jit_solution(6482889261171741877)
XLA Ops:
  0.0 1.6 %dynamic-slice_bitcast_fusion = bf16[8,16,864]{2,1,0:T(8,128)(2,1)} fusion(bf16[10,2,16,864]{3,2,1,0:T(8,128)(2,1)} %bitcast.17, s32[]{:T(128)S(6)} %select_n.25), kind=kLoop, calls=%fused_computation.2 | loop fusion | bytes 442372 | tf_op jit(solution)/shard_map/reshape | solution.py:377
  1.6 7.3 %all-to-all-start = ((bf16[8,16,864]{2,1,0:T(8,128)(2,1)}), bf16[8,16,864]{2,1,0:T(8,128)(2,1)S(1)}, u32[]{:S(2)}, u32[]{:S(2)}) async-start(bf16[8,16,864]{2,1,0:T(8,128)(2,1)} %dynamic-slice_bitcast_fusion), calls=%async_computation | async-start | bytes 458752 | tf_op jit(solution)/shard_map/all_to_all | solution.py:376
  8.9 0.9 %slice.42 = bf16[64,864]{1,0:T(8,128)(2,1)S(1)} slice(bf16[320,864]{1,0:T(8,128)(2,1)} %bitcast.18), slice={[0:64], [0:864]} | slice | bytes 221184 | tf_op jit(solution)/shard_map/slice | solution.py:366
  9.9 0.1 collective-permute-start
  10.0 1.2 %collective-permute-done = bf16[32,864]{1,0:T(8,128)(2,1)S(1)} collective-permute-done((bf16[32,864]{1,0:T(8,128)(2,1)S(1)}, bf16[32,864]{1,0:T(8,128)(2,1)S(1)}, u32[]{:S(2)}, u32[]{:S(2)}) %collective-permute-start) | collective-permute-done | bytes 55328 | tf_op jit(solution)/shard_map/ppermute | solution.py:369
  11.2 0.0 copy-start.1
  11.2 0.0 copy-start.13
  11.2 0.0 copy-start.2
  11.2 2.1 %collective-permute-start.2 = (bf16[2,32,864]{2,1,0:T(8,128)(2,1)S(1)}, bf16[2,32,864]{2,1,0:T(8,128)(2,1)S(1)}, u32[]{:S(2)}, u32[]{:S(2)}) collective-permute-start(bf16[2,32,864]{2,1,0:T(8,128)(2,1)S(1)} %pad_maximum_fusion.refs_4_), channel_id=1, source_target_pairs={{4,0},{5,1},{8,4},{9,5},{12,8},{13,9},{14,12},{15,13},{10,14},{11,... | collective-permute-start | bytes 331784 | tf_op jit(solution)/shard_map/ppermute | solution.py:414
  13.3 0.1 collective-permute-start.1
  13.4 4.8 %class_tables.1.refs_12_ = bf16[4,3584,256]{2,1,0:T(8,128)(2,1)} custom-call(s32[1]{0:T(128)} %constant.37.clone.1.held_ref), custom_call_target="tpu_custom_call" | custom-call | flops 58720256 | bytes 7340032 | tf_op jit(solution)/shard_map/class_tables/pallas_call | solution.py:103
  18.2 0.0 copy-done.1
  18.2 0.0 collective-permute-done.2.refs_6_
  18.2 0.3 collective-permute-done.1.refs_5_
  18.6 0.0 all-to-all-done.refs_0_
  18.6 1.6 %collective-permute-start.5 = (bf16[8,16,864]{2,1,0:T(8,128)(2,1)S(1)}, bf16[8,16,864]{2,1,0:T(8,128)(2,1)S(1)}, u32[]{:S(2)}, u32[]{:S(2)}) collective-permute-start(bf16[8,16,864]{2,1,0:T(8,128)(2,1)S(1)} %all-to-all-done.refs_0_), channel_id=1, source_target_pairs={{0,16},{16,0},{1,17},{17,1},{2,18},{18,2},{3,19},{19,3},{4,20},{20... | collective-permute-start | bytes 663560 | tf_op jit(solution)/shard_map/ppermute | solution.py:392
  20.1 1.6 %collective-permute-start.3 = (bf16[2,32,864]{2,1,0:T(8,128)(2,1)S(1)}, bf16[2,32,864]{2,1,0:T(8,128)(2,1)S(1)}, u32[]{:S(2)}, u32[]{:S(2)}) collective-permute-start(bf16[2,32,864]{2,1,0:T(8,128)(2,1)S(1)} %collective-permute-done.1.refs_5_), channel_id=1, source_target_pairs={{0,4},{1,5},{4,8},{5,9},{8,12},{9,13},{12,14},{13,15},{14,10},{15,... | collective-permute-start | bytes 331784 | tf_op jit(solution)/shard_map/ppermute | solution.py:410
  21.7 0.4 collective-permute-start.4
  22.8 0.0 copy-done.13
  22.8 0.1 reshape.15
  22.9 2.0 %collective-permute-done.3.refs_7_ = bf16[2,32,864]{2,1,0:T(8,128)(2,1)S(1)} collective-permute-done((bf16[2,32,864]{2,1,0:T(8,128)(2,1)S(1)}, bf16[2,32,864]{2,1,0:T(8,128)(2,1)S(1)}, u32[]{:S(2)}, u32[]{:S(2)}) %collective-permute-start.3) | collective-permute-done | bytes 110624 | tf_op jit(solution)/shard_map/ppermute | solution.py:410
  24.9 1.6 %collective-permute-done.4.refs_8_ = bf16[2,32,864]{2,1,0:T(8,128)(2,1)S(1)} collective-permute-done((bf16[2,32,864]{2,1,0:T(8,128)(2,1)S(1)}, bf16[2,32,864]{2,1,0:T(8,128)(2,1)S(1)}, u32[]{:S(2)}, u32[]{:S(2)}) %collective-permute-start.4) | collective-permute-done | bytes 110624 | tf_op jit(solution)/shard_map/ppermute | solution.py:414
  26.5 0.0 collective-permute-done.5.refs_2_
  26.5 1.5 %collective-permute-start.7 = (bf16[2,32,864]{2,1,0:T(8,128)(2,1)S(1)}, bf16[2,32,864]{2,1,0:T(8,128)(2,1)S(1)}, u32[]{:S(2)}, u32[]{:S(2)}) collective-permute-start(bf16[2,32,864]{2,1,0:T(8,128)(2,1)S(1)} %collective-permute-done.3.refs_7_), channel_id=1, source_target_pairs={{0,4},{1,5},{4,8},{5,9},{8,12},{9,13},{12,14},{13,15},{14,10},{15,... | collective-permute-start | bytes 331784 | tf_op jit(solution)/shard_map/ppermute | solution.py:410
  28.1 0.6 collective-permute-start.8
  28.6 0.0 collective-permute-start.9
  28.6 0.5 collective-permute-start.10
  29.1 0.6 pad_add_fusion.place_ref
  29.7 0.6 collective-permute-start.6
  30.3 1.1 %collective-permute-done.7.refs_9_ = bf16[2,32,864]{2,1,0:T(8,128)(2,1)S(1)} collective-permute-done((bf16[2,32,864]{2,1,0:T(8,128)(2,1)S(1)}, bf16[2,32,864]{2,1,0:T(8,128)(2,1)S(1)}, u32[]{:S(2)}, u32[]{:S(2)}) %collective-permute-start.7) | collective-permute-done | bytes 110624 | tf_op jit(solution)/shard_map/ppermute | solution.py:410
  31.4 1.5 %collective-permute-done.8.refs_10_ = bf16[2,32,864]{2,1,0:T(8,128)(2,1)S(1)} collective-permute-done((bf16[2,32,864]{2,1,0:T(8,128)(2,1)S(1)}, bf16[2,32,864]{2,1,0:T(8,128)(2,1)S(1)}, u32[]{:S(2)}, u32[]{:S(2)}) %collective-permute-start.8) | collective-permute-done | bytes 110624 | tf_op jit(solution)/shard_map/ppermute | solution.py:414
  32.8 1.5 %collective-permute-start.11 = (bf16[2,32,864]{2,1,0:T(8,128)(2,1)S(1)}, bf16[2,32,864]{2,1,0:T(8,128)(2,1)S(1)}, u32[]{:S(2)}, u32[]{:S(2)}) collective-permute-start(bf16[2,32,864]{2,1,0:T(8,128)(2,1)S(1)} %collective-permute-done.7.refs_9_), channel_id=1, source_target_pairs={{0,4},{1,5},{4,8},{5,9},{8,12},{9,13},{12,14},{13,15},{14,10},{15,... | collective-permute-start | bytes 331784 | tf_op jit(solution)/shard_map/ppermute | solution.py:410
  34.3 0.0 collective-permute-done.6
  34.3 1.2 %pad_maximum_fusion.1.scalar_ref = f32[326]{0:T(512)} fusion(f32[4]{0:T(128)S(1)} %reshape.15, f32[1]{0:T(128)} %collective-permute-done.6, f32[1]{0:T(128)S(6)} %copy.8, f32[320]{0:T(512)S(1)} %copy-done.2), kind=kLoop, calls=%fused_computation.18 | loop fusion | flops 978 | bytes 2608 | tf_op jit(solution)/shard_map/concatenate | solution.py:404
  35.5 1.3 %pair_weights.1 = f32[1,8,128]{2,1,0:T(8,128)} custom-call(s32[2]{0:T(128)} %pad_add_fusion.place_ref, f32[326]{0:T(512)} %pad_maximum_fusion.1.scalar_ref), custom_call_target="tpu_custom_call" | custom-call | flops 16777216 | bytes 1048576 | tf_op jit(solution)/shard_map/pair_weights/pallas_call | solution.py:120
  36.9 0.8 collective-permute-done.11.refs_11_
  37.6 0.0 collective-permute-done.9.refs_1_
  37.6 0.0 collective-permute-done.10.refs_3_
  37.7 0.5 copy-done.12
  38.3 0.1 copy-done.4
  38.4 0.1 copy-done.5
  38.5 19.7 %pair_moment.1 = (f32[128,896]{1,0:T(8,128)}, bf16[128,896]{1,0:T(8,128)(2,1)}, f32[384,896]{1,0:T(8,128)}, bf16[384,896]{1,0:T(8,128)(2,1)}) custom-call(s32[2]{0:T(128)} %pad_add_fusion.place_ref, f32[8,128]{1,0:T(8,128)} %bitcast.20, bf16[8,16,864]{2,1,0:T(8,128)(2,1)} %copy-done, bf16[8,16,864]{2,1,0:T(8,128)(2,1)} %copy-done.4, ...), custom_call_target="tpu_custom_call" | custom-call | flops 7516192768 | bytes 16777216 | tf_op jit(solution)/shard_map/pair_moment/pallas_call | solution.py:303
  58.2 0.1 collective-permute-start.13
  58.3 0.5 collective-permute-start.12
  58.8 1.2 %collective-permute-done.13 = bf16[128,896]{1,0:T(8,128)(2,1)S(1)} collective-permute-done((bf16[128,896]{1,0:T(8,128)(2,1)}, bf16[128,896]{1,0:T(8,128)(2,1)S(1)}, u32[]{:S(2)}, u32[]{:S(2)}) %collective-permute-start.13) | collective-permute-done | bytes 229408 | tf_op jit(solution)/shard_map/ppermute | solution.py:424
  60.0 1.1 %add_convert_fusion = bf16[128,896]{1,0:T(8,128)(2,1)S(1)} fusion(f32[128,896]{1,0:T(8,128)} %get-tuple-element.35, bf16[128,896]{1,0:T(8,128)(2,1)S(1)} %collective-permute-done.13), kind=kLoop, calls=%fused_computation.1 | loop fusion | flops 344064 | bytes 917504 | tf_op jit(solution)/shard_map/convert.1
  61.1 1.5 %collective-permute-start.14 = (bf16[54,896]{1,0:T(8,128)(2,1)S(1)}, bf16[54,896]{1,0:T(8,128)(2,1)S(1)}, u32[]{:S(2)}, u32[]{:S(2)}) collective-permute-start(bf16[54,896]{1,0:T(8,128)(2,1)S(1)} %get-tuple-element.42), channel_id=1, source_target_pairs={{0,4},{1,5},{4,8},{5,9},{8,12},{9,13},{12,14},{13,15},{14,10},{15,... | collective-permute-start | bytes 290312 | tf_op jit(solution)/shard_map/ppermute | solution.py:345
  62.6 0.6 collective-permute-start.18
  63.2 0.0 collective-permute-done.12
  63.2 1.5 %convert_add_fusion = f32[384,896]{1,0:T(8,128)S(1)} fusion(f32[384,896]{1,0:T(8,128)} %get-tuple-element.33, bf16[384,896]{1,0:T(8,128)(2,1)S(1)} %collective-permute-done.12), kind=kLoop, calls=%fused_computation | loop fusion | flops 688128 | bytes 3440640 | tf_op jit(solution)/shard_map/add | solution.py:425
  64.6 1.4 %collective-permute-done.14 = bf16[54,896]{1,0:T(8,128)(2,1)S(1)} collective-permute-done((bf16[54,896]{1,0:T(8,128)(2,1)S(1)}, bf16[54,896]{1,0:T(8,128)(2,1)S(1)}, u32[]{:S(2)}, u32[]{:S(2)}) %collective-permute-start.14) | collective-permute-done | bytes 96800 | tf_op jit(solution)/shard_map/ppermute | solution.py:345
  66.0 1.5 %collective-permute-start.15 = (bf16[54,896]{1,0:T(8,128)(2,1)S(1)}, bf16[54,896]{1,0:T(8,128)(2,1)S(1)}, u32[]{:S(2)}, u32[]{:S(2)}) collective-permute-start(bf16[54,896]{1,0:T(8,128)(2,1)S(1)} %fusion.6), channel_id=1, source_target_pairs={{0,4},{1,5},{4,8},{5,9},{8,12},{9,13},{12,14},{13,15},{14,10},{15,... | collective-permute-start | bytes 290312 | tf_op jit(solution)/shard_map/ppermute | solution.py:345
  67.6 0.0 collective-permute-done.18
  67.6 3.2 %collective-permute-done.15 = bf16[54,896]{1,0:T(8,128)(2,1)S(1)} collective-permute-done((bf16[54,896]{1,0:T(8,128)(2,1)S(1)}, bf16[54,896]{1,0:T(8,128)(2,1)S(1)}, u32[]{:S(2)}, u32[]{:S(2)}) %collective-permute-start.15) | collective-permute-done | bytes 96800 | tf_op jit(solution)/shard_map/ppermute | solution.py:345
  70.8 1.5 %collective-permute-start.16 = (bf16[54,896]{1,0:T(8,128)(2,1)S(1)}, bf16[54,896]{1,0:T(8,128)(2,1)S(1)}, u32[]{:S(2)}, u32[]{:S(2)}) collective-permute-start(bf16[54,896]{1,0:T(8,128)(2,1)S(1)} %get-tuple-element.40), channel_id=1, source_target_pairs={{0,4},{1,5},{4,8},{5,9},{8,12},{9,13},{12,14},{13,15},{14,10},{15,... | collective-permute-start | bytes 290312 | tf_op jit(solution)/shard_map/ppermute | solution.py:345
  72.3 0.6 collective-permute-start.19
  72.8 2.6 %collective-permute-done.16 = bf16[54,896]{1,0:T(8,128)(2,1)S(1)} collective-permute-done((bf16[54,896]{1,0:T(8,128)(2,1)S(1)}, bf16[54,896]{1,0:T(8,128)(2,1)S(1)}, u32[]{:S(2)}, u32[]{:S(2)}) %collective-permute-start.16) | collective-permute-done | bytes 96800 | tf_op jit(solution)/shard_map/ppermute | solution.py:345
  75.5 1.5 %collective-permute-done.19 = bf16[54,896]{1,0:T(8,128)(2,1)S(1)} collective-permute-done((bf16[54,896]{1,0:T(8,128)(2,1)S(1)}, bf16[54,896]{1,0:T(8,128)(2,1)S(1)}, u32[]{:S(2)}, u32[]{:S(2)}) %collective-permute-start.19) | collective-permute-done | bytes 96800 | tf_op jit(solution)/shard_map/ppermute | solution.py:347
  76.9 0.1 fusion.4
  77.0 1.6 %collective-permute-start.17 = (bf16[54,896]{1,0:T(8,128)(2,1)S(1)}, bf16[54,896]{1,0:T(8,128)(2,1)S(1)}, u32[]{:S(2)}, u32[]{:S(2)}) collective-permute-start(bf16[54,896]{1,0:T(8,128)(2,1)S(1)} %get-tuple-element.37), channel_id=1, source_target_pairs={{0,4},{1,5},{4,8},{5,9},{8,12},{9,13},{12,14},{13,15},{14,10},{15,... | collective-permute-start | bytes 290312 | tf_op jit(solution)/shard_map/ppermute | solution.py:345
  78.6 0.5 collective-permute-start.20
  79.1 2.6 %collective-permute-done.17 = bf16[54,896]{1,0:T(8,128)(2,1)S(1)} collective-permute-done((bf16[54,896]{1,0:T(8,128)(2,1)S(1)}, bf16[54,896]{1,0:T(8,128)(2,1)S(1)}, u32[]{:S(2)}, u32[]{:S(2)}) %collective-permute-start.17) | collective-permute-done | bytes 96800 | tf_op jit(solution)/shard_map/ppermute | solution.py:345
  81.7 1.5 %collective-permute-done.20 = bf16[54,896]{1,0:T(8,128)(2,1)S(1)} collective-permute-done((bf16[54,896]{1,0:T(8,128)(2,1)S(1)}, bf16[54,896]{1,0:T(8,128)(2,1)S(1)}, u32[]{:S(2)}, u32[]{:S(2)}) %collective-permute-start.20) | collective-permute-done | bytes 96800 | tf_op jit(solution)/shard_map/ppermute | solution.py:347
  83.3 0.9 %copy.6 = f32[1,54,864]{2,0,1:T(1,128)} copy(f32[1,54,864]{2,1,0:T(8,128)S(1)} %fusion.1) | data formatting | bytes 373248 | tf_op jit(solution)/shard_map/stack | solution.py:434
  (26 shorter events, 0.2 us)
Async XLA Ops:
  1.6 16.9 %all-to-all-start = ((bf16[8,16,864]{2,1,0:T(8,128)(2,1)}), bf16[8,16,864]{2,1,0:T(8,128)(2,1)S(1)}, u32[]{:S(2)}, u32[]{:S(2)}) async-start(bf16[8,16,864]{2,1,0:T(8,128)(2,1)} %dynamic-slice_bitcast_fusion), calls=%async_computation | async-start | bytes 458752 | tf_op jit(solution)/shard_map/all_to_all | solution.py:376
  9.9 1.3 %collective-permute-start = (bf16[32,864]{1,0:T(8,128)(2,1)S(1)}, bf16[32,864]{1,0:T(8,128)(2,1)S(1)}, u32[]{:S(2)}, u32[]{:S(2)}) collective-permute-start(bf16[32,864]{1,0:T(8,128)(2,1)S(1)} %get-tuple-element.45), channel_id=1, source_target_pairs={{0,1},{1,0},{2,3},{3,2},{4,5},{5,4},{6,7},{7,6},{8,9},{9,8},{10,11... | collective-permute-start | bytes 165896 | tf_op jit(solution)/shard_map/ppermute | solution.py:369
  11.2 7.0 %copy-start.1 = (bf16[2,32,864]{2,1,0:T(8,128)(2,1)}, bf16[2,32,864]{2,1,0:T(8,128)(2,1)S(1)}, u32[]{:S(2)}) copy-start(bf16[2,32,864]{2,1,0:T(8,128)(2,1)S(1)} %pad_maximum_fusion.refs_4_) | copy-start | bytes 331780
  11.2 11.6 %copy-start.13 = (f32[2,2]{1,0:T(2,128)S(1)}, f32[2,2]{1,0:T(2,128)}, u32[]{:S(2)}) copy-start(f32[2,2]{1,0:T(2,128)} %param.7) | copy-start | bytes 52
  11.2 23.1 %copy-start.2 = (f32[320]{0:T(512)S(1)}, f32[320]{0:T(512)}, u32[]{:S(2)}) copy-start(f32[320]{0:T(512)} %param.5) | copy-start | bytes 3844
  11.2 7.0 %collective-permute-start.2 = (bf16[2,32,864]{2,1,0:T(8,128)(2,1)S(1)}, bf16[2,32,864]{2,1,0:T(8,128)(2,1)S(1)}, u32[]{:S(2)}, u32[]{:S(2)}) collective-permute-start(bf16[2,32,864]{2,1,0:T(8,128)(2,1)S(1)} %pad_maximum_fusion.refs_4_), channel_id=1, source_target_pairs={{4,0},{5,1},{8,4},{9,5},{12,8},{13,9},{14,12},{15,13},{10,14},{11,... | collective-permute-start | bytes 331784 | tf_op jit(solution)/shard_map/ppermute | solution.py:414
  13.3 5.3 %collective-permute-start.1 = (bf16[2,32,864]{2,1,0:T(8,128)(2,1)S(1)}, bf16[2,32,864]{2,1,0:T(8,128)(2,1)S(1)}, u32[]{:S(2)}, u32[]{:S(2)}) collective-permute-start(bf16[2,32,864]{2,1,0:T(8,128)(2,1)S(1)} %pad_maximum_fusion.refs_4_), channel_id=1, source_target_pairs={{0,4},{1,5},{4,8},{5,9},{8,12},{9,13},{12,14},{13,15},{14,10},{15,... | collective-permute-start | bytes 331784 | tf_op jit(solution)/shard_map/ppermute | solution.py:410
  18.2 19.4 %copy-start.6 = (bf16[2,32,864]{2,1,0:T(8,128)(2,1)}, bf16[2,32,864]{2,1,0:T(8,128)(2,1)S(1)}, u32[]{:S(2)}) copy-start(bf16[2,32,864]{2,1,0:T(8,128)(2,1)S(1)} %collective-permute-done.2.refs_6_) | copy-start | bytes 331780
  18.6 19.1 %copy-start.7 = (bf16[2,32,864]{2,1,0:T(8,128)(2,1)}, bf16[2,32,864]{2,1,0:T(8,128)(2,1)S(1)}, u32[]{:S(2)}) copy-start(bf16[2,32,864]{2,1,0:T(8,128)(2,1)S(1)} %collective-permute-done.1.refs_5_) | copy-start | bytes 331780
  18.6 19.1 %copy-start = (bf16[8,16,864]{2,1,0:T(8,128)(2,1)}, bf16[8,16,864]{2,1,0:T(8,128)(2,1)S(1)}, u32[]{:S(2)}) copy-start(bf16[8,16,864]{2,1,0:T(8,128)(2,1)S(1)} %all-to-all-done.refs_0_) | copy-start | bytes 663556
  18.6 8.0 %collective-permute-start.5 = (bf16[8,16,864]{2,1,0:T(8,128)(2,1)S(1)}, bf16[8,16,864]{2,1,0:T(8,128)(2,1)S(1)}, u32[]{:S(2)}, u32[]{:S(2)}) collective-permute-start(bf16[8,16,864]{2,1,0:T(8,128)(2,1)S(1)} %all-to-all-done.refs_0_), channel_id=1, source_target_pairs={{0,16},{16,0},{1,17},{17,1},{2,18},{18,2},{3,19},{19,3},{4,20},{20... | collective-permute-start | bytes 663560 | tf_op jit(solution)/shard_map/ppermute | solution.py:392
  20.1 4.8 %collective-permute-start.3 = (bf16[2,32,864]{2,1,0:T(8,128)(2,1)S(1)}, bf16[2,32,864]{2,1,0:T(8,128)(2,1)S(1)}, u32[]{:S(2)}, u32[]{:S(2)}) collective-permute-start(bf16[2,32,864]{2,1,0:T(8,128)(2,1)S(1)} %collective-permute-done.1.refs_5_), channel_id=1, source_target_pairs={{0,4},{1,5},{4,8},{5,9},{8,12},{9,13},{12,14},{13,15},{14,10},{15,... | collective-permute-start | bytes 331784 | tf_op jit(solution)/shard_map/ppermute | solution.py:410
  21.7 4.8 %collective-permute-start.4 = (bf16[2,32,864]{2,1,0:T(8,128)(2,1)S(1)}, bf16[2,32,864]{2,1,0:T(8,128)(2,1)S(1)}, u32[]{:S(2)}, u32[]{:S(2)}) collective-permute-start(bf16[2,32,864]{2,1,0:T(8,128)(2,1)S(1)} %collective-permute-done.2.refs_6_), channel_id=1, source_target_pairs={{4,0},{5,1},{8,4},{9,5},{12,8},{13,9},{14,12},{15,13},{10,14},{11,... | collective-permute-start | bytes 331784 | tf_op jit(solution)/shard_map/ppermute | solution.py:414
  24.9 12.8 %copy-start.8 = (bf16[2,32,864]{2,1,0:T(8,128)(2,1)}, bf16[2,32,864]{2,1,0:T(8,128)(2,1)S(1)}, u32[]{:S(2)}) copy-start(bf16[2,32,864]{2,1,0:T(8,128)(2,1)S(1)} %collective-permute-done.3.refs_7_) | copy-start | bytes 331780
  26.5 11.2 %copy-start.9 = (bf16[2,32,864]{2,1,0:T(8,128)(2,1)}, bf16[2,32,864]{2,1,0:T(8,128)(2,1)S(1)}, u32[]{:S(2)}) copy-start(bf16[2,32,864]{2,1,0:T(8,128)(2,1)S(1)} %collective-permute-done.4.refs_8_) | copy-start | bytes 331780
  26.5 11.2 %copy-start.3 = (bf16[8,16,864]{2,1,0:T(8,128)(2,1)}, bf16[8,16,864]{2,1,0:T(8,128)(2,1)S(1)}, u32[]{:S(2)}) copy-start(bf16[8,16,864]{2,1,0:T(8,128)(2,1)S(1)} %collective-permute-done.5.refs_2_) | copy-start | bytes 663556
  26.5 4.8 %collective-permute-start.7 = (bf16[2,32,864]{2,1,0:T(8,128)(2,1)S(1)}, bf16[2,32,864]{2,1,0:T(8,128)(2,1)S(1)}, u32[]{:S(2)}, u32[]{:S(2)}) collective-permute-start(bf16[2,32,864]{2,1,0:T(8,128)(2,1)S(1)} %collective-permute-done.3.refs_7_), channel_id=1, source_target_pairs={{0,4},{1,5},{4,8},{5,9},{8,12},{9,13},{12,14},{13,15},{14,10},{15,... | collective-permute-start | bytes 331784 | tf_op jit(solution)/shard_map/ppermute | solution.py:410
  28.1 4.8 %collective-permute-start.8 = (bf16[2,32,864]{2,1,0:T(8,128)(2,1)S(1)}, bf16[2,32,864]{2,1,0:T(8,128)(2,1)S(1)}, u32[]{:S(2)}, u32[]{:S(2)}) collective-permute-start(bf16[2,32,864]{2,1,0:T(8,128)(2,1)S(1)} %collective-permute-done.4.refs_8_), channel_id=1, source_target_pairs={{4,0},{5,1},{8,4},{9,5},{12,8},{13,9},{14,12},{15,13},{10,14},{11,... | collective-permute-start | bytes 331784 | tf_op jit(solution)/shard_map/ppermute | solution.py:414
  28.6 9.0 %collective-permute-start.9 = (bf16[8,16,864]{2,1,0:T(8,128)(2,1)S(1)}, bf16[8,16,864]{2,1,0:T(8,128)(2,1)S(1)}, u32[]{:S(2)}, u32[]{:S(2)}) collective-permute-start(bf16[8,16,864]{2,1,0:T(8,128)(2,1)S(1)} %all-to-all-done.refs_0_), channel_id=1, source_target_pairs={{0,1},{1,0},{2,3},{3,2},{4,5},{5,4},{6,7},{7,6},{8,9},{9,8},{10,11... | collective-permute-start | bytes 663560 | tf_op jit(solution)/shard_map/ppermute | solution.py:395
  28.6 9.0 %collective-permute-start.10 = (bf16[8,16,864]{2,1,0:T(8,128)(2,1)S(1)}, bf16[8,16,864]{2,1,0:T(8,128)(2,1)S(1)}, u32[]{:S(2)}, u32[]{:S(2)}) collective-permute-start(bf16[8,16,864]{2,1,0:T(8,128)(2,1)S(1)} %collective-permute-done.5.refs_2_), channel_id=1, source_target_pairs={{0,1},{1,0},{2,3},{3,2},{4,5},{5,4},{6,7},{7,6},{8,9},{9,8},{10,11... | collective-permute-start | bytes 663560 | tf_op jit(solution)/shard_map/ppermute | solution.py:397
  29.7 4.6 %collective-permute-start.6 = (f32[1]{0:T(128)}, f32[1]{0:T(128)}, u32[]{:S(2)}, u32[]{:S(2)}) collective-permute-start(f32[1]{0:T(128)} %param.6), channel_id=1, source_target_pairs={{16,0},{0,16},{17,1},{1,17},{18,2},{2,18},{19,3},{3,19},{20,4},{4,... | collective-permute-start | bytes 20 | tf_op jit(solution)/shard_map/ppermute | solution.py:400
  31.4 6.3 %copy-start.10 = (bf16[2,32,864]{2,1,0:T(8,128)(2,1)}, bf16[2,32,864]{2,1,0:T(8,128)(2,1)S(1)}, u32[]{:S(2)}) copy-start(bf16[2,32,864]{2,1,0:T(8,128)(2,1)S(1)} %collective-permute-done.7.refs_9_) | copy-start | bytes 331780
  32.8 4.9 %copy-start.11 = (bf16[2,32,864]{2,1,0:T(8,128)(2,1)}, bf16[2,32,864]{2,1,0:T(8,128)(2,1)S(1)}, u32[]{:S(2)}) copy-start(bf16[2,32,864]{2,1,0:T(8,128)(2,1)S(1)} %collective-permute-done.8.refs_10_) | copy-start | bytes 331780
  32.8 4.8 %collective-permute-start.11 = (bf16[2,32,864]{2,1,0:T(8,128)(2,1)S(1)}, bf16[2,32,864]{2,1,0:T(8,128)(2,1)S(1)}, u32[]{:S(2)}, u32[]{:S(2)}) collective-permute-start(bf16[2,32,864]{2,1,0:T(8,128)(2,1)S(1)} %collective-permute-done.7.refs_9_), channel_id=1, source_target_pairs={{0,4},{1,5},{4,8},{5,9},{8,12},{9,13},{12,14},{13,15},{14,10},{15,... | collective-permute-start | bytes 331784 | tf_op jit(solution)/shard_map/ppermute | solution.py:410
  37.6 0.7 copy-start.12
  37.6 0.7 copy-start.4
  37.7 0.8 copy-start.5
  58.2 1.8 %collective-permute-start.13 = (bf16[128,896]{1,0:T(8,128)(2,1)}, bf16[128,896]{1,0:T(8,128)(2,1)S(1)}, u32[]{:S(2)}, u32[]{:S(2)}) collective-permute-start(bf16[128,896]{1,0:T(8,128)(2,1)} %get-tuple-element.36), channel_id=1, source_target_pairs={{0,1},{1,0},{2,3},{3,2},{4,5},{5,4},{6,7},{7,6},{8,9},{9,8},{10,11... | collective-permute-start | bytes 688136 | tf_op jit(solution)/shard_map/ppermute | solution.py:424
  58.3 4.9 %collective-permute-start.12 = (bf16[384,896]{1,0:T(8,128)(2,1)}, bf16[384,896]{1,0:T(8,128)(2,1)S(1)}, u32[]{:S(2)}, u32[]{:S(2)}) collective-permute-start(bf16[384,896]{1,0:T(8,128)(2,1)} %get-tuple-element.34), channel_id=1, source_target_pairs={{0,1},{1,0},{2,3},{3,2},{4,5},{5,4},{6,7},{7,6},{8,9},{9,8},{10,11... | collective-permute-start | bytes 2064392 | tf_op jit(solution)/shard_map/ppermute | solution.py:425
  61.1 4.9 %collective-permute-start.14 = (bf16[54,896]{1,0:T(8,128)(2,1)S(1)}, bf16[54,896]{1,0:T(8,128)(2,1)S(1)}, u32[]{:S(2)}, u32[]{:S(2)}) collective-permute-start(bf16[54,896]{1,0:T(8,128)(2,1)S(1)} %get-tuple-element.42), channel_id=1, source_target_pairs={{0,4},{1,5},{4,8},{5,9},{8,12},{9,13},{12,14},{13,15},{14,10},{15,... | collective-permute-start | bytes 290312 | tf_op jit(solution)/shard_map/ppermute | solution.py:345
  62.6 5.0 %collective-permute-start.18 = (bf16[54,896]{1,0:T(8,128)(2,1)S(1)}, bf16[54,896]{1,0:T(8,128)(2,1)S(1)}, u32[]{:S(2)}, u32[]{:S(2)}) collective-permute-start(bf16[54,896]{1,0:T(8,128)(2,1)S(1)} %get-tuple-element.43), channel_id=1, source_target_pairs={{4,0},{5,1},{8,4},{9,5},{12,8},{13,9},{14,12},{15,13},{10,14},{11,... | collective-permute-start | bytes 290312 | tf_op jit(solution)/shard_map/ppermute | solution.py:347
  66.0 4.7 %collective-permute-start.15 = (bf16[54,896]{1,0:T(8,128)(2,1)S(1)}, bf16[54,896]{1,0:T(8,128)(2,1)S(1)}, u32[]{:S(2)}, u32[]{:S(2)}) collective-permute-start(bf16[54,896]{1,0:T(8,128)(2,1)S(1)} %fusion.6), channel_id=1, source_target_pairs={{0,4},{1,5},{4,8},{5,9},{8,12},{9,13},{12,14},{13,15},{14,10},{15,... | collective-permute-start | bytes 290312 | tf_op jit(solution)/shard_map/ppermute | solution.py:345
  70.8 4.7 %collective-permute-start.16 = (bf16[54,896]{1,0:T(8,128)(2,1)S(1)}, bf16[54,896]{1,0:T(8,128)(2,1)S(1)}, u32[]{:S(2)}, u32[]{:S(2)}) collective-permute-start(bf16[54,896]{1,0:T(8,128)(2,1)S(1)} %get-tuple-element.40), channel_id=1, source_target_pairs={{0,4},{1,5},{4,8},{5,9},{8,12},{9,13},{12,14},{13,15},{14,10},{15,... | collective-permute-start | bytes 290312 | tf_op jit(solution)/shard_map/ppermute | solution.py:345
  72.3 4.6 %collective-permute-start.19 = (bf16[54,896]{1,0:T(8,128)(2,1)S(1)}, bf16[54,896]{1,0:T(8,128)(2,1)S(1)}, u32[]{:S(2)}, u32[]{:S(2)}) collective-permute-start(bf16[54,896]{1,0:T(8,128)(2,1)S(1)} %get-tuple-element.41), channel_id=1, source_target_pairs={{4,0},{5,1},{8,4},{9,5},{12,8},{13,9},{14,12},{15,13},{10,14},{11,... | collective-permute-start | bytes 290312 | tf_op jit(solution)/shard_map/ppermute | solution.py:347
  77.0 4.7 %collective-permute-start.17 = (bf16[54,896]{1,0:T(8,128)(2,1)S(1)}, bf16[54,896]{1,0:T(8,128)(2,1)S(1)}, u32[]{:S(2)}, u32[]{:S(2)}) collective-permute-start(bf16[54,896]{1,0:T(8,128)(2,1)S(1)} %get-tuple-element.37), channel_id=1, source_target_pairs={{0,4},{1,5},{4,8},{5,9},{8,12},{9,13},{12,14},{13,15},{14,10},{15,... | collective-permute-start | bytes 290312 | tf_op jit(solution)/shard_map/ppermute | solution.py:345
  78.6 4.6 %collective-permute-start.20 = (bf16[54,896]{1,0:T(8,128)(2,1)S(1)}, bf16[54,896]{1,0:T(8,128)(2,1)S(1)}, u32[]{:S(2)}, u32[]{:S(2)}) collective-permute-start(bf16[54,896]{1,0:T(8,128)(2,1)S(1)} %get-tuple-element.38), channel_id=1, source_target_pairs={{4,0},{5,1},{8,4},{9,5},{12,8},{13,9},{14,12},{15,13},{10,14},{11,... | collective-permute-start | bytes 290312 | tf_op jit(solution)/shard_map/ppermute | solution.py:347

commit v7 on v5

--- a/solution.py
+++ b/solution.py
@@ -401,10 +401,10 @@
     for hop in range(1, chips // 2 + 1):
         if hop == 2:
             from_left, from_right, emp, tables = lax.optimization_barrier((from_left, from_right, emp, tables))
-            emp_parts += [emp, lax.ppermute(emp, "space", swap)]
             traded = lax.ppermute(emp, "tm", [(0, 1), (1, 0)]) if splits > 1 else None
         elif hop == 3:
-            from_left, from_right, traded = lax.optimization_barrier((from_left, from_right, traded))
+            from_left, from_right, emp, traded = lax.optimization_barrier((from_left, from_right, emp, traded))
+            emp_parts += [emp, lax.ppermute(emp, "space", swap)]
             if splits > 1:
                 emp_parts += [traded, lax.ppermute(traded, "space", swap)]
             held_times = hold(times, (from_left, from_right))
@@ -412,7 +412,7 @@
                 lax.ppermute(held_times, "tm", [((d + step) % tm, d) for d in range(tm)]) for step in range(1, tm)
             ]
         elif hop == 4:
-            from_left, from_right, every_time = lax.optimization_barrier((from_left, from_right, every_time))
+            from_left, from_right = lax.optimization_barrier((from_left, from_right))
             scalars = jnp.concatenate([gaps] + every_time + [cos_weights.reshape(-1)])
             weights = all_pair_weights(
                 place, hold(scalars, (from_left, from_right)), tm, own_count, time_count, own_occ, own_emp

time: 82.4 us -> 82.3 us (level)
    ppermute x1, waiting for transfers between devices: 3.2 us -> 0.01 us  [local(): lax.ppermute(held_times, 'tm', [((d + step) % tm, d) for d in range(tm)])]
    ppermute x3, waiting for transfers between devices: 1.66 us -> 3.12 us  [local(): from_right = lax.ppermute(from_right, 'space', back)]
    ppermute x4, waiting for transfers between devices: 3.12 us -> 4.21 us  [local(): from_left = lax.ppermute(from_left, 'space', ahead)]
  transfers between devices with their start and end apart: 22 -> 22, of which waited for: 13 -> 14; matrix products, arithmetic and copies ran while one was open for 7% -> 7% of each run, Pallas kernels for 7% -> 7%
where the time goes in v7:
time: 82.3 us; the launch traced here: 81.8 us
  starting transfers between devices  26 us (32%)
  Pallas kernels  23.6 us (29%)
  waiting for transfers between devices  22.5 us (27%)
  other arithmetic  4.53 us (6%)
  local copies, waits for them, and re-layouts  4.31 us (5%)
  between operations  0.86 us (1%)
    pallas_call x1, Pallas kernels, pair_moment(): pl.pallas_call(functools.partial(pair_kernel, offsets, splits), out_shape...  17.5 us
    ppermute x4, waiting for transfers between devices, reduce_ring(): lax.ppermute(from_left.astype(jnp.bfloat16), 'space', ahead)  9.76 us
    all_to_all x1, starting transfers between devices, local(): lax.all_to_all(emp_columns.reshape(chips, own_emp // splits, rows), 'spac...  7.28 us
    ppermute x4, starting transfers between devices, reduce_ring(): lax.ppermute(from_left.astype(jnp.bfloat16), 'space', ahead)  6.13 us
    pallas_call x1, Pallas kernels, class_tables(): pl.pallas_call(table_kernel, grid=(4,), out_shape=jax.ShapeDtypeStruct((4...  4.79 us
    ppermute x4, starting transfers between devices, local(): from_left = lax.ppermute(from_left, 'space', ahead)  4.65 us
    ppermute x4, waiting for transfers between devices, local(): from_left = lax.ppermute(from_left, 'space', ahead)  4.21 us
    ppermute x3, waiting for transfers between devices, local(): from_right = lax.ppermute(from_right, 'space', back)  3.12 us
  transfers between devices with their start and end apart: 22, of which 14 were waited for; matrix products, arithmetic and copies ran while one was open for 7% of the time, Pallas kernels for 7%

profile of v7, /device:TPU:0, one launch (start us, length us, event | category | flops | bytes accessed | tf_op | source)
XLA Modules:
  0.0 81.8 jit_solution(3415820775942369095)
XLA Ops:
  0.0 1.6 %dynamic-slice_bitcast_fusion = bf16[8,16,864]{2,1,0:T(8,128)(2,1)} fusion(bf16[10,2,16,864]{3,2,1,0:T(8,128)(2,1)} %bitcast.17, s32[]{:T(128)S(6)} %select_n.25), kind=kLoop, calls=%fused_computation.2 | loop fusion | bytes 442372 | tf_op jit(solution)/shard_map/reshape | solution.py:389
  1.6 7.3 %all-to-all-start = ((bf16[8,16,864]{2,1,0:T(8,128)(2,1)}), bf16[8,16,864]{2,1,0:T(8,128)(2,1)S(1)}, u32[]{:S(2)}, u32[]{:S(2)}) async-start(bf16[8,16,864]{2,1,0:T(8,128)(2,1)} %dynamic-slice_bitcast_fusion), calls=%async_computation | async-start | bytes 458752 | tf_op jit(solution)/shard_map/all_to_all | solution.py:388
  8.9 0.9 %slice.42 = bf16[64,864]{1,0:T(8,128)(2,1)S(1)} slice(bf16[320,864]{1,0:T(8,128)(2,1)} %bitcast.18), slice={[0:64], [0:864]} | slice | bytes 221184 | tf_op jit(solution)/shard_map/slice | solution.py:378
  9.9 0.1 collective-permute-start
  10.0 1.2 %collective-permute-done = bf16[32,864]{1,0:T(8,128)(2,1)S(1)} collective-permute-done((bf16[32,864]{1,0:T(8,128)(2,1)S(1)}, bf16[32,864]{1,0:T(8,128)(2,1)S(1)}, u32[]{:S(2)}, u32[]{:S(2)}) %collective-permute-start) | collective-permute-done | bytes 55328 | tf_op jit(solution)/shard_map/ppermute | solution.py:381
  11.2 0.0 copy-start.1
  11.2 0.0 copy-start.13
  11.2 0.0 copy-start.2
  11.2 2.1 %collective-permute-start.2 = (bf16[2,32,864]{2,1,0:T(8,128)(2,1)S(1)}, bf16[2,32,864]{2,1,0:T(8,128)(2,1)S(1)}, u32[]{:S(2)}, u32[]{:S(2)}) collective-permute-start(bf16[2,32,864]{2,1,0:T(8,128)(2,1)S(1)} %pad_maximum_fusion.refs_4_), channel_id=1, source_target_pairs={{4,0},{5,1},{8,4},{9,5},{12,8},{13,9},{14,12},{15,13},{10,14},{11,... | collective-permute-start | bytes 331784 | tf_op jit(solution)/shard_map/ppermute | solution.py:426
  13.3 0.1 collective-permute-start.1
  13.4 4.8 %class_tables.1.refs_12_ = bf16[4,3584,256]{2,1,0:T(8,128)(2,1)} custom-call(s32[1]{0:T(128)} %constant.37.clone.1.held_ref), custom_call_target="tpu_custom_call" | custom-call | flops 58720256 | bytes 7340032 | tf_op jit(solution)/shard_map/class_tables/pallas_call | solution.py:103
  18.2 0.0 collective-permute-done.2.refs_6_
  18.2 0.3 collective-permute-done.1.refs_5_
  18.6 0.0 all-to-all-done.refs_0_
  18.6 1.6 %collective-permute-start.5 = (bf16[8,16,864]{2,1,0:T(8,128)(2,1)S(1)}, bf16[8,16,864]{2,1,0:T(8,128)(2,1)S(1)}, u32[]{:S(2)}, u32[]{:S(2)}) collective-permute-start(bf16[8,16,864]{2,1,0:T(8,128)(2,1)S(1)} %all-to-all-done.refs_0_), channel_id=1, source_target_pairs={{0,16},{16,0},{1,17},{17,1},{2,18},{18,2},{3,19},{19,3},{4,20},{20... | collective-permute-start | bytes 663560 | tf_op jit(solution)/shard_map/ppermute | solution.py:404
  20.1 1.6 %collective-permute-start.3 = (bf16[2,32,864]{2,1,0:T(8,128)(2,1)S(1)}, bf16[2,32,864]{2,1,0:T(8,128)(2,1)S(1)}, u32[]{:S(2)}, u32[]{:S(2)}) collective-permute-start(bf16[2,32,864]{2,1,0:T(8,128)(2,1)S(1)} %collective-permute-done.1.refs_5_), channel_id=1, source_target_pairs={{0,4},{1,5},{4,8},{5,9},{8,12},{9,13},{12,14},{13,15},{14,10},{15,... | collective-permute-start | bytes 331784 | tf_op jit(solution)/shard_map/ppermute | solution.py:422
  21.7 0.4 collective-permute-start.4
  22.8 0.1 reshape.15
  22.9 2.0 %collective-permute-done.3.refs_7_ = bf16[2,32,864]{2,1,0:T(8,128)(2,1)S(1)} collective-permute-done((bf16[2,32,864]{2,1,0:T(8,128)(2,1)S(1)}, bf16[2,32,864]{2,1,0:T(8,128)(2,1)S(1)}, u32[]{:S(2)}, u32[]{:S(2)}) %collective-permute-start.3) | collective-permute-done | bytes 110624 | tf_op jit(solution)/shard_map/ppermute | solution.py:422
  24.9 1.6 %collective-permute-done.4.refs_8_ = bf16[2,32,864]{2,1,0:T(8,128)(2,1)S(1)} collective-permute-done((bf16[2,32,864]{2,1,0:T(8,128)(2,1)S(1)}, bf16[2,32,864]{2,1,0:T(8,128)(2,1)S(1)}, u32[]{:S(2)}, u32[]{:S(2)}) %collective-permute-start.4) | collective-permute-done | bytes 110624 | tf_op jit(solution)/shard_map/ppermute | solution.py:426
  26.5 0.0 collective-permute-done.5.refs_2_
  26.5 1.5 %collective-permute-start.7 = (bf16[2,32,864]{2,1,0:T(8,128)(2,1)S(1)}, bf16[2,32,864]{2,1,0:T(8,128)(2,1)S(1)}, u32[]{:S(2)}, u32[]{:S(2)}) collective-permute-start(bf16[2,32,864]{2,1,0:T(8,128)(2,1)S(1)} %collective-permute-done.3.refs_7_), channel_id=1, source_target_pairs={{0,4},{1,5},{4,8},{5,9},{8,12},{9,13},{12,14},{13,15},{14,10},{15,... | collective-permute-start | bytes 331784 | tf_op jit(solution)/shard_map/ppermute | solution.py:422
  28.1 0.6 collective-permute-start.8
  28.6 0.0 collective-permute-start.9
  28.6 0.5 collective-permute-start.10
  29.1 0.6 pad_add_fusion.place_ref
  29.7 0.6 collective-permute-start.6
  30.3 1.1 %collective-permute-done.7.refs_9_ = bf16[2,32,864]{2,1,0:T(8,128)(2,1)S(1)} collective-permute-done((bf16[2,32,864]{2,1,0:T(8,128)(2,1)S(1)}, bf16[2,32,864]{2,1,0:T(8,128)(2,1)S(1)}, u32[]{:S(2)}, u32[]{:S(2)}) %collective-permute-start.7) | collective-permute-done | bytes 110624 | tf_op jit(solution)/shard_map/ppermute | solution.py:422
  31.4 1.5 %collective-permute-done.8.refs_10_ = bf16[2,32,864]{2,1,0:T(8,128)(2,1)S(1)} collective-permute-done((bf16[2,32,864]{2,1,0:T(8,128)(2,1)S(1)}, bf16[2,32,864]{2,1,0:T(8,128)(2,1)S(1)}, u32[]{:S(2)}, u32[]{:S(2)}) %collective-permute-start.8) | collective-permute-done | bytes 110624 | tf_op jit(solution)/shard_map/ppermute | solution.py:426
  32.8 1.5 %collective-permute-start.11 = (bf16[2,32,864]{2,1,0:T(8,128)(2,1)S(1)}, bf16[2,32,864]{2,1,0:T(8,128)(2,1)S(1)}, u32[]{:S(2)}, u32[]{:S(2)}) collective-permute-start(bf16[2,32,864]{2,1,0:T(8,128)(2,1)S(1)} %collective-permute-done.7.refs_9_), channel_id=1, source_target_pairs={{0,4},{1,5},{4,8},{5,9},{8,12},{9,13},{12,14},{13,15},{14,10},{15,... | collective-permute-start | bytes 331784 | tf_op jit(solution)/shard_map/ppermute | solution.py:422
  34.3 0.0 collective-permute-done.6
  34.3 0.0 copy-done.2
  34.3 1.2 %pad_maximum_fusion.1.scalar_ref = f32[326]{0:T(512)} fusion(f32[4]{0:T(128)S(1)} %reshape.15, f32[1]{0:T(128)} %collective-permute-done.6, f32[1]{0:T(128)S(6)} %copy.8, f32[320]{0:T(512)S(1)} %copy-done.2), kind=kLoop, calls=%fused_computation.18 | loop fusion | flops 978 | bytes 2608 | tf_op jit(solution)/shard_map/concatenate | solution.py:416
  35.5 1.3 %pair_weights.1 = f32[1,8,128]{2,1,0:T(8,128)} custom-call(s32[2]{0:T(128)} %pad_add_fusion.place_ref, f32[326]{0:T(512)} %pad_maximum_fusion.1.scalar_ref), custom_call_target="tpu_custom_call" | custom-call | flops 16777216 | bytes 1048576 | tf_op jit(solution)/shard_map/pair_weights/pallas_call | solution.py:120
  36.9 0.8 collective-permute-done.11.refs_11_
  37.6 0.0 collective-permute-done.9.refs_1_
  37.6 0.0 collective-permute-done.10.refs_3_
  37.7 0.0 copy-start.5
  37.7 0.5 copy-done.12
  38.3 0.1 copy-done.4
  38.4 0.1 copy-done.5
  38.5 17.5 %pair_moment.1 = (f32[128,896]{1,0:T(8,128)}, bf16[128,896]{1,0:T(8,128)(2,1)}, f32[384,896]{1,0:T(8,128)}, bf16[384,896]{1,0:T(8,128)(2,1)}) custom-call(s32[2]{0:T(128)} %pad_add_fusion.place_ref, f32[8,128]{1,0:T(8,128)} %bitcast.20, bf16[8,16,864]{2,1,0:T(8,128)(2,1)} %copy-done, bf16[8,16,864]{2,1,0:T(8,128)(2,1)} %copy-done.4, ...), custom_call_target="tpu_custom_call" | custom-call | flops 7516192768 | bytes 16777216 | tf_op jit(solution)/shard_map/pair_moment/pallas_call | solution.py:315
  55.9 0.1 collective-permute-start.13
  56.0 0.5 collective-permute-start.12
  56.5 1.2 %collective-permute-done.13 = bf16[128,896]{1,0:T(8,128)(2,1)S(1)} collective-permute-done((bf16[128,896]{1,0:T(8,128)(2,1)}, bf16[128,896]{1,0:T(8,128)(2,1)S(1)}, u32[]{:S(2)}, u32[]{:S(2)}) %collective-permute-start.13) | collective-permute-done | bytes 229408 | tf_op jit(solution)/shard_map/ppermute | solution.py:436
  57.7 1.1 %add_convert_fusion = bf16[128,896]{1,0:T(8,128)(2,1)S(1)} fusion(f32[128,896]{1,0:T(8,128)} %get-tuple-element.35, bf16[128,896]{1,0:T(8,128)(2,1)S(1)} %collective-permute-done.13), kind=kLoop, calls=%fused_computation.1 | loop fusion | flops 344064 | bytes 917504 | tf_op jit(solution)/shard_map/convert.1
  58.8 1.5 %collective-permute-start.14 = (bf16[54,896]{1,0:T(8,128)(2,1)S(1)}, bf16[54,896]{1,0:T(8,128)(2,1)S(1)}, u32[]{:S(2)}, u32[]{:S(2)}) collective-permute-start(bf16[54,896]{1,0:T(8,128)(2,1)S(1)} %get-tuple-element.42), channel_id=1, source_target_pairs={{0,4},{1,5},{4,8},{5,9},{8,12},{9,13},{12,14},{13,15},{14,10},{15,... | collective-permute-start | bytes 290312 | tf_op jit(solution)/shard_map/ppermute | solution.py:357
  60.3 0.6 collective-permute-start.18
  60.9 0.0 collective-permute-done.12
  60.9 1.5 %convert_add_fusion = f32[384,896]{1,0:T(8,128)S(1)} fusion(f32[384,896]{1,0:T(8,128)} %get-tuple-element.33, bf16[384,896]{1,0:T(8,128)(2,1)S(1)} %collective-permute-done.12), kind=kLoop, calls=%fused_computation | loop fusion | flops 688128 | bytes 3440640 | tf_op jit(solution)/shard_map/add | solution.py:437
  62.4 1.4 %collective-permute-done.14 = bf16[54,896]{1,0:T(8,128)(2,1)S(1)} collective-permute-done((bf16[54,896]{1,0:T(8,128)(2,1)S(1)}, bf16[54,896]{1,0:T(8,128)(2,1)S(1)}, u32[]{:S(2)}, u32[]{:S(2)}) %collective-permute-start.14) | collective-permute-done | bytes 96800 | tf_op jit(solution)/shard_map/ppermute | solution.py:357
  63.8 1.5 %collective-permute-start.15 = (bf16[54,896]{1,0:T(8,128)(2,1)S(1)}, bf16[54,896]{1,0:T(8,128)(2,1)S(1)}, u32[]{:S(2)}, u32[]{:S(2)}) collective-permute-start(bf16[54,896]{1,0:T(8,128)(2,1)S(1)} %fusion.6), channel_id=1, source_target_pairs={{0,4},{1,5},{4,8},{5,9},{8,12},{9,13},{12,14},{13,15},{14,10},{15,... | collective-permute-start | bytes 290312 | tf_op jit(solution)/shard_map/ppermute | solution.py:357
  65.3 0.0 collective-permute-done.18
  65.3 3.2 %collective-permute-done.15 = bf16[54,896]{1,0:T(8,128)(2,1)S(1)} collective-permute-done((bf16[54,896]{1,0:T(8,128)(2,1)S(1)}, bf16[54,896]{1,0:T(8,128)(2,1)S(1)}, u32[]{:S(2)}, u32[]{:S(2)}) %collective-permute-start.15) | collective-permute-done | bytes 96800 | tf_op jit(solution)/shard_map/ppermute | solution.py:357
  68.5 1.5 %collective-permute-start.16 = (bf16[54,896]{1,0:T(8,128)(2,1)S(1)}, bf16[54,896]{1,0:T(8,128)(2,1)S(1)}, u32[]{:S(2)}, u32[]{:S(2)}) collective-permute-start(bf16[54,896]{1,0:T(8,128)(2,1)S(1)} %get-tuple-element.40), channel_id=1, source_target_pairs={{0,4},{1,5},{4,8},{5,9},{8,12},{9,13},{12,14},{13,15},{14,10},{15,... | collective-permute-start | bytes 290312 | tf_op jit(solution)/shard_map/ppermute | solution.py:357
  70.0 0.6 collective-permute-start.19
  70.6 2.6 %collective-permute-done.16 = bf16[54,896]{1,0:T(8,128)(2,1)S(1)} collective-permute-done((bf16[54,896]{1,0:T(8,128)(2,1)S(1)}, bf16[54,896]{1,0:T(8,128)(2,1)S(1)}, u32[]{:S(2)}, u32[]{:S(2)}) %collective-permute-start.16) | collective-permute-done | bytes 96800 | tf_op jit(solution)/shard_map/ppermute | solution.py:357
  73.2 1.5 %collective-permute-done.19 = bf16[54,896]{1,0:T(8,128)(2,1)S(1)} collective-permute-done((bf16[54,896]{1,0:T(8,128)(2,1)S(1)}, bf16[54,896]{1,0:T(8,128)(2,1)S(1)}, u32[]{:S(2)}, u32[]{:S(2)}) %collective-permute-start.19) | collective-permute-done | bytes 96800 | tf_op jit(solution)/shard_map/ppermute | solution.py:359
  74.6 0.1 fusion.4
  74.7 1.6 %collective-permute-start.17 = (bf16[54,896]{1,0:T(8,128)(2,1)S(1)}, bf16[54,896]{1,0:T(8,128)(2,1)S(1)}, u32[]{:S(2)}, u32[]{:S(2)}) collective-permute-start(bf16[54,896]{1,0:T(8,128)(2,1)S(1)} %get-tuple-element.37), channel_id=1, source_target_pairs={{0,4},{1,5},{4,8},{5,9},{8,12},{9,13},{12,14},{13,15},{14,10},{15,... | collective-permute-start | bytes 290312 | tf_op jit(solution)/shard_map/ppermute | solution.py:357
  76.3 0.5 collective-permute-start.20
  76.8 2.6 %collective-permute-done.17 = bf16[54,896]{1,0:T(8,128)(2,1)S(1)} collective-permute-done((bf16[54,896]{1,0:T(8,128)(2,1)S(1)}, bf16[54,896]{1,0:T(8,128)(2,1)S(1)}, u32[]{:S(2)}, u32[]{:S(2)}) %collective-permute-start.17) | collective-permute-done | bytes 96800 | tf_op jit(solution)/shard_map/ppermute | solution.py:357
  79.4 1.5 %collective-permute-done.20 = bf16[54,896]{1,0:T(8,128)(2,1)S(1)} collective-permute-done((bf16[54,896]{1,0:T(8,128)(2,1)S(1)}, bf16[54,896]{1,0:T(8,128)(2,1)S(1)}, u32[]{:S(2)}, u32[]{:S(2)}) %collective-permute-start.20) | collective-permute-done | bytes 96800 | tf_op jit(solution)/shard_map/ppermute | solution.py:359
  81.0 0.9 %copy.6 = f32[1,54,864]{2,0,1:T(1,128)} copy(f32[1,54,864]{2,1,0:T(8,128)S(1)} %fusion.1) | data formatting | bytes 373248 | tf_op jit(solution)/shard_map/stack | solution.py:446
  (26 shorter events, 0.2 us)
Async XLA Ops:
  1.6 16.9 %all-to-all-start = ((bf16[8,16,864]{2,1,0:T(8,128)(2,1)}), bf16[8,16,864]{2,1,0:T(8,128)(2,1)S(1)}, u32[]{:S(2)}, u32[]{:S(2)}) async-start(bf16[8,16,864]{2,1,0:T(8,128)(2,1)} %dynamic-slice_bitcast_fusion), calls=%async_computation | async-start | bytes 458752 | tf_op jit(solution)/shard_map/all_to_all | solution.py:388
  9.9 1.3 %collective-permute-start = (bf16[32,864]{1,0:T(8,128)(2,1)S(1)}, bf16[32,864]{1,0:T(8,128)(2,1)S(1)}, u32[]{:S(2)}, u32[]{:S(2)}) collective-permute-start(bf16[32,864]{1,0:T(8,128)(2,1)S(1)} %get-tuple-element.45), channel_id=1, source_target_pairs={{0,1},{1,0},{2,3},{3,2},{4,5},{5,4},{6,7},{7,6},{8,9},{9,8},{10,11... | collective-permute-start | bytes 165896 | tf_op jit(solution)/shard_map/ppermute | solution.py:381
  11.2 7.0 %copy-start.1 = (bf16[2,32,864]{2,1,0:T(8,128)(2,1)}, bf16[2,32,864]{2,1,0:T(8,128)(2,1)S(1)}, u32[]{:S(2)}) copy-start(bf16[2,32,864]{2,1,0:T(8,128)(2,1)S(1)} %pad_maximum_fusion.refs_4_) | copy-start | bytes 331780
  11.2 11.6 %copy-start.13 = (f32[2,2]{1,0:T(2,128)S(1)}, f32[2,2]{1,0:T(2,128)}, u32[]{:S(2)}) copy-start(f32[2,2]{1,0:T(2,128)} %param.7) | copy-start | bytes 52
  11.2 23.1 %copy-start.2 = (f32[320]{0:T(512)S(1)}, f32[320]{0:T(512)}, u32[]{:S(2)}) copy-start(f32[320]{0:T(512)} %param.5) | copy-start | bytes 3844
  11.2 7.0 %collective-permute-start.2 = (bf16[2,32,864]{2,1,0:T(8,128)(2,1)S(1)}, bf16[2,32,864]{2,1,0:T(8,128)(2,1)S(1)}, u32[]{:S(2)}, u32[]{:S(2)}) collective-permute-start(bf16[2,32,864]{2,1,0:T(8,128)(2,1)S(1)} %pad_maximum_fusion.refs_4_), channel_id=1, source_target_pairs={{4,0},{5,1},{8,4},{9,5},{12,8},{13,9},{14,12},{15,13},{10,14},{11,... | collective-permute-start | bytes 331784 | tf_op jit(solution)/shard_map/ppermute | solution.py:426
  13.3 5.3 %collective-permute-start.1 = (bf16[2,32,864]{2,1,0:T(8,128)(2,1)S(1)}, bf16[2,32,864]{2,1,0:T(8,128)(2,1)S(1)}, u32[]{:S(2)}, u32[]{:S(2)}) collective-permute-start(bf16[2,32,864]{2,1,0:T(8,128)(2,1)S(1)} %pad_maximum_fusion.refs_4_), channel_id=1, source_target_pairs={{0,4},{1,5},{4,8},{5,9},{8,12},{9,13},{12,14},{13,15},{14,10},{15,... | collective-permute-start | bytes 331784 | tf_op jit(solution)/shard_map/ppermute | solution.py:422
  18.2 19.4 %copy-start.6 = (bf16[2,32,864]{2,1,0:T(8,128)(2,1)}, bf16[2,32,864]{2,1,0:T(8,128)(2,1)S(1)}, u32[]{:S(2)}) copy-start(bf16[2,32,864]{2,1,0:T(8,128)(2,1)S(1)} %collective-permute-done.2.refs_6_) | copy-start | bytes 331780
  18.6 19.1 %copy-start.7 = (bf16[2,32,864]{2,1,0:T(8,128)(2,1)}, bf16[2,32,864]{2,1,0:T(8,128)(2,1)S(1)}, u32[]{:S(2)}) copy-start(bf16[2,32,864]{2,1,0:T(8,128)(2,1)S(1)} %collective-permute-done.1.refs_5_) | copy-start | bytes 331780
  18.6 19.1 %copy-start = (bf16[8,16,864]{2,1,0:T(8,128)(2,1)}, bf16[8,16,864]{2,1,0:T(8,128)(2,1)S(1)}, u32[]{:S(2)}) copy-start(bf16[8,16,864]{2,1,0:T(8,128)(2,1)S(1)} %all-to-all-done.refs_0_) | copy-start | bytes 663556
  18.6 8.0 %collective-permute-start.5 = (bf16[8,16,864]{2,1,0:T(8,128)(2,1)S(1)}, bf16[8,16,864]{2,1,0:T(8,128)(2,1)S(1)}, u32[]{:S(2)}, u32[]{:S(2)}) collective-permute-start(bf16[8,16,864]{2,1,0:T(8,128)(2,1)S(1)} %all-to-all-done.refs_0_), channel_id=1, source_target_pairs={{0,16},{16,0},{1,17},{17,1},{2,18},{18,2},{3,19},{19,3},{4,20},{20... | collective-permute-start | bytes 663560 | tf_op jit(solution)/shard_map/ppermute | solution.py:404
  20.1 4.8 %collective-permute-start.3 = (bf16[2,32,864]{2,1,0:T(8,128)(2,1)S(1)}, bf16[2,32,864]{2,1,0:T(8,128)(2,1)S(1)}, u32[]{:S(2)}, u32[]{:S(2)}) collective-permute-start(bf16[2,32,864]{2,1,0:T(8,128)(2,1)S(1)} %collective-permute-done.1.refs_5_), channel_id=1, source_target_pairs={{0,4},{1,5},{4,8},{5,9},{8,12},{9,13},{12,14},{13,15},{14,10},{15,... | collective-permute-start | bytes 331784 | tf_op jit(solution)/shard_map/ppermute | solution.py:422
  21.7 4.8 %collective-permute-start.4 = (bf16[2,32,864]{2,1,0:T(8,128)(2,1)S(1)}, bf16[2,32,864]{2,1,0:T(8,128)(2,1)S(1)}, u32[]{:S(2)}, u32[]{:S(2)}) collective-permute-start(bf16[2,32,864]{2,1,0:T(8,128)(2,1)S(1)} %collective-permute-done.2.refs_6_), channel_id=1, source_target_pairs={{4,0},{5,1},{8,4},{9,5},{12,8},{13,9},{14,12},{15,13},{10,14},{11,... | collective-permute-start | bytes 331784 | tf_op jit(solution)/shard_map/ppermute | solution.py:426
  24.9 12.8 %copy-start.8 = (bf16[2,32,864]{2,1,0:T(8,128)(2,1)}, bf16[2,32,864]{2,1,0:T(8,128)(2,1)S(1)}, u32[]{:S(2)}) copy-start(bf16[2,32,864]{2,1,0:T(8,128)(2,1)S(1)} %collective-permute-done.3.refs_7_) | copy-start | bytes 331780
  26.5 11.2 %copy-start.9 = (bf16[2,32,864]{2,1,0:T(8,128)(2,1)}, bf16[2,32,864]{2,1,0:T(8,128)(2,1)S(1)}, u32[]{:S(2)}) copy-start(bf16[2,32,864]{2,1,0:T(8,128)(2,1)S(1)} %collective-permute-done.4.refs_8_) | copy-start | bytes 331780
  26.5 11.2 %copy-start.3 = (bf16[8,16,864]{2,1,0:T(8,128)(2,1)}, bf16[8,16,864]{2,1,0:T(8,128)(2,1)S(1)}, u32[]{:S(2)}) copy-start(bf16[8,16,864]{2,1,0:T(8,128)(2,1)S(1)} %collective-permute-done.5.refs_2_) | copy-start | bytes 663556
  26.5 4.8 %collective-permute-start.7 = (bf16[2,32,864]{2,1,0:T(8,128)(2,1)S(1)}, bf16[2,32,864]{2,1,0:T(8,128)(2,1)S(1)}, u32[]{:S(2)}, u32[]{:S(2)}) collective-permute-start(bf16[2,32,864]{2,1,0:T(8,128)(2,1)S(1)} %collective-permute-done.3.refs_7_), channel_id=1, source_target_pairs={{0,4},{1,5},{4,8},{5,9},{8,12},{9,13},{12,14},{13,15},{14,10},{15,... | collective-permute-start | bytes 331784 | tf_op jit(solution)/shard_map/ppermute | solution.py:422
  28.1 4.8 %collective-permute-start.8 = (bf16[2,32,864]{2,1,0:T(8,128)(2,1)S(1)}, bf16[2,32,864]{2,1,0:T(8,128)(2,1)S(1)}, u32[]{:S(2)}, u32[]{:S(2)}) collective-permute-start(bf16[2,32,864]{2,1,0:T(8,128)(2,1)S(1)} %collective-permute-done.4.refs_8_), channel_id=1, source_target_pairs={{4,0},{5,1},{8,4},{9,5},{12,8},{13,9},{14,12},{15,13},{10,14},{11,... | collective-permute-start | bytes 331784 | tf_op jit(solution)/shard_map/ppermute | solution.py:426
  28.6 9.0 %collective-permute-start.9 = (bf16[8,16,864]{2,1,0:T(8,128)(2,1)S(1)}, bf16[8,16,864]{2,1,0:T(8,128)(2,1)S(1)}, u32[]{:S(2)}, u32[]{:S(2)}) collective-permute-start(bf16[8,16,864]{2,1,0:T(8,128)(2,1)S(1)} %all-to-all-done.refs_0_), channel_id=1, source_target_pairs={{0,1},{1,0},{2,3},{3,2},{4,5},{5,4},{6,7},{7,6},{8,9},{9,8},{10,11... | collective-permute-start | bytes 663560 | tf_op jit(solution)/shard_map/ppermute | solution.py:407
  28.6 9.0 %collective-permute-start.10 = (bf16[8,16,864]{2,1,0:T(8,128)(2,1)S(1)}, bf16[8,16,864]{2,1,0:T(8,128)(2,1)S(1)}, u32[]{:S(2)}, u32[]{:S(2)}) collective-permute-start(bf16[8,16,864]{2,1,0:T(8,128)(2,1)S(1)} %collective-permute-done.5.refs_2_), channel_id=1, source_target_pairs={{0,1},{1,0},{2,3},{3,2},{4,5},{5,4},{6,7},{7,6},{8,9},{9,8},{10,11... | collective-permute-start | bytes 663560 | tf_op jit(solution)/shard_map/ppermute | solution.py:409
  29.7 4.6 %collective-permute-start.6 = (f32[1]{0:T(128)}, f32[1]{0:T(128)}, u32[]{:S(2)}, u32[]{:S(2)}) collective-permute-start(f32[1]{0:T(128)} %param.6), channel_id=1, source_target_pairs={{16,0},{0,16},{17,1},{1,17},{18,2},{2,18},{19,3},{3,19},{20,4},{4,... | collective-permute-start | bytes 20 | tf_op jit(solution)/shard_map/ppermute | solution.py:412
  31.4 6.3 %copy-start.10 = (bf16[2,32,864]{2,1,0:T(8,128)(2,1)}, bf16[2,32,864]{2,1,0:T(8,128)(2,1)S(1)}, u32[]{:S(2)}) copy-start(bf16[2,32,864]{2,1,0:T(8,128)(2,1)S(1)} %collective-permute-done.7.refs_9_) | copy-start | bytes 331780
  32.8 4.9 %copy-start.11 = (bf16[2,32,864]{2,1,0:T(8,128)(2,1)}, bf16[2,32,864]{2,1,0:T(8,128)(2,1)S(1)}, u32[]{:S(2)}) copy-start(bf16[2,32,864]{2,1,0:T(8,128)(2,1)S(1)} %collective-permute-done.8.refs_10_) | copy-start | bytes 331780
  32.8 4.8 %collective-permute-start.11 = (bf16[2,32,864]{2,1,0:T(8,128)(2,1)S(1)}, bf16[2,32,864]{2,1,0:T(8,128)(2,1)S(1)}, u32[]{:S(2)}, u32[]{:S(2)}) collective-permute-start(bf16[2,32,864]{2,1,0:T(8,128)(2,1)S(1)} %collective-permute-done.7.refs_9_), channel_id=1, source_target_pairs={{0,4},{1,5},{4,8},{5,9},{8,12},{9,13},{12,14},{13,15},{14,10},{15,... | collective-permute-start | bytes 331784 | tf_op jit(solution)/shard_map/ppermute | solution.py:422
  37.6 0.7 copy-start.12
  37.6 0.7 copy-start.4
  37.7 0.8 copy-start.5
  55.9 1.8 %collective-permute-start.13 = (bf16[128,896]{1,0:T(8,128)(2,1)}, bf16[128,896]{1,0:T(8,128)(2,1)S(1)}, u32[]{:S(2)}, u32[]{:S(2)}) collective-permute-start(bf16[128,896]{1,0:T(8,128)(2,1)} %get-tuple-element.36), channel_id=1, source_target_pairs={{0,1},{1,0},{2,3},{3,2},{4,5},{5,4},{6,7},{7,6},{8,9},{9,8},{10,11... | collective-permute-start | bytes 688136 | tf_op jit(solution)/shard_map/ppermute | solution.py:436
  56.0 4.9 %collective-permute-start.12 = (bf16[384,896]{1,0:T(8,128)(2,1)}, bf16[384,896]{1,0:T(8,128)(2,1)S(1)}, u32[]{:S(2)}, u32[]{:S(2)}) collective-permute-start(bf16[384,896]{1,0:T(8,128)(2,1)} %get-tuple-element.34), channel_id=1, source_target_pairs={{0,1},{1,0},{2,3},{3,2},{4,5},{5,4},{6,7},{7,6},{8,9},{9,8},{10,11... | collective-permute-start | bytes 2064392 | tf_op jit(solution)/shard_map/ppermute | solution.py:437
  58.8 4.9 %collective-permute-start.14 = (bf16[54,896]{1,0:T(8,128)(2,1)S(1)}, bf16[54,896]{1,0:T(8,128)(2,1)S(1)}, u32[]{:S(2)}, u32[]{:S(2)}) collective-permute-start(bf16[54,896]{1,0:T(8,128)(2,1)S(1)} %get-tuple-element.42), channel_id=1, source_target_pairs={{0,4},{1,5},{4,8},{5,9},{8,12},{9,13},{12,14},{13,15},{14,10},{15,... | collective-permute-start | bytes 290312 | tf_op jit(solution)/shard_map/ppermute | solution.py:357
  60.3 5.0 %collective-permute-start.18 = (bf16[54,896]{1,0:T(8,128)(2,1)S(1)}, bf16[54,896]{1,0:T(8,128)(2,1)S(1)}, u32[]{:S(2)}, u32[]{:S(2)}) collective-permute-start(bf16[54,896]{1,0:T(8,128)(2,1)S(1)} %get-tuple-element.43), channel_id=1, source_target_pairs={{4,0},{5,1},{8,4},{9,5},{12,8},{13,9},{14,12},{15,13},{10,14},{11,... | collective-permute-start | bytes 290312 | tf_op jit(solution)/shard_map/ppermute | solution.py:359
  63.8 4.7 %collective-permute-start.15 = (bf16[54,896]{1,0:T(8,128)(2,1)S(1)}, bf16[54,896]{1,0:T(8,128)(2,1)S(1)}, u32[]{:S(2)}, u32[]{:S(2)}) collective-permute-start(bf16[54,896]{1,0:T(8,128)(2,1)S(1)} %fusion.6), channel_id=1, source_target_pairs={{0,4},{1,5},{4,8},{5,9},{8,12},{9,13},{12,14},{13,15},{14,10},{15,... | collective-permute-start | bytes 290312 | tf_op jit(solution)/shard_map/ppermute | solution.py:357
  68.5 4.7 %collective-permute-start.16 = (bf16[54,896]{1,0:T(8,128)(2,1)S(1)}, bf16[54,896]{1,0:T(8,128)(2,1)S(1)}, u32[]{:S(2)}, u32[]{:S(2)}) collective-permute-start(bf16[54,896]{1,0:T(8,128)(2,1)S(1)} %get-tuple-element.40), channel_id=1, source_target_pairs={{0,4},{1,5},{4,8},{5,9},{8,12},{9,13},{12,14},{13,15},{14,10},{15,... | collective-permute-start | bytes 290312 | tf_op jit(solution)/shard_map/ppermute | solution.py:357
  70.0 4.6 %collective-permute-start.19 = (bf16[54,896]{1,0:T(8,128)(2,1)S(1)}, bf16[54,896]{1,0:T(8,128)(2,1)S(1)}, u32[]{:S(2)}, u32[]{:S(2)}) collective-permute-start(bf16[54,896]{1,0:T(8,128)(2,1)S(1)} %get-tuple-element.41), channel_id=1, source_target_pairs={{4,0},{5,1},{8,4},{9,5},{12,8},{13,9},{14,12},{15,13},{10,14},{11,... | collective-permute-start | bytes 290312 | tf_op jit(solution)/shard_map/ppermute | solution.py:359
  74.7 4.7 %collective-permute-start.17 = (bf16[54,896]{1,0:T(8,128)(2,1)S(1)}, bf16[54,896]{1,0:T(8,128)(2,1)S(1)}, u32[]{:S(2)}, u32[]{:S(2)}) collective-permute-start(bf16[54,896]{1,0:T(8,128)(2,1)S(1)} %get-tuple-element.37), channel_id=1, source_target_pairs={{0,4},{1,5},{4,8},{5,9},{8,12},{9,13},{12,14},{13,15},{14,10},{15,... | collective-permute-start | bytes 290312 | tf_op jit(solution)/shard_map/ppermute | solution.py:357
  76.3 4.6 %collective-permute-start.20 = (bf16[54,896]{1,0:T(8,128)(2,1)S(1)}, bf16[54,896]{1,0:T(8,128)(2,1)S(1)}, u32[]{:S(2)}, u32[]{:S(2)}) collective-permute-start(bf16[54,896]{1,0:T(8,128)(2,1)S(1)} %get-tuple-element.38), channel_id=1, source_target_pairs={{4,0},{5,1},{8,4},{9,5},{12,8},{13,9},{14,12},{15,13},{10,14},{11,... | collective-permute-start | bytes 290312 | tf_op jit(solution)/shard_map/ppermute | solution.py:359
